TPU v7x, 256 devices: a whole 4x4x8 slice. The times are simulated.
256 devices in a mesh: node: 32 (over x, z), local: 8 (over y, core).
Axes of the slice: x: 4, y: 4, z: 8, core: 2. Of those that a mesh axis runs over, the one named last changes fastest.
Arguments:
- tokens_in: bfloat16 [4096, 4096], P('node', 'local'), may hold values from -6 to 6
- grad_out: bfloat16 [4096, 4096], P('node', 'local'), may hold values from -6 to 6
- expert_ids: int32 [4096, 4], P('node'), may hold values from 0 to 31, all different within a row; in each aligned block of 128 rows (0 to 127, 128 to 255, ...) at most 24 rows name the same one
- w_gate: bfloat16 [32, 4096, 2048], P('node', None, 'local'), may hold values from -0.09375 to 0.09375
- w_up: bfloat16 [32, 4096, 2048], P('node', None, 'local'), may hold values from -0.09375 to 0.09375
- w_down: bfloat16 [32, 2048, 4096], P('node', 'local'), may hold values from -0.125 to 0.125
Outputs:
- grad_in: bfloat16 [4096, 4096], P('node', 'local')
- grad_gate: bfloat16 [32, 4096, 2048], P('node', None, 'local')
- grad_up: bfloat16 [32, 4096, 2048], P('node', None, 'local')
- grad_down: bfloat16 [32, 2048, 4096], P('node', 'local')
Inputs may be any that keep to these rules, and one draw needn't show every extreme that they name: `expert_ids`: each token names 4 different experts; within the tokens of one index of node (aligned blocks of 128 tokens) an expert is named by at most 24 tokens, a bound that some block reaches.
All inputs are finite; a program needn't handle non-finite values.
Results may differ from a plain program's by a relative error of at most 0.019.
Values may be sent and summed in bfloat16 or wider, within the bound.
No kernel may reach another device: no remote copies, remote signals or barrier semaphores. Data moves between devices by JAX's collectives and lax.ppermute only.
A program may use at most 128 MiB of HBM per device.

v0:
```python
import jax
import jax.numpy as jnp
from jax import lax
from jax.sharding import PartitionSpec as P


def route_slots(block_ids, experts, capacity):
    flattened = block_ids.reshape(-1)
    matches = (flattened[:, None] == jnp.arange(experts, dtype=jnp.int32)[None, :]).astype(
        jnp.int32
    )
    earlier = jnp.cumsum(matches, axis=0) - matches
    position = jnp.sum(earlier * matches, axis=1)
    return flattened * capacity + position


def slot_owners(slot_index, experts, capacity, topk):
    token_index = jnp.arange(slot_index.shape[0], dtype=jnp.int32) // topk
    owners = jnp.zeros((experts * capacity,), jnp.int32).at[slot_index].set(token_index)
    filled = jnp.zeros((experts * capacity,), jnp.int32).at[slot_index].set(1)
    return (owners, filled)


def pack_rows(row_table, owners, filled):
    picked = row_table[owners]
    return jnp.where(filled[:, None] > 0, picked, jnp.zeros_like(picked))


def body(tokens_in, grad_out, expert_ids, w_gate, w_up, w_down):
    experts = lax.axis_size("node")
    token_count = expert_ids.shape[0]
    topk = expert_ids.shape[1]
    capacity = token_count * topk * 3 // (2 * experts)
    slot_index = route_slots(expert_ids, experts, capacity)
    owners, filled = slot_owners(slot_index, experts, capacity, topk)

    def packed(row_table):
        return pack_rows(row_table, owners, filled).reshape(experts, capacity, row_table.shape[1])

    whole_in, whole_grad = (
        lax.all_gather(tokens_in, "local", axis=1, tiled=True),
        lax.all_gather(grad_out, "local", axis=1, tiled=True),
    )
    arrived_in, arrived_grad = (
        lax.all_to_all(packed(whole_in), "node", split_axis=0, concat_axis=0, tiled=True),
        lax.all_to_all(packed(whole_grad), "node", split_axis=0, concat_axis=0, tiled=True),
    )
    row_count = experts * capacity
    rows_in = arrived_in.reshape(row_count, -1)
    rows_grad = arrived_grad.reshape(row_count, -1)
    width = rows_in.shape[1]
    gate_w = w_gate[0]
    up_w = w_up[0]
    down_w = w_down[0]
    gate_pre = jnp.dot(rows_in, gate_w, preferred_element_type=jnp.float32)
    up_pre = jnp.dot(rows_in, up_w, preferred_element_type=jnp.float32)
    hidden_grad = jnp.einsum("rd,fd->rf", rows_grad, down_w, preferred_element_type=jnp.float32)
    sigmoid_gate = jax.nn.sigmoid(gate_pre)
    swish_gate = gate_pre * sigmoid_gate
    active = (swish_gate * up_pre).astype(jnp.bfloat16)
    gate_grad = (
        hidden_grad * up_pre * sigmoid_gate * (1.0 + gate_pre * (1.0 - sigmoid_gate))
    ).astype(jnp.bfloat16)
    up_grad = (hidden_grad * swish_gate).astype(jnp.bfloat16)
    down_total = jnp.einsum(
        "rf,rd->fd", active, rows_grad, preferred_element_type=jnp.float32
    ).astype(jnp.bfloat16)
    gate_total = jnp.einsum(
        "rd,rf->df", rows_in, gate_grad, preferred_element_type=jnp.float32
    ).astype(jnp.bfloat16)
    up_total = jnp.einsum("rd,rf->df", rows_in, up_grad, preferred_element_type=jnp.float32).astype(
        jnp.bfloat16
    )
    partial_value = jnp.einsum("rf,df->rd", gate_grad, gate_w, preferred_element_type=jnp.float32)
    partial_value = partial_value + jnp.einsum(
        "rf,df->rd", up_grad, up_w, preferred_element_type=jnp.float32
    )
    rounded = partial_value.astype(jnp.bfloat16)
    widened = (
        lax.optimization_barrier(rounded).astype(jnp.float32).reshape(experts, capacity, width)
    )
    summed = lax.psum_scatter(
        widened.astype(jnp.bfloat16), "local", scatter_dimension=2, tiled=True
    ).astype(jnp.float32)
    returned = lax.all_to_all(
        summed.astype(jnp.bfloat16), "node", split_axis=0, concat_axis=0, tiled=True
    ).astype(summed.dtype)
    picked = returned.reshape(row_count, -1)[slot_index]
    grad_in = jnp.sum(picked.reshape(token_count, topk, -1), axis=1).astype(jnp.bfloat16)
    return (grad_in, gate_total[None], up_total[None], down_total[None])


def solution(mesh):
    placed = (
        P("node", "local"),
        P("node", "local"),
        P("node", None),
        P("node", None, "local"),
        P("node", None, "local"),
        P("node", "local", None),
    )
    return jax.shard_map(
        body,
        mesh=mesh,
        in_specs=placed,
        out_specs=(
            P("node", "local"),
            P("node", None, "local"),
            P("node", None, "local"),
            P("node", "local", None),
        ),
        check_vma=False,
    )
```

profile of v0, /device:TPU:32, one launch (start us, length us, event | category | flops | bytes accessed | tf_op | source)
XLA Modules:
  0.0 488.1 jit_solution(9167963114695174240)
XLA Ops:
  12.2 2.4 scatter_custom_fusion.1
  14.6 2.4 scatter_custom_fusion
  17.2 21.2 %all-gather.5.cloned.1.call-done = bf16[128,4096]{1,0:T(8,128)(2,1)} async-done(((bf16[128,512]{1,0:T(8,128)(2,1)}), bf16[128,4096]{1,0:T(8,128)(2,1)}) %all-gather.5.cloned.1.call-update) | async-done | bytes 1048592 | tf_op jit(solution)/shard_map/all_gather | solution.py:41
  38.4 13.3 %gather_fusion.1 = bf16[768,4096]{1,0:T(8,128)(2,1)} fusion(bf16[128,4096]{1,0:T(8,128)(2,1)} %all-gather.5.cloned.1.call-done, s32[1024]{0:T(1024)S(1)} %pad_clamp_fusion.1), kind=kCustom, calls=%fused_computation.1 | custom fusion | bytes 12585984 | tf_op jit(solution)/shard_map/gather | solution.py:25
  51.7 14.4 %all-gather.3.cloned.1.call-done = bf16[128,4096]{1,0:T(8,128)(2,1)} async-done(((bf16[128,512]{1,0:T(8,128)(2,1)}), bf16[128,4096]{1,0:T(8,128)(2,1)}) %all-gather.3.cloned.1.call-update) | async-done | bytes 1048592 | tf_op jit(solution)/shard_map/all_gather | solution.py:42
  66.1 13.3 %gather_fusion = bf16[768,4096]{1,0:T(8,128)(2,1)} fusion(bf16[128,4096]{1,0:T(8,128)(2,1)} %all-gather.3.cloned.1.call-done, s32[1024]{0:T(1024)S(1)} %pad_clamp_fusion.1), kind=kCustom, calls=%fused_computation | custom fusion | bytes 12585984 | tf_op jit(solution)/shard_map/gather | solution.py:25
  79.4 8.1 %broadcast_select_fusion.1 = (bf16[32,24,4096]{2,1,0:T(8,128)(2,1)}, bf16[32,24,4096]{2,1,0:T(8,128)(2,1)S(1)}) fusion(bf16[32,24,4096]{2,1,0:T(8,128)(2,1)} %bitcast.61, pred[32,24]{1,0:T(8,128)(4,1)S(1)} %broadcast_in_dim.36, bf16[32,24,4096]{2,1,0:T(8,128)(2,1)} %bitcast.60), kind=kLoop, calls=%fused_computation.7 | loop fusion | flops 6291456 | bytes 25166592 | tf_op jit(solution)/shard_map/jit(_where)/select_n | solution.py:26
  87.6 151.0 %all_to_all.15 = bf16[32,24,4096]{2,1,0:T(8,128)(2,1)} all-to-all(bf16[32,24,4096]{2,1,0:T(8,128)(2,1)S(1)} %get-tuple-element.7), channel_id=1, replica_groups=mesh['node'=32,'local'=8] {'node'}, dimensions={0} | all-to-all | bytes 12582912 | tf_op jit(solution)/shard_map/all_to_all | solution.py:45
  238.6 5.5 %all-to-all-start = ((bf16[32,24,4096]{2,1,0:T(8,128)(2,1)}), bf16[32,24,4096]{2,1,0:T(8,128)(2,1)}, u32[]{:S(2)}, u32[]{:S(2)}) async-start(bf16[32,24,4096]{2,1,0:T(8,128)(2,1)} %get-tuple-element.6), calls=%async_computation | async-start | bytes 12582912 | tf_op jit(solution)/shard_map/all_to_all | solution.py:46
  244.3 4.7 fusion.5
  249.6 2.7 fusion.8
  252.3 131.9 %all-to-all-done = bf16[32,24,4096]{2,1,0:T(8,128)(2,1)} async-done(((bf16[32,24,4096]{2,1,0:T(8,128)(2,1)}), bf16[32,24,4096]{2,1,0:T(8,128)(2,1)}, u32[]{:S(2)}, u32[]{:S(2)}) %all-to-all-start) | async-done | bytes 6291488 | tf_op jit(solution)/shard_map/all_to_all | solution.py:46
  384.1 6.3 %multiply_convert_fusion.1 = (bf16[768,256]{1,0:T(8,128)(2,1)}, bf16[768,256]{1,0:T(8,128)(2,1)S(1)}) fusion(f32[768,256]{1,0:T(8,128)S(1)} %fusion.5, f32[768,256]{1,0:T(8,128)} %fusion.8, bf16[768,4096]{1,0:T(8,128)(2,1)} %bitcast.4, bf16[1,256,4096]{2,1,0:T(8,128)(2,1)} %param.11), kind=kOutput, calls=%fused_computation.25 | convolution fusion | flops 1613168640 | bytes 10747904 | tf_op jit(solution)/shard_map/rd,fd->rf/dot_general | solution.py:57
  390.4 1.8 fusion.3
  392.3 5.4 %add_convert_fusion = bf16[768,4096]{1,0:T(8,128)(2,1)} fusion(f32[768,4096]{1,0:T(8,128)S(1)} %fusion.3, bf16[768,256]{1,0:T(8,128)(2,1)} %get-tuple-element.4, bf16[1,4096,256]{2,1,0:T(8,128)(2,1)S(1)} %copy-done.5), kind=kOutput, calls=%fused_computation.5 | convolution fusion | flops 1616904192 | bytes 21364736 | tf_op jit(solution)/shard_map/rf,df->rd/dot_general | solution.py:75
  397.7 42.6 %reduce-scatter.2.cloned.1.call-done = bf16[32,24,512]{2,1,0:T(8,128)(2,1)} async-done(((bf16[32,24,4096]{2,1,0:T(8,128)(2,1)}), bf16[32,24,512]{2,1,0:T(8,128)(2,1)}) %reduce-scatter.2.cloned.1.call-update) | async-done | bytes 786448 | tf_op jit(solution)/shard_map/reduce_scatter | solution.py:82
  440.3 10.1 %all-to-all-start.2 = ((bf16[32,24,512]{2,1,0:T(8,128)(2,1)}), bf16[32,24,512]{2,1,0:T(8,128)(2,1)S(1)}, u32[]{:S(2)}, u32[]{:S(2)}) async-start(bf16[32,24,512]{2,1,0:T(8,128)(2,1)} %reduce-scatter.2.cloned.1.call-done), calls=%async_computation.3 | async-start | bytes 1572864 | tf_op jit(solution)/shard_map/all_to_all | solution.py:85
  450.4 6.0 %fusion.1 = bf16[1,4096,256]{2,1,0:T(8,128)(2,1)} fusion(bf16[768,4096]{1,0:T(8,128)(2,1)} %bitcast.64, bf16[768,256]{1,0:T(8,128)(2,1)} %get-tuple-element.4), kind=kOutput, calls=%fused_computation.12 | convolution fusion | flops 1611661312 | bytes 8781824 | tf_op jit(solution)/shard_map/rd,rf->df/dot_general | solution.py:71
  456.4 6.1 %fusion = bf16[1,4096,256]{2,1,0:T(8,128)(2,1)} fusion(bf16[768,4096]{1,0:T(8,128)(2,1)} %bitcast.65, bf16[768,256]{1,0:T(8,128)(2,1)S(1)} %get-tuple-element.5), kind=kOutput, calls=%fused_computation.11 | convolution fusion | flops 1611661312 | bytes 8781824 | tf_op jit(solution)/shard_map/rd,rf->df/dot_general | solution.py:68
  462.5 6.0 %fusion.2 = bf16[1,256,4096]{2,1,0:T(8,128)(2,1)} fusion(bf16[768,4096]{1,0:T(8,128)(2,1)} %bitcast.4, f32[768,256]{1,0:T(8,128)S(1)} %copy-done.3, f32[768,256]{1,0:T(8,128)S(1)} %copy-done.2), kind=kOutput, calls=%fused_computation.13 | convolution fusion | flops 1612840960 | bytes 9961472 | tf_op jit(solution)/shard_map/rf,rd->fd/dot_general | solution.py:65
  468.5 4.5 all-to-all-done.2
  472.9 1.4 bitcast_convert_fusion
  474.4 3.4 gather_fusion.2
  479.1 2.5 reduce_sum.22
  (44 shorter events, 7.1 us)
Async XLA Ops:
  7.2 237.1 %copy-start = (bf16[1,4096,256]{2,1,0:T(8,128)(2,1)S(1)}, bf16[1,4096,256]{2,1,0:T(8,128)(2,1)}, u32[]{:S(2)}) copy-start(bf16[1,4096,256]{2,1,0:T(8,128)(2,1)} %param.9) | copy-start | bytes 6291460
  7.2 31.3 %all-gather.5.cloned.1.call-start = ((), (), s32[]{:S(2)}) async-start(), calls=%async_computation.5 | async-start | bytes 1179648 | tf_op jit(solution)/shard_map/all_gather | solution.py:41
  7.9 58.2 %all-gather.3.cloned.1.call-start = ((), (), s32[]{:S(2)}) async-start(), calls=%async_computation.4 | async-start | bytes 1179648 | tf_op jit(solution)/shard_map/all_gather | solution.py:42
  238.6 145.5 %all-to-all-start = ((bf16[32,24,4096]{2,1,0:T(8,128)(2,1)}), bf16[32,24,4096]{2,1,0:T(8,128)(2,1)}, u32[]{:S(2)}, u32[]{:S(2)}) async-start(bf16[32,24,4096]{2,1,0:T(8,128)(2,1)} %get-tuple-element.6), calls=%async_computation | async-start | bytes 12582912 | tf_op jit(solution)/shard_map/all_to_all | solution.py:46
  244.1 196.2 %reduce-scatter.2.cloned.1.call-start = ((), (), s32[]{:S(2)}) async-start(), calls=%async_computation.6 | async-start | bytes 7077888 | tf_op jit(solution)/shard_map/reduce_scatter | solution.py:82
  244.3 4.8 slice-start
  244.3 4.8 copy-start.4
  244.3 5.3 %slice-start.1 = ((s8[6291456]{0:T(1024)(128)(4,1)}), s8[2097152]{0:T(1024)(128)(4,1)S(1)}, s32[]{:S(2)}) async-start(s8[6291456]{0:T(1024)(128)(4,1)} %bitcast.66), calls=%async_computation.8 | async-start | bytes 4194304
  249.6 140.8 %copy-start.1 = (f32[768,256]{1,0:T(8,128)}, f32[768,256]{1,0:T(8,128)S(1)}, u32[]{:S(2)}) copy-start(f32[768,256]{1,0:T(8,128)S(1)} %fusion.5) | copy-start | bytes 2359300
  390.4 1.8 copy-start.5
  440.3 32.6 %all-to-all-start.2 = ((bf16[32,24,512]{2,1,0:T(8,128)(2,1)}), bf16[32,24,512]{2,1,0:T(8,128)(2,1)S(1)}, u32[]{:S(2)}, u32[]{:S(2)}) async-start(bf16[32,24,512]{2,1,0:T(8,128)(2,1)} %reduce-scatter.2.cloned.1.call-done), calls=%async_computation.3 | async-start | bytes 1572864 | tf_op jit(solution)/shard_map/all_to_all | solution.py:85
  456.4 6.1 %copy-start.2 = (f32[768,256]{1,0:T(8,128)S(1)}, f32[768,256]{1,0:T(8,128)}, u32[]{:S(2)}) copy-start(f32[768,256]{1,0:T(8,128)} %copy-done.1) | copy-start | bytes 2359300
  456.4 6.1 %copy-start.3 = (f32[768,256]{1,0:T(8,128)S(1)}, f32[768,256]{1,0:T(8,128)}, u32[]{:S(2)}) copy-start(f32[768,256]{1,0:T(8,128)} %fusion.8) | copy-start | bytes 2359300
Sparse Core Ops, SparseCore 0:
  9.9 28.5 all-gather.4
  40.3 25.8 all-gather.2
  397.8 42.4 reduce-scatter.1
where the time goes:
time: 489 us; the launch traced here: 488 us
  waiting for transfers between devices  216 us (44%)
  blocking collectives  151 us (31%)
  matrix products  39 us (8%)
  local copies, waits for them, and re-layouts  38.3 us (8%)
  starting transfers between devices  15.8 us (3%)
  other arithmetic  14.1 us (3%)
  between operations  13.9 us (3%)
    all_to_all x1, blocking collectives, body(): lax.all_to_all(packed(whole_in), 'node', split_axis=0, concat_axis=0, til...  151 us
    all_to_all x1, waiting for transfers between devices, body(): lax.all_to_all(packed(whole_grad), 'node', split_axis=0, concat_axis=0, t...  132 us
    reduce_scatter x1, waiting for transfers between devices, body(): lax.psum_scatter(widened.astype(jnp.bfloat16), 'local', scatter_dimension...  42.6 us
    gather x2, local copies, waits for them, and re-layouts, pack_rows(): picked = row_table[owners]  26.6 us
    all_gather x1, waiting for transfers between devices, body(): lax.all_gather(tokens_in, 'local', axis=1, tiled=True)  21.2 us
    all_gather x1, waiting for transfers between devices, body(): lax.all_gather(grad_out, 'local', axis=1, tiled=True)  14.4 us
    all_to_all x1, starting transfers between devices, body(): lax.all_to_all(summed.astype(jnp.bfloat16), 'node', split_axis=0, concat_...  10.1 us
  transfers between devices with their start and end apart: 5, of which 5 were waited for; matrix products, arithmetic and copies ran while one was open for 10% of the time, Pallas kernels for 0%

commit v1 on v0

v1 whole, which is shorter than its diff:
```python
import jax
import jax.numpy as jnp
from jax import lax
from jax.sharding import PartitionSpec as P


def slot_onehot(block_ids, experts, capacity):
    tokens = block_ids.shape[0]
    named = jnp.sum(
        (block_ids[:, :, None] == jnp.arange(experts, dtype=jnp.int32)).astype(jnp.bfloat16), axis=1
    )
    row = lax.broadcasted_iota(jnp.int32, (tokens, tokens), 0)
    column = lax.broadcasted_iota(jnp.int32, (tokens, tokens), 1)
    before = (column < row).astype(jnp.bfloat16)
    earlier = jnp.einsum("se,ts->et", named, before, preferred_element_type=jnp.float32)
    place = jnp.where(named.T > 0, earlier.astype(jnp.int32), -1)
    slot = jnp.arange(capacity, dtype=jnp.int32)
    onehot = (place[:, None, :] == slot[None, :, None]).astype(jnp.bfloat16)
    return onehot.reshape(experts * capacity, tokens)


def body(tokens_in, grad_out, expert_ids, w_gate, w_up, w_down):
    experts = lax.axis_size("node")
    token_count, topk = expert_ids.shape
    capacity = token_count * topk * 3 // (2 * experts)
    onehot = slot_onehot(expert_ids, experts, capacity)

    def rows_of(table):
        packed = jnp.dot(onehot, table, preferred_element_type=jnp.float32).astype(jnp.bfloat16)
        arrived = lax.all_to_all(packed, "node", split_axis=0, concat_axis=0, tiled=True)
        return lax.all_gather(arrived, "local", axis=1, tiled=True)

    rows_in = rows_of(tokens_in)
    rows_grad = rows_of(grad_out)
    gate_w, up_w, down_w = w_gate[0], w_up[0], w_down[0]
    gate_pre = jnp.dot(rows_in, gate_w, preferred_element_type=jnp.float32)
    up_pre = jnp.dot(rows_in, up_w, preferred_element_type=jnp.float32)
    hidden_grad = jnp.einsum("rd,fd->rf", rows_grad, down_w, preferred_element_type=jnp.float32)
    sigmoid_gate = jax.nn.sigmoid(gate_pre)
    swish_gate = gate_pre * sigmoid_gate
    active = (swish_gate * up_pre).astype(jnp.bfloat16)
    gate_grad = (
        hidden_grad * up_pre * sigmoid_gate * (1.0 + gate_pre * (1.0 - sigmoid_gate))
    ).astype(jnp.bfloat16)
    up_grad = (hidden_grad * swish_gate).astype(jnp.bfloat16)
    partial_value = jnp.einsum("rf,df->rd", gate_grad, gate_w, preferred_element_type=jnp.float32)
    partial_value = partial_value + jnp.einsum(
        "rf,df->rd", up_grad, up_w, preferred_element_type=jnp.float32
    )
    summed = lax.psum_scatter(
        partial_value.astype(jnp.bfloat16), "local", scatter_dimension=1, tiled=True
    )
    returned = lax.all_to_all(summed, "node", split_axis=0, concat_axis=0, tiled=True)
    down_total = jnp.einsum("rf,rd->fd", active, rows_grad, preferred_element_type=jnp.float32)
    gate_total = jnp.einsum("rd,rf->df", rows_in, gate_grad, preferred_element_type=jnp.float32)
    up_total = jnp.einsum("rd,rf->df", rows_in, up_grad, preferred_element_type=jnp.float32)
    grad_in = jnp.einsum("st,sd->td", onehot, returned, preferred_element_type=jnp.float32)
    narrow = jnp.bfloat16
    return (
        grad_in.astype(narrow),
        gate_total.astype(narrow)[None],
        up_total.astype(narrow)[None],
        down_total.astype(narrow)[None],
    )


def solution(mesh):
    placed = (
        P("node", "local"),
        P("node", "local"),
        P("node", None),
        P("node", None, "local"),
        P("node", None, "local"),
        P("node", "local", None),
    )
    return jax.shard_map(
        body,
        mesh=mesh,
        in_specs=placed,
        out_specs=(
            P("node", "local"),
            P("node", None, "local"),
            P("node", None, "local"),
            P("node", "local", None),
        ),
        check_vma=False,
    )
```

time: 489 us -> 229 us (0.47)
  waiting for transfers between devices: 216 us -> 101 us
  blocking collectives: 151 us -> 61.8 us
  local copies, waits for them, and re-layouts: 38.3 us -> 0.63 us
  other arithmetic: 14.1 us -> 1 us
  starting transfers between devices: 15.8 us -> 10.2 us
    all_to_all x2 -> x1, waiting for transfers between devices: 136 us -> 7.05 us  [body(): lax.all_to_all(summed, 'node', split_axis=0, concat_axis=0, tiled=True)]
    all_to_all x1 -> x2, blocking collectives: 151 us -> 61.8 us  [rows_of(): lax.all_to_all(packed, 'node', split_axis=0, concat_axis=0, tiled=True)]
    gather x3 -> x0, local copies, waits for them, and re-layouts: 30 us -> none  [the longest x2 26.6 us: pack_rows(): picked = row_table[owners]]
    all_gather x2, waiting for transfers between devices: 35.6 us -> 48.6 us  [rows_of(): return lax.all_gather(arrived, 'local', axis=1, tiled=True)]
    select_n x4 -> x0, other arithmetic: 8.16 us -> none  [the longest x1 8.14 us: pack_rows(): return jnp.where(filled[:, None] > 0, picked, jnp.zeros_like(picked))]
    all_to_all x2 -> x1, starting transfers between devices: 15.5 us -> 10.1 us  [body(): lax.all_to_all(summed, 'node', split_axis=0, concat_axis=0, tiled=True)]
    scatter x2 -> x0, local copies, waits for them, and re-layouts: 4.89 us -> none  [the longest x1 2.45 us: slot_owners(): jnp.zeros((experts * capacity,), jnp.int32).at[slot_index].set(token_index)]
  transfers between devices with their start and end apart: 5 -> 4, of which waited for: 5 -> 4; matrix products, arithmetic and copies ran while one was open for 10% -> 11% of each run, Pallas kernels for 0% -> 0%
where the time goes in v1:
time: 229 us; the launch traced here: 228 us
  waiting for transfers between devices  101 us (44%)
  blocking collectives  61.8 us (27%)
  matrix products  40.1 us (18%)
  between operations  13.9 us (6%)
  starting transfers between devices  10.2 us (4%)
    all_to_all x2, blocking collectives, rows_of(): lax.all_to_all(packed, 'node', split_axis=0, concat_axis=0, tiled=True)  61.8 us
    all_gather x2, waiting for transfers between devices, rows_of(): return lax.all_gather(arrived, 'local', axis=1, tiled=True)  48.6 us
    reduce_scatter x1, waiting for transfers between devices, body(): lax.psum_scatter(partial_value.astype(jnp.bfloat16), 'local', scatter_dim...  45.3 us
    all_to_all x1, starting transfers between devices, body(): lax.all_to_all(summed, 'node', split_axis=0, concat_axis=0, tiled=True)  10.1 us
    all_to_all x1, waiting for transfers between devices, body(): lax.all_to_all(summed, 'node', split_axis=0, concat_axis=0, tiled=True)  7.05 us
    dot_general x1, matrix products, body(): jnp.einsum('rd,fd->rf', rows_grad, down_w, preferred_element_type=jnp.flo...  6.27 us
    dot_general x1, matrix products, body(): jnp.einsum('rd,rf->df', rows_in, up_grad, preferred_element_type=jnp.floa...  6.15 us
    dot_general x1, matrix products, body(): jnp.einsum('rd,rf->df', rows_in, gate_grad, preferred_element_type=jnp.fl...  6.12 us
  transfers between devices with their start and end apart: 4, of which 4 were waited for; matrix products, arithmetic and copies ran while one was open for 11% of the time, Pallas kernels for 0%

profile of v1, /device:TPU:32, one launch (start us, length us, event | category | flops | bytes accessed | tf_op | source)
XLA Modules:
  0.0 228.5 jit_solution(14017460336485756517)
XLA Ops:
  7.2 0.8 fusion.18
  8.1 0.1 fusion.13
  8.2 0.1 eq.45
  8.3 0.2 bitcast_compare_fusion
  8.5 1.3 convolution_convert_fusion.3
  9.8 34.3 %all_to_all.33 = bf16[32,24,512]{2,1,0:T(8,128)(2,1)} all-to-all(bf16[32,24,512]{2,1,0:T(8,128)(2,1)S(1)} %bitcast.55), channel_id=1, replica_groups=mesh['node'=32,'local'=8] {'node'}, dimensions={0} | all-to-all | bytes 1572864 | tf_op jit(solution)/shard_map/all_to_all | solution.py:30
  44.0 0.0 all-gather.3.cloned.1.call-start
  44.1 1.3 convolution_convert_fusion.4
  45.4 27.5 %all_to_all.34 = bf16[32,24,512]{2,1,0:T(8,128)(2,1)} all-to-all(bf16[32,24,512]{2,1,0:T(8,128)(2,1)S(1)} %bitcast.54), channel_id=1, replica_groups=mesh['node'=32,'local'=8] {'node'}, dimensions={0} | all-to-all | bytes 1572864 | tf_op jit(solution)/shard_map/all_to_all | solution.py:30
  73.0 11.1 %all-gather.5.cloned.1.call-done = bf16[768,4096]{1,0:T(8,128)(2,1)} async-done(((bf16[768,512]{1,0:T(8,128)(2,1)}), bf16[768,4096]{1,0:T(8,128)(2,1)}) %all-gather.5.cloned.1.call-update) | async-done | bytes 6291472 | tf_op jit(solution)/shard_map/all_gather | solution.py:31
  84.0 4.7 %fusion.5 = f32[768,256]{1,0:T(8,128)S(1)} fusion(bf16[768,4096]{1,0:T(8,128)(2,1)} %all-gather.5.cloned.1.call-done, bf16[1,4096,256]{2,1,0:T(8,128)(2,1)S(1)} %copy-done), kind=kOutput, calls=%fused_computation.9 | convolution fusion | flops 1610612736 | bytes 9175040 | tf_op jit(solution)/shard_map/dot_general | solution.py:36
  88.8 0.5 copy-done.6
  89.3 2.7 %fusion.8 = f32[768,256]{1,0:T(8,128)} fusion(bf16[768,4096]{1,0:T(8,128)(2,1)S(1)} %copy-done.6, bf16[1,4096,256]{2,1,0:T(8,128)(2,1)S(1)} %copy-done.4), kind=kOutput, calls=%fused_computation.12 | convolution fusion | flops 1610612736 | bytes 9175040 | tf_op jit(solution)/shard_map/dot_general | solution.py:37
  92.0 37.5 %all-gather.3.cloned.1.call-done = bf16[768,4096]{1,0:T(8,128)(2,1)} async-done(((bf16[768,512]{1,0:T(8,128)(2,1)}), bf16[768,4096]{1,0:T(8,128)(2,1)}) %all-gather.3.cloned.1.call-update) | async-done | bytes 6291472 | tf_op jit(solution)/shard_map/all_gather | solution.py:31
  129.5 6.3 %multiply_convert_fusion.1 = (bf16[768,256]{1,0:T(8,128)(2,1)}, bf16[768,256]{1,0:T(8,128)(2,1)S(1)}) fusion(f32[768,256]{1,0:T(8,128)S(1)} %fusion.5, f32[768,256]{1,0:T(8,128)} %fusion.8, bf16[768,4096]{1,0:T(8,128)(2,1)} %all-gather.3.cloned.1.call-done, bf16[1,256,4096]{2,1,0:T(8,128)(2,1)} %param.11), kind=kOutput, calls=%fused_computation.23 | convolution fusion | flops 1613168640 | bytes 10747904 | tf_op jit(solution)/shard_map/rd,fd->rf/dot_general | solution.py:38
  135.7 1.8 fusion.3
  137.6 5.5 %add_convert_fusion = bf16[768,4096]{1,0:T(8,128)(2,1)} fusion(f32[768,4096]{1,0:T(8,128)S(1)} %fusion.3, bf16[768,256]{1,0:T(8,128)(2,1)} %get-tuple-element.4, bf16[1,4096,256]{2,1,0:T(8,128)(2,1)S(1)} %copy-done.5), kind=kOutput, calls=%fused_computation | convolution fusion | flops 1616904192 | bytes 21364736 | tf_op jit(solution)/shard_map/rf,df->rd/dot_general | solution.py:47
  143.1 45.3 %reduce-scatter.2.cloned.1.call-done = bf16[768,512]{1,0:T(8,128)(2,1)} async-done(((bf16[768,4096]{1,0:T(8,128)(2,1)}), bf16[768,512]{1,0:T(8,128)(2,1)}) %reduce-scatter.2.cloned.1.call-update) | async-done | bytes 786448 | tf_op jit(solution)/shard_map/reduce_scatter | solution.py:50
  188.3 10.1 %all-to-all-start.2 = ((bf16[32,24,512]{2,1,0:T(8,128)(2,1)}), bf16[32,24,512]{2,1,0:T(8,128)(2,1)S(1)}, u32[]{:S(2)}, u32[]{:S(2)}) async-start(bf16[32,24,512]{2,1,0:T(8,128)(2,1)} %bitcast.56), calls=%async_computation.3 | async-start | bytes 1572864 | tf_op jit(solution)/shard_map/all_to_all | solution.py:53
  198.4 6.1 %fusion.1 = bf16[1,4096,256]{2,1,0:T(8,128)(2,1)} fusion(bf16[768,4096]{1,0:T(8,128)(2,1)} %all-gather.5.cloned.1.call-done, bf16[768,256]{1,0:T(8,128)(2,1)} %get-tuple-element.4), kind=kOutput, calls=%fused_computation.5 | convolution fusion | flops 1611661312 | bytes 8781824 | tf_op jit(solution)/shard_map/rd,rf->df/dot_general | solution.py:56
  204.6 6.1 %fusion = bf16[1,4096,256]{2,1,0:T(8,128)(2,1)} fusion(bf16[768,4096]{1,0:T(8,128)(2,1)} %all-gather.5.cloned.1.call-done, bf16[768,256]{1,0:T(8,128)(2,1)S(1)} %get-tuple-element.5), kind=kOutput, calls=%fused_computation.4 | convolution fusion | flops 1611661312 | bytes 8781824 | tf_op jit(solution)/shard_map/rd,rf->df/dot_general | solution.py:55
  210.7 3.2 %fusion.2 = bf16[1,256,4096]{2,1,0:T(8,128)(2,1)} fusion(bf16[768,4096]{1,0:T(8,128)(2,1)S(1)} %bitcast.51, f32[768,256]{1,0:T(8,128)S(1)} %copy-done.3, f32[768,256]{1,0:T(8,128)S(1)} %copy-done.2), kind=kOutput, calls=%fused_computation.6 | convolution fusion | flops 1612840960 | bytes 9961472 | tf_op jit(solution)/shard_map/rf,rd->fd/dot_general | solution.py:54
  213.9 7.0 %all-to-all-done.2 = bf16[32,24,512]{2,1,0:T(8,128)(2,1)S(1)} async-done(((bf16[32,24,512]{2,1,0:T(8,128)(2,1)}), bf16[32,24,512]{2,1,0:T(8,128)(2,1)S(1)}, u32[]{:S(2)}, u32[]{:S(2)}) %all-to-all-start.2) | async-done | bytes 786464 | tf_op jit(solution)/shard_map/all_to_all | solution.py:53
  221.0 1.0 fusion.12
  (24 shorter events, 0.2 us)
Async XLA Ops:
  7.2 76.9 %copy-start = (bf16[1,4096,256]{2,1,0:T(8,128)(2,1)S(1)}, bf16[1,4096,256]{2,1,0:T(8,128)(2,1)}, u32[]{:S(2)}) copy-start(bf16[1,4096,256]{2,1,0:T(8,128)(2,1)} %param.9) | copy-start | bytes 6291460
  7.2 76.9 %all-gather.5.cloned.1.call-start = ((), (), s32[]{:S(2)}) async-start(), calls=%async_computation.5 | async-start | bytes 7077888 | tf_op jit(solution)/shard_map/all_gather | solution.py:31
  44.0 85.4 %all-gather.3.cloned.1.call-start = ((), (), s32[]{:S(2)}) async-start(), calls=%async_computation.4 | async-start | bytes 7077888 | tf_op jit(solution)/shard_map/all_gather | solution.py:31
  72.9 115.4 %reduce-scatter.2.cloned.1.call-start = ((), (), s32[]{:S(2)}) async-start(), calls=%async_computation.6 | async-start | bytes 7077888 | tf_op jit(solution)/shard_map/reduce_scatter | solution.py:50
  84.0 4.7 %copy-start.4 = (bf16[1,4096,256]{2,1,0:T(8,128)(2,1)S(1)}, bf16[1,4096,256]{2,1,0:T(8,128)(2,1)}, u32[]{:S(2)}) copy-start(bf16[1,4096,256]{2,1,0:T(8,128)(2,1)} %param.10) | copy-start | bytes 6291460
  84.0 5.2 %copy-start.6 = (bf16[768,4096]{1,0:T(8,128)(2,1)S(1)}, bf16[768,4096]{1,0:T(8,128)(2,1)}, u32[]{:S(2)}) copy-start(bf16[768,4096]{1,0:T(8,128)(2,1)} %all-gather.5.cloned.1.call-done) | copy-start | bytes 18874372
  89.3 40.2 %copy-start.1 = (f32[768,256]{1,0:T(8,128)}, f32[768,256]{1,0:T(8,128)S(1)}, u32[]{:S(2)}) copy-start(f32[768,256]{1,0:T(8,128)S(1)} %fusion.5) | copy-start | bytes 2359300
  135.7 1.8 copy-start.5
  188.3 32.6 %all-to-all-start.2 = ((bf16[32,24,512]{2,1,0:T(8,128)(2,1)}), bf16[32,24,512]{2,1,0:T(8,128)(2,1)S(1)}, u32[]{:S(2)}, u32[]{:S(2)}) async-start(bf16[32,24,512]{2,1,0:T(8,128)(2,1)} %bitcast.56), calls=%async_computation.3 | async-start | bytes 1572864 | tf_op jit(solution)/shard_map/all_to_all | solution.py:53
  198.4 12.3 %slice-start = ((s8[6291456]{0:T(1024)(128)(4,1)}), s8[4194304]{0:T(1024)(128)(4,1)S(1)}, s32[]{:S(2)}) async-start(s8[6291456]{0:T(1024)(128)(4,1)} %bitcast.50), calls=%async_computation.7 | async-start | bytes 8388608
  204.6 6.1 %slice-start.1 = ((s8[6291456]{0:T(1024)(128)(4,1)}), s8[2097152]{0:T(1024)(128)(4,1)S(1)}, s32[]{:S(2)}) async-start(s8[6291456]{0:T(1024)(128)(4,1)} %bitcast.50), calls=%async_computation.8 | async-start | bytes 4194304
  204.6 6.1 %copy-start.2 = (f32[768,256]{1,0:T(8,128)S(1)}, f32[768,256]{1,0:T(8,128)}, u32[]{:S(2)}) copy-start(f32[768,256]{1,0:T(8,128)} %copy-done.1) | copy-start | bytes 2359300
  204.6 6.1 %copy-start.3 = (f32[768,256]{1,0:T(8,128)S(1)}, f32[768,256]{1,0:T(8,128)}, u32[]{:S(2)}) copy-start(f32[768,256]{1,0:T(8,128)} %fusion.8) | copy-start | bytes 2359300
Sparse Core Ops, SparseCore 0:
  44.2 39.8 all-gather.4
  85.9 43.5 all-gather.2
  143.2 45.0 reduce-scatter.1

commit v2 on v1

v2 whole, which is shorter than its diff:
```python
import functools

import jax
import jax.numpy as jnp
from jax import lax
from jax.experimental import pallas as pl
from jax.experimental.pallas import tpu as pltpu
from jax.sharding import PartitionSpec as P

F32 = jnp.float32
BF16 = jnp.bfloat16
HBM = pl.BlockSpec(memory_space=pltpu.HBM)
SMEM = pl.BlockSpec(memory_space=pltpu.SMEM)
VMEM = pl.BlockSpec(memory_space=pltpu.VMEM)
MIB = 1024 * 1024


def slot_places(block_ids, experts):
    tokens = block_ids.shape[0]
    named = jnp.sum(
        (block_ids[:, :, None] == jnp.arange(experts, dtype=jnp.int32)).astype(BF16), axis=1
    )
    row = lax.broadcasted_iota(jnp.int32, (tokens, tokens), 0)
    column = lax.broadcasted_iota(jnp.int32, (tokens, tokens), 1)
    before = (column < row).astype(BF16)
    earlier = jnp.einsum("se,ts->et", named, before, preferred_element_type=F32)
    return jnp.where(named.T > 0, earlier.astype(jnp.int32), -1)


def slot_onehot(places, first, count):
    experts, tokens = places.shape
    slot = first + jnp.arange(count, dtype=jnp.int32)
    onehot = (places[:, None, :] == slot[None, :, None]).astype(BF16)
    return onehot.reshape(experts * count, tokens)


def chip_step(value, step):
    size = lax.axis_size("local")
    chips = size // 2
    pairs = []
    for y in range(chips):
        pairs.append((2 * y, 2 * ((y + step) % chips)))
        pairs.append((2 * y + 1, 2 * ((y - step) % chips) + 1))
    return lax.ppermute(value, "local", pairs)


def core_swap(value):
    return lax.ppermute(value, "local", [(i, i ^ 1) for i in range(lax.axis_size("local"))])


def pin(values):
    return [pltpu.with_memory_space_constraint(value, pltpu.HBM) for value in values]


def after(value, *others):
    return lax.optimization_barrier((value, *others))[0]


def ring_gather(own, beside=()):
    back = chip_step(own, 1)
    on = chip_step(own, -1)
    sibling = core_swap(own)
    far = chip_step(after(back, *beside), 1)
    return (own, sibling, back, core_swap(back), on, core_swap(on)), far


def ring_order():
    size = lax.axis_size("local")
    chips = size // 2
    me = lax.axis_index("local")
    chip, core = me // 2, me % 2
    blocks = []
    for step in (0, -1, 1, 2):
        for other in (0, 1):
            from_core = (core + other) % 2
            moved = step * (1 - 2 * from_core)
            blocks.append(2 * ((chip + moved + chips) % chips) + from_core)
    return jnp.stack(blocks).astype(jnp.int32)


def piece_copies(pieces, buffer, sem):
    return [pltpu.make_async_copy(pieces[j], buffer.at[j], sem.at[j]) for j in range(8)]


def wait_for(ref, sem):
    pltpu.make_async_copy(ref, ref, sem).wait()


def finish(outs, sem):
    def step(j, carry):
        wait_for(outs.at[j], sem.at[j])
        return carry

    lax.fori_loop(0, outs.shape[0], step, 0)


def cost(rows, depth, columns, moved):
    return pl.CostEstimate(
        flops=2 * rows * depth * columns, bytes_accessed=moved, transcendentals=0
    )


def params(mib):
    return pltpu.CompilerParams(vmem_limit_bytes=mib * MIB)


def prepare_kernel(order, gate_a, gate_b, up_a, up_b, down_a, down_b, w_gu, own_t, send_t, w_dn):
    del order
    hidden = gate_a.shape[1]
    for i, (gate, up, down, turned) in enumerate(
        ((gate_a, up_a, down_a, own_t), (gate_b, up_b, down_b, send_t))
    ):
        w_gu[i, :, :hidden] = gate[...]
        w_gu[i, :, hidden:] = up[...]
        turned[0, :hidden, :] = gate[...].T
        turned[0, hidden:, :] = up[...].T
        w_dn[i] = down[...].T


def prepare_call(order, w_gate, w_up, w_down):
    depth, hidden = w_gate.shape
    width = depth // 8

    def rows(core):
        return pl.BlockSpec((width, hidden), lambda d, order: (order[2 * d + core], 0))

    def columns(core):
        return pl.BlockSpec((hidden, width), lambda d, order: (0, order[2 * d + core]))

    def out(count, *shape):
        return pl.BlockSpec((count, *shape), lambda d, order: (d, 0, 0))

    turned = pltpu.HBM((4, 2 * hidden, width), BF16)
    return pl.pallas_call(
        prepare_kernel,
        out_shape=(
            pltpu.HBM((8, width, 2 * hidden), BF16),
            turned,
            turned,
            pltpu.HBM((8, width, hidden), BF16),
        ),
        grid_spec=pltpu.PrefetchScalarGridSpec(
            num_scalar_prefetch=1,
            grid=(4,),
            in_specs=[rows(0), rows(1), rows(0), rows(1), columns(0), columns(1)],
            out_specs=(
                out(2, width, 2 * hidden),
                out(1, 2 * hidden, width),
                out(1, 2 * hidden, width),
                out(2, width, hidden),
            ),
        ),
        compiler_params=params(14),
        cost_estimate=cost(depth, hidden, 768, depth * hidden * 16),
        name="prepare",
    )(order, *pin((w_gate, w_gate, w_up, w_up, w_down, w_down)))


def gate_up_kernel(*refs):
    pieces, weights = refs[:8], refs[8]
    active, swish, slope, rows_in, w_gu, acc, row_sem, w_sem = refs[9:]
    hidden = active.shape[1]
    for j in range(8):
        pltpu.make_async_copy(weights.at[j], w_gu.at[j], w_sem.at[j]).start()
    for copy in piece_copies(pieces, rows_in, row_sem):
        copy.start()
    acc[...] = jnp.zeros_like(acc)

    def step(j, carry):
        wait_for(w_gu.at[j], w_sem.at[j])
        wait_for(rows_in.at[j], row_sem.at[j])
        acc[...] += jnp.dot(rows_in[j], w_gu[j], preferred_element_type=F32)
        return carry

    lax.fori_loop(0, 8, step, 0)
    gate_pre = acc[:, :hidden]
    up_pre = acc[:, hidden:]
    sigmoid_gate = jax.nn.sigmoid(gate_pre)
    swish_gate = gate_pre * sigmoid_gate
    swish[...] = swish_gate
    active[...] = (swish_gate * up_pre).astype(BF16)
    slope[...] = up_pre * sigmoid_gate * (1.0 + gate_pre * (1.0 - sigmoid_gate))


def gate_up_call(pieces, w_gu):
    rows, width = pieces[0].shape
    both = w_gu.shape[2]
    hidden = both // 2
    dma = pltpu.SemaphoreType.DMA((8,))
    return pl.pallas_call(
        gate_up_kernel,
        out_shape=(
            jax.ShapeDtypeStruct((rows, hidden), BF16),
            jax.ShapeDtypeStruct((rows, hidden), F32),
            jax.ShapeDtypeStruct((rows, hidden), F32),
        ),
        in_specs=[HBM] * 9,
        out_specs=(VMEM, VMEM, VMEM),
        scratch_shapes=[
            pltpu.VMEM((8, rows, width), BF16),
            pltpu.VMEM((8, width, both), BF16),
            pltpu.VMEM((rows, both), F32),
            dma,
            dma,
        ],
        compiler_params=params(16),
        cost_estimate=cost(rows, 8 * width, both, 8 * width * (rows + both) * 2),
        name="gate_up",
    )(*pin((*pieces, w_gu)))


def hidden_kernel(first, count, *refs):
    pieces, weights, before = refs[:count], refs[count], refs[count + 1]
    total, rows_grad, w_dn, row_sem, w_sem = refs[count + 2 :]
    for j in range(count):
        pltpu.make_async_copy(weights.at[first + j], w_dn.at[j], w_sem.at[j]).start()
        pltpu.make_async_copy(pieces[j], rows_grad.at[j], row_sem.at[j]).start()
    total[...] = jnp.zeros_like(total) if before is None else before[...]

    def step(j, carry):
        wait_for(w_dn.at[j], w_sem.at[j])
        wait_for(rows_grad.at[j], row_sem.at[j])
        total[...] += jnp.dot(rows_grad[j], w_dn[j], preferred_element_type=F32)
        return carry

    lax.fori_loop(0, count, step, 0)


def hidden_start_kernel(count, *refs):
    hidden_kernel(0, count, *refs[: count + 1], None, *refs[count + 1 :])


def hidden_end_kernel(first, count, *refs):
    before, swish, slope, grads, rows_grad, w_dn, acc, row_sem, w_sem = refs[count + 1 :]
    hidden_kernel(
        first, count, *refs[: count + 1], before, acc, rows_grad, w_dn, row_sem, w_sem
    )
    hidden = acc.shape[1]
    hidden_grad = acc[...]
    grads[:, :hidden] = (hidden_grad * slope[...]).astype(BF16)
    grads[:, hidden:] = (hidden_grad * swish[...]).astype(BF16)


def hidden_scratch(count, rows, width, hidden):
    dma = pltpu.SemaphoreType.DMA((count,))
    return [pltpu.VMEM((count, rows, width), BF16), pltpu.VMEM((count, width, hidden), BF16)], [
        dma,
        dma,
    ]


def hidden_start_call(pieces, w_dn):
    rows, width = pieces[0].shape
    hidden, count = w_dn.shape[2], len(pieces)
    buffers, sems = hidden_scratch(count, rows, width, hidden)
    return pl.pallas_call(
        functools.partial(hidden_start_kernel, count),
        out_shape=jax.ShapeDtypeStruct((rows, hidden), F32),
        in_specs=[HBM] * (count + 1),
        out_specs=VMEM,
        scratch_shapes=buffers + sems,
        compiler_params=params(15),
        cost_estimate=cost(rows, count * width, hidden, count * width * (rows + hidden) * 2),
        name="hidden_start",
    )(*pin((*pieces, w_dn)))


def hidden_end_call(pieces, w_dn, before, swish, slope):
    rows, width = pieces[0].shape
    hidden, count = w_dn.shape[2], len(pieces)
    buffers, sems = hidden_scratch(count, rows, width, hidden)
    return pl.pallas_call(
        functools.partial(hidden_end_kernel, w_dn.shape[0] - count, count),
        out_shape=jax.ShapeDtypeStruct((rows, 2 * hidden), BF16),
        in_specs=[HBM] * (count + 1) + [VMEM] * 3,
        out_specs=VMEM,
        scratch_shapes=buffers + [pltpu.VMEM((rows, hidden), F32)] + sems,
        compiler_params=params(12),
        cost_estimate=cost(rows, count * width, hidden, count * width * (rows + hidden) * 2),
        name="hidden_end",
    )(*pin((*pieces, w_dn)), before, swish, slope)


def partial_kernel(blocks, *refs):
    count = len(blocks)
    grads, other, own_w, other_w = refs[:4]
    outs = refs[4 : 4 + count]
    own_buf, other_buf, result, own_sem, other_sem, out_sem = refs[4 + count :]
    for i, j in enumerate(blocks):
        pltpu.make_async_copy(own_w.at[j], own_buf.at[i], own_sem.at[i]).start()
        pltpu.make_async_copy(other_w.at[j], other_buf.at[i], other_sem.at[i]).start()
    for i in range(count):
        wait_for(own_buf.at[i], own_sem.at[i])
        total = jnp.dot(grads[...], own_buf[i], preferred_element_type=F32)
        wait_for(other_buf.at[i], other_sem.at[i])
        total = total + jnp.dot(other[...], other_buf[i], preferred_element_type=F32)
        result[i] = total.astype(BF16)
        pltpu.make_async_copy(result.at[i], outs[i], out_sem.at[i]).start()
    finish(result, out_sem)


def partial_call(grads, other, own_w, other_w, blocks):
    both, width = own_w.shape[1:]
    rows, count = grads.shape[0], len(blocks)
    dma = pltpu.SemaphoreType.DMA((count,))
    return pl.pallas_call(
        functools.partial(partial_kernel, blocks),
        out_shape=[pltpu.HBM((rows, width), BF16)] * count,
        in_specs=[VMEM, VMEM, HBM, HBM],
        out_specs=[HBM] * count,
        scratch_shapes=[
            pltpu.VMEM((count, both, width), BF16),
            pltpu.VMEM((count, both, width), BF16),
            pltpu.VMEM((count, rows, width), BF16),
            dma,
            dma,
            dma,
        ],
        compiler_params=params(12),
        cost_estimate=cost(
            rows, 2 * both, count * width, count * 2 * width * (rows + 2 * both) * 2
        ),
        name="partial",
    )(grads, other, *pin((own_w, other_w)))


def down_total_kernel(order, *refs):
    pieces = refs[:8]
    active, grad_down, rows_grad, out, row_sem, out_sem = refs[8:]
    width = out.shape[2]
    for copy in piece_copies(pieces, rows_grad, row_sem):
        copy.start()

    def step(j, carry):
        wait_for(rows_grad.at[j], row_sem.at[j])
        out[j] = jnp.dot(active[...], rows_grad[j], preferred_element_type=F32).astype(BF16)
        at = pl.ds(pl.multiple_of(order[j] * width, width), width)
        pltpu.make_async_copy(out.at[j], grad_down.at[:, at], out_sem.at[j]).start()
        return carry

    lax.fori_loop(0, 8, step, 0)
    finish(out, out_sem)


def down_total_call(order, pieces, active):
    width = pieces[0].shape[1]
    hidden, rows = active.shape
    dma = pltpu.SemaphoreType.DMA((8,))
    return pl.pallas_call(
        down_total_kernel,
        out_shape=jax.ShapeDtypeStruct((hidden, 8 * width), BF16),
        in_specs=[SMEM] + [HBM] * 8 + [VMEM],
        out_specs=HBM,
        scratch_shapes=[
            pltpu.VMEM((8, rows, width), BF16),
            pltpu.VMEM((8, hidden, width), BF16),
            dma,
            dma,
        ],
        compiler_params=params(12),
        cost_estimate=cost(rows, 8 * width, hidden, 8 * width * (rows + hidden) * 2),
        name="down_total",
    )(order, *pin(pieces), active)


def gate_up_total_kernel(order, *refs):
    pieces = refs[:8]
    grads, grad_gate, grad_up, rows_in, out_gate, out_up, row_sem, gate_sem, up_sem = refs[8:]
    width, hidden = out_gate.shape[1:]
    for copy in piece_copies(pieces, rows_in, row_sem):
        copy.start()

    def step(j, carry):
        wait_for(rows_in.at[j], row_sem.at[j])
        both = lax.dot_general(
            rows_in[j], grads[...], (((0,), (0,)), ((), ())), preferred_element_type=F32
        )
        out_gate[j] = both[:, :hidden].astype(BF16)
        out_up[j] = both[:, hidden:].astype(BF16)
        at = pl.ds(pl.multiple_of(order[j] * width, width), width)
        pltpu.make_async_copy(out_gate.at[j], grad_gate.at[at, :], gate_sem.at[j]).start()
        pltpu.make_async_copy(out_up.at[j], grad_up.at[at, :], up_sem.at[j]).start()
        return carry

    lax.fori_loop(0, 8, step, 0)
    finish(out_gate, gate_sem)
    finish(out_up, up_sem)


def gate_up_total_call(order, pieces, grads):
    width = pieces[0].shape[1]
    rows, both = grads.shape
    hidden = both // 2
    dma = pltpu.SemaphoreType.DMA((8,))
    total = jax.ShapeDtypeStruct((8 * width, hidden), BF16)
    return pl.pallas_call(
        gate_up_total_kernel,
        out_shape=(total, total),
        in_specs=[SMEM] + [HBM] * 8 + [VMEM],
        out_specs=(HBM, HBM),
        scratch_shapes=[
            pltpu.VMEM((8, rows, width), BF16),
            pltpu.VMEM((8, width, hidden), BF16),
            pltpu.VMEM((8, width, hidden), BF16),
            dma,
            dma,
            dma,
        ],
        compiler_params=params(16),
        cost_estimate=cost(rows, 8 * width, both, 8 * width * (rows + both) * 2),
        name="gate_up_total",
    )(order, *pin(pieces), grads)


def body(tokens_in, grad_out, expert_ids, w_gate, w_up, w_down):
    experts = lax.axis_size("node")
    token_count, topk = expert_ids.shape
    capacity = token_count * topk * 3 // (2 * experts)
    places = slot_places(expert_ids, experts)
    onehot = slot_onehot(places, 0, capacity)

    def packed(table):
        return jnp.dot(onehot, table, preferred_element_type=F32).astype(BF16)

    def exchange(value):
        return lax.all_to_all(value, "node", split_axis=0, concat_axis=0, tiled=True)

    packed_grad = packed(grad_out)
    order = after(ring_order(), packed_grad)
    w_gu, own_w, send_w, w_dn = prepare_call(order, w_gate[0], w_up[0], w_down[0])
    arrived_in = after(exchange(packed(tokens_in)), w_gu)
    arrived_grad = exchange(after(packed_grad, arrived_in))
    near_in, far_in = ring_gather(arrived_in)
    pieces_in = (*near_in, far_in, core_swap(far_in))
    other_w = core_swap(after(send_w, near_in[2]))
    active, swish, slope = gate_up_call(pieces_in, w_gu)
    near_grad, far_grad = ring_gather(after(arrived_grad, far_in), (active,))
    before = hidden_start_call(near_grad, w_dn)
    far_grad = after(far_grad, before)
    far_grad = (far_grad, core_swap(far_grad))
    pieces_grad = (*near_grad, *far_grad)
    grads = hidden_end_call(far_grad, w_dn, before, swish, slope)
    other = core_swap(grads)

    def partial_of(*blocks):
        return partial_call(grads, other, own_w, other_w, blocks)

    far = chip_step(partial_of(3)[0], 1)
    back = chip_step(partial_of(1)[0], -1)
    own, on = partial_of(0, 2)
    down_total = down_total_call(order, pieces_grad, active.T)
    joined = on.astype(F32) + after(far, down_total).astype(F32)
    on = chip_step(joined.astype(BF16), 1)
    total = (own.astype(F32) + back.astype(F32) + on.astype(F32)).astype(BF16)

    gate_total, up_total = gate_up_total_call(order, pieces_in, grads)
    returned = exchange(after(total, gate_total))
    grad_in = jnp.einsum("st,sd->td", onehot, returned, preferred_element_type=F32)
    return (grad_in.astype(BF16), gate_total[None], up_total[None], down_total[None])


def solution(mesh):
    placed = (
        P("node", "local"),
        P("node", "local"),
        P("node", None),
        P("node", None, "local"),
        P("node", None, "local"),
        P("node", "local", None),
    )
    return jax.shard_map(
        body,
        mesh=mesh,
        in_specs=placed,
        out_specs=(
            P("node", "local"),
            P("node", None, "local"),
            P("node", None, "local"),
            P("node", "local", None),
        ),
        check_vma=False,
    )
```

time: 229 us -> 184 us (0.80)
  Pallas kernels: 0 us -> 43.2 us
  matrix products: 40.1 us -> 3.63 us
  waiting for transfers between devices: 101 us -> 67.8 us
  blocking collectives: 61.8 us -> 30.9 us
  starting transfers between devices: 10.2 us -> 30 us
  between operations: 13.9 us -> 1.08 us
  local copies, waits for them, and re-layouts: 0.63 us -> 4.44 us
    all_gather x2 -> x0, waiting for transfers between devices: 48.6 us -> none  [rows_of(): return lax.all_gather(arrived, 'local', axis=1, tiled=True)]
    reduce_scatter x1 -> x0, waiting for transfers between devices: 45.3 us -> none  [body(): lax.psum_scatter(partial_value.astype(jnp.bfloat16), 'local', scatter_dim...]
    pallas_call x0 -> x9, Pallas kernels: none -> 43.2 us  [the longest x3 10.4 us: partial_call(): pl.pallas_call(functools.partial(partial_kernel, blocks), out_shape=[pltp...]
    ppermute x0 -> x19, waiting for transfers between devices: none -> 41 us  [the longest x9 36.5 us: chip_step(): return lax.ppermute(value, 'local', pairs)]
    dot_general x12 -> x4, matrix products: 40.1 us -> 3.63 us  [the longest x2 2.52 us: packed(): return jnp.dot(onehot, table, preferred_element_type=F32).astype(BF16)]
    all_to_all x2 -> x1, blocking collectives: 61.8 us -> 30.9 us  [exchange(): lax.all_to_all(value, 'node', split_axis=0, concat_axis=0, tiled=True)]
    all_to_all x1 -> x2, waiting for transfers between devices: 7.05 us -> 26.9 us  [exchange(): lax.all_to_all(value, 'node', split_axis=0, concat_axis=0, tiled=True)]
    ppermute x0 -> x19, starting transfers between devices: none -> 13.9 us  [the longest x9 11.7 us: chip_step(): return lax.ppermute(value, 'local', pairs)]
  transfers between devices with their start and end apart: 4 -> 21, of which waited for: 4 -> 10; matrix products, arithmetic and copies ran while one was open for 11% -> 2% of each run, Pallas kernels for 0% -> 22%
where the time goes in v2:
time: 184 us
  waiting for transfers between devices  67.8 us (37%)
  Pallas kernels  43.2 us (23%)
  blocking collectives  30.9 us (17%)
  starting transfers between devices  30 us (16%)
  local copies, waits for them, and re-layouts  4.44 us (2%)
  matrix products  3.63 us (2%)
  other arithmetic  2.6 us (1%)
    ppermute x9, waiting for transfers between devices, chip_step(): return lax.ppermute(value, 'local', pairs)  36.5 us
    all_to_all x1, blocking collectives, exchange(): lax.all_to_all(value, 'node', split_axis=0, concat_axis=0, tiled=True)  30.9 us
    all_to_all x2, waiting for transfers between devices, exchange(): lax.all_to_all(value, 'node', split_axis=0, concat_axis=0, tiled=True)  26.9 us
    all_to_all x2, starting transfers between devices, exchange(): lax.all_to_all(value, 'node', split_axis=0, concat_axis=0, tiled=True)  16.1 us
    ppermute x9, starting transfers between devices, chip_step(): return lax.ppermute(value, 'local', pairs)  11.7 us
    pallas_call x3, Pallas kernels, partial_call(): pl.pallas_call(functools.partial(partial_kernel, blocks), out_shape=[pltp...  10.4 us
    pallas_call x1, Pallas kernels, prepare_call(): pl.pallas_call(prepare_kernel, out_shape=(pltpu.HBM((8, width, 2 * hidden...  7.75 us
    pallas_call x1, Pallas kernels, gate_up_total_call(): pl.pallas_call(gate_up_total_kernel, out_shape=(total, total), in_specs=[...  7.57 us
  transfers between devices with their start and end apart: 21, of which 10 were waited for; matrix products, arithmetic and copies ran while one was open for 2% of the time, Pallas kernels for 22%

profile of v2, /device:TPU:32, one launch (start us, length us, event | category | flops | bytes accessed | tf_op | source)
XLA Modules:
  0.0 183.7 jit_solution(17921308290827812357)
XLA Ops:
  3.1 11.2 %all-to-all-start = ((bf16[32,24,512]{2,1,0:T(8,128)(2,1)}), bf16[32,24,512]{2,1,0:T(8,128)(2,1)S(1)}, u32[]{:S(2)}, u32[]{:S(2)}) async-start(bf16[32,24,512]{2,1,0:T(8,128)(2,1)} %bitcast.2), calls=%async_computation | async-start | bytes 1572864 | tf_op jit(solution)/shard_map/all_to_all | solution.py:426
  15.8 7.7 %prepare.1 = (bf16[8,512,512]{2,1,0:T(8,128)(2,1)}, bf16[4,512,512]{2,1,0:T(8,128)(2,1)}, bf16[4,512,512]{2,1,0:T(8,128)(2,1)}, bf16[8,512,256]{2,1,0:T(8,128)(2,1)}) custom-call(s32[8]{0:T(128)S(1)} %stack.35.order, bf16[4096,256]{1,0:T(8,128)(2,1)} %bitcast.35, bf16[4096,256]{1,0:T(8,128)(2,1)} %bitcast.36, bf16[4096,256]{1,0:T(8,128)(2,1)} %bitcast.37, ...), custom_call_target="tpu_custom_call" | custom-call | flops 1610612736 | bytes 16777216 | tf_op jit(solution)/shard_map/prepare/pallas_call | solution.py:134
  23.5 13.9 %all-to-all-done = bf16[32,24,512]{2,1,0:T(8,128)(2,1)S(1)} async-done(((bf16[32,24,512]{2,1,0:T(8,128)(2,1)}), bf16[32,24,512]{2,1,0:T(8,128)(2,1)S(1)}, u32[]{:S(2)}, u32[]{:S(2)}) %all-to-all-start) | async-done | bytes 786464 | tf_op jit(solution)/shard_map/all_to_all | solution.py:426
  39.1 4.9 %all-to-all-start.1 = ((bf16[32,24,512]{2,1,0:T(8,128)(2,1)}), bf16[32,24,512]{2,1,0:T(8,128)(2,1)S(1)}, u32[]{:S(2)}, u32[]{:S(2)}) async-start(bf16[32,24,512]{2,1,0:T(8,128)(2,1)} %bitcast.15), calls=%async_computation.1 | async-start | bytes 1572864 | tf_op jit(solution)/shard_map/all_to_all | solution.py:426
  44.0 6.7 %collective-permute-done.refs_2_ = bf16[768,512]{1,0:T(8,128)(2,1)S(1)} collective-permute-done((bf16[768,512]{1,0:T(8,128)(2,1)S(1)}, bf16[768,512]{1,0:T(8,128)(2,1)S(1)}, u32[]{:S(2)}, u32[]{:S(2)}) %collective-permute-start) | collective-permute-done | bytes 786464 | tf_op jit(solution)/shard_map/ppermute | solution.py:44
  51.0 2.9 %collective-permute-start.5 = (bf16[768,512]{1,0:T(8,128)(2,1)S(1)}, bf16[768,512]{1,0:T(8,128)(2,1)}, u32[]{:S(2)}, u32[]{:S(2)}) collective-permute-start(bf16[768,512]{1,0:T(8,128)(2,1)S(1)} %bitcast.49), channel_id=1, source_target_pairs={{0,6},{1,3},{2,0},{3,5},{4,2},{5,7},{6,4},{7,1},{8,14},{9,11},{10,... | collective-permute-start | bytes 2359304 | tf_op jit(solution)/shard_map/ppermute | solution.py:44
  54.4 12.9 %all-to-all-done.1 = bf16[32,24,512]{2,1,0:T(8,128)(2,1)S(1)} async-done(((bf16[32,24,512]{2,1,0:T(8,128)(2,1)}), bf16[32,24,512]{2,1,0:T(8,128)(2,1)S(1)}, u32[]{:S(2)}, u32[]{:S(2)}) %all-to-all-start.1) | async-done | bytes 786464 | tf_op jit(solution)/shard_map/all_to_all | solution.py:426
  67.4 3.9 %collective-permute-done.1.refs_6_ = bf16[768,512]{1,0:T(8,128)(2,1)} collective-permute-done((bf16[768,512]{1,0:T(8,128)(2,1)S(1)}, bf16[768,512]{1,0:T(8,128)(2,1)}, u32[]{:S(2)}, u32[]{:S(2)}) %collective-permute-start.1) | collective-permute-done | bytes 786464 | tf_op jit(solution)/shard_map/ppermute | solution.py:44
  71.2 3.2 %collective-permute-start.11 = (bf16[768,512]{1,0:T(8,128)(2,1)S(1)}, bf16[768,512]{1,0:T(8,128)(2,1)S(1)}, u32[]{:S(2)}, u32[]{:S(2)}) collective-permute-start(bf16[768,512]{1,0:T(8,128)(2,1)S(1)} %bitcast.42), channel_id=1, source_target_pairs={{0,6},{1,3},{2,0},{3,5},{4,2},{5,7},{6,4},{7,1},{8,14},{9,11},{10,... | collective-permute-start | bytes 2359304 | tf_op jit(solution)/shard_map/ppermute | solution.py:44
  75.1 12.6 %collective-permute-done.2.refs_2_ = bf16[768,512]{1,0:T(8,128)(2,1)S(1)} collective-permute-done((bf16[768,512]{1,0:T(8,128)(2,1)S(1)}, bf16[768,512]{1,0:T(8,128)(2,1)S(1)}, u32[]{:S(2)}, u32[]{:S(2)}) %collective-permute-start.2) | collective-permute-done | bytes 786464 | tf_op jit(solution)/shard_map/ppermute | solution.py:44
  90.0 6.3 %gate_up.1 = (bf16[768,256]{1,0:T(8,128)(2,1)S(1)}, f32[768,256]{1,0:T(8,128)S(1)}, f32[768,256]{1,0:T(8,128)S(1)}) custom-call(bf16[768,512]{1,0:T(8,128)(2,1)} %bitcast.51, bf16[768,512]{1,0:T(8,128)(2,1)} %collective-permute-done.3.refs_1_, bf16[768,512]{1,0:T(8,128)(2,1)} %copy-done.14, bf16[768,512]{1,0:T(8,128)(2,1)} %collective-permute-done.4.refs_3_, ...), custom_call_target="tpu_custom_call" | custom-call | flops 3221225472 | bytes 10485760 | tf_op jit(solution)/shard_map/gate_up/pallas_call | solution.py:190
  98.3 3.5 %hidden_start.1.refs_3_ = f32[768,256]{1,0:T(8,128)S(1)} custom-call(bf16[768,512]{1,0:T(8,128)(2,1)} %bitcast.44, bf16[768,512]{1,0:T(8,128)(2,1)} %copy-done.5, bf16[768,512]{1,0:T(8,128)(2,1)} %copy-done.3, bf16[768,512]{1,0:T(8,128)(2,1)} %copy-done.6, bf16[768,512]{1,0:T(8,128)(2,1)} %copy-done.4, bf16[768,512]{1,0:T(8,128)(2,1)} %copy-done.7, ...), custom_call_target="tpu_custom_call" | custom-call | flops 1207959552 | bytes 6291456 | tf_op jit(solution)/shard_map/hidden_start/pallas_call | solution.py:256
  101.9 7.8 %collective-permute-done.8.refs_0_.refs_6_ = bf16[768,512]{1,0:T(8,128)(2,1)S(1)} collective-permute-done((bf16[768,512]{1,0:T(8,128)(2,1)S(1)}, bf16[768,512]{1,0:T(8,128)(2,1)S(1)}, u32[]{:S(2)}, u32[]{:S(2)}) %collective-permute-start.8) | collective-permute-done | bytes 786464 | tf_op jit(solution)/shard_map/ppermute | solution.py:44
  109.7 2.3 %collective-permute-done.13.refs_1_.refs_7_ = bf16[768,512]{1,0:T(8,128)(2,1)S(1)} collective-permute-done((bf16[768,512]{1,0:T(8,128)(2,1)S(1)}, bf16[768,512]{1,0:T(8,128)(2,1)S(1)}, u32[]{:S(2)}, u32[]{:S(2)}) %collective-permute-start.13) | collective-permute-done | bytes 786464 | tf_op jit(solution)/shard_map/ppermute | solution.py:48
  112.8 2.1 %hidden_end.1.refs_0_.refs_8_ = bf16[768,512]{1,0:T(8,128)(2,1)S(1)} custom-call(bf16[768,512]{1,0:T(8,128)(2,1)} %copy-done.8, bf16[768,512]{1,0:T(8,128)(2,1)} %copy-done.9, bf16[8,512,256]{2,1,0:T(8,128)(2,1)} %get-tuple-element.31.refs_6_.refs_2_, f32[768,256]{1,0:T(8,128)S(1)} %hidden_start.1.refs_3_, f32[768,256]{1,0:T(8,128)S(1)} %get-tuple-element.33.refs_4_, ...), custom_call_target="tpu_custom_call" | custom-call | flops 402653184 | bytes 2097152 | tf_op jit(solution)/shard_map/hidden_end/pallas_call | solution.py:272
  115.2 2.1 %collective-permute-done.14.refs_1_ = bf16[768,512]{1,0:T(8,128)(2,1)S(1)} collective-permute-done((bf16[768,512]{1,0:T(8,128)(2,1)S(1)}, bf16[768,512]{1,0:T(8,128)(2,1)S(1)}, u32[]{:S(2)}, u32[]{:S(2)}) %collective-permute-start.14) | collective-permute-done | bytes 786464 | tf_op jit(solution)/shard_map/ppermute | solution.py:48
  117.3 3.1 %partial.5 = bf16[768,512]{1,0:T(8,128)(2,1)} custom-call(bf16[768,512]{1,0:T(8,128)(2,1)S(1)} %hidden_end.1.refs_0_.refs_8_, bf16[768,512]{1,0:T(8,128)(2,1)S(1)} %collective-permute-done.14.refs_1_, bf16[4,512,512]{2,1,0:T(8,128)(2,1)} %get-tuple-element.35.refs_2_, bf16[4,512,512]{2,1,0:T(8,128)(2,1)} %copy-done.1), custom_call_target="tpu_custom_call" | custom-call | flops 805306368 | bytes 3670016 | tf_op jit(solution)/shard_map/partial/pallas_call | solution.py:306
  120.7 5.5 %down_total.1 = bf16[256,4096]{1,0:T(8,128)(2,1)} custom-call(s32[8]{0:T(128)S(1)} %stack.35.order, bf16[768,512]{1,0:T(8,128)(2,1)} %bitcast.45, bf16[768,512]{1,0:T(8,128)(2,1)} %copy-done.5, bf16[768,512]{1,0:T(8,128)(2,1)} %copy-done.3, bf16[768,512]{1,0:T(8,128)(2,1)} %copy-done.6, bf16[768,512]{1,0:T(8,128)(2,1)} %copy-done.4, ...), custom_call_target="tpu_custom_call" | custom-call | flops 1610612736 | bytes 8388608 | tf_op jit(solution)/shard_map/down_total/pallas_call | solution.py:349
  126.2 3.1 %partial.4 = bf16[768,512]{1,0:T(8,128)(2,1)} custom-call(bf16[768,512]{1,0:T(8,128)(2,1)S(1)} %hidden_end.1.refs_0_.refs_8_, bf16[768,512]{1,0:T(8,128)(2,1)S(1)} %collective-permute-done.14.refs_1_, bf16[4,512,512]{2,1,0:T(8,128)(2,1)} %get-tuple-element.35.refs_2_, bf16[4,512,512]{2,1,0:T(8,128)(2,1)} %copy-done.1), custom_call_target="tpu_custom_call" | custom-call | flops 805306368 | bytes 3670016 | tf_op jit(solution)/shard_map/partial/pallas_call | solution.py:306
  129.3 3.3 %collective-permute-start.16 = (bf16[768,512]{1,0:T(8,128)(2,1)}, bf16[768,512]{1,0:T(8,128)(2,1)S(1)}, u32[]{:S(2)}, u32[]{:S(2)}) collective-permute-start(bf16[768,512]{1,0:T(8,128)(2,1)} %partial.4), channel_id=1, source_target_pairs={{0,6},{1,3},{2,0},{3,5},{4,2},{5,7},{6,4},{7,1},{8,14},{9,11},{10,... | collective-permute-start | bytes 2359304 | tf_op jit(solution)/shard_map/ppermute | solution.py:44
  132.6 4.2 %partial.3 = (bf16[768,512]{1,0:T(8,128)(2,1)}, bf16[768,512]{1,0:T(8,128)(2,1)}) custom-call(bf16[768,512]{1,0:T(8,128)(2,1)S(1)} %hidden_end.1.refs_0_.refs_8_, bf16[768,512]{1,0:T(8,128)(2,1)S(1)} %collective-permute-done.14.refs_1_, bf16[4,512,512]{2,1,0:T(8,128)(2,1)} %get-tuple-element.35.refs_2_, bf16[4,512,512]{2,1,0:T(8,128)(2,1)} %copy-done.1), custom_call_target="tpu_custom_call" | custom-call | flops 1610612736 | bytes 7340032 | tf_op jit(solution)/shard_map/partial/pallas_call | solution.py:306
  138.3 7.6 %gate_up_total.1 = (bf16[4096,256]{1,0:T(8,128)(2,1)}, bf16[4096,256]{1,0:T(8,128)(2,1)}) custom-call(s32[8]{0:T(128)S(1)} %stack.35.order, bf16[768,512]{1,0:T(8,128)(2,1)} %bitcast.52, bf16[768,512]{1,0:T(8,128)(2,1)} %collective-permute-done.3.refs_1_, bf16[768,512]{1,0:T(8,128)(2,1)} %copy-done.14, bf16[768,512]{1,0:T(8,128)(2,1)} %collective-permute-done.4.refs_3_, ...), custom_call_target="tpu_custom_call" | custom-call | flops 3221225472 | bytes 10485760 | tf_op jit(solution)/shard_map/gate_up_total/pallas_call | solution.py:396
  146.4 5.0 %collective-permute-done.18 = bf16[768,512]{1,0:T(8,128)(2,1)S(1)} collective-permute-done((bf16[768,512]{1,0:T(8,128)(2,1)S(1)}, bf16[768,512]{1,0:T(8,128)(2,1)S(1)}, u32[]{:S(2)}, u32[]{:S(2)}) %collective-permute-start.18) | collective-permute-done | bytes 786464 | tf_op jit(solution)/shard_map/ppermute | solution.py:44
  151.8 30.9 %all_to_all.33 = bf16[32,24,512]{2,1,0:T(8,128)(2,1)S(1)} all-to-all(bf16[32,24,512]{2,1,0:T(8,128)(2,1)S(1)} %bitcast.46), channel_id=1, replica_groups=mesh['node'=32,'local'=8] {'node'}, dimensions={0} | all-to-all | bytes 1572864 | tf_op jit(solution)/shard_map/all_to_all | solution.py:426
  (74 shorter events, 15.8 us)
Async XLA Ops:
  3.1 34.4 %all-to-all-start = ((bf16[32,24,512]{2,1,0:T(8,128)(2,1)}), bf16[32,24,512]{2,1,0:T(8,128)(2,1)S(1)}, u32[]{:S(2)}, u32[]{:S(2)}) async-start(bf16[32,24,512]{2,1,0:T(8,128)(2,1)} %bitcast.2), calls=%async_computation | async-start | bytes 1572864 | tf_op jit(solution)/shard_map/all_to_all | solution.py:426
  37.5 50.7 %copy-start.10 = (bf16[32,24,512]{2,1,0:T(8,128)(2,1)}, bf16[32,24,512]{2,1,0:T(8,128)(2,1)S(1)}, u32[]{:S(2)}) copy-start(bf16[32,24,512]{2,1,0:T(8,128)(2,1)S(1)} %all-to-all-done) | copy-start | bytes 2359300
  37.5 13.2 %collective-permute-start = (bf16[768,512]{1,0:T(8,128)(2,1)S(1)}, bf16[768,512]{1,0:T(8,128)(2,1)S(1)}, u32[]{:S(2)}, u32[]{:S(2)}) collective-permute-start(bf16[768,512]{1,0:T(8,128)(2,1)S(1)} %bitcast.48), channel_id=1, source_target_pairs={{0,2},{1,7},{2,4},{3,1},{4,6},{5,3},{6,0},{7,5},{8,10},{9,15},{10,... | collective-permute-start | bytes 2359304 | tf_op jit(solution)/shard_map/ppermute | solution.py:44
  39.1 28.3 %all-to-all-start.1 = ((bf16[32,24,512]{2,1,0:T(8,128)(2,1)}), bf16[32,24,512]{2,1,0:T(8,128)(2,1)S(1)}, u32[]{:S(2)}, u32[]{:S(2)}) async-start(bf16[32,24,512]{2,1,0:T(8,128)(2,1)} %bitcast.15), calls=%async_computation.1 | async-start | bytes 1572864 | tf_op jit(solution)/shard_map/all_to_all | solution.py:426
  50.7 37.5 %copy-start.14 = (bf16[768,512]{1,0:T(8,128)(2,1)}, bf16[768,512]{1,0:T(8,128)(2,1)S(1)}, u32[]{:S(2)}) copy-start(bf16[768,512]{1,0:T(8,128)(2,1)S(1)} %collective-permute-done.refs_2_) | copy-start | bytes 2359300
  50.7 20.6 %collective-permute-start.1 = (bf16[768,512]{1,0:T(8,128)(2,1)S(1)}, bf16[768,512]{1,0:T(8,128)(2,1)}, u32[]{:S(2)}, u32[]{:S(2)}) collective-permute-start(bf16[768,512]{1,0:T(8,128)(2,1)S(1)} %collective-permute-done.refs_2_), channel_id=1, source_target_pairs={{0,2},{1,7},{2,4},{3,1},{4,6},{5,3},{6,0},{7,5},{8,10},{9,15},{10,... | collective-permute-start | bytes 2359304 | tf_op jit(solution)/shard_map/ppermute | solution.py:44
  51.0 23.4 %collective-permute-start.5 = (bf16[768,512]{1,0:T(8,128)(2,1)S(1)}, bf16[768,512]{1,0:T(8,128)(2,1)}, u32[]{:S(2)}, u32[]{:S(2)}) collective-permute-start(bf16[768,512]{1,0:T(8,128)(2,1)S(1)} %bitcast.49), channel_id=1, source_target_pairs={{0,6},{1,3},{2,0},{3,5},{4,2},{5,7},{6,4},{7,1},{8,14},{9,11},{10,... | collective-permute-start | bytes 2359304 | tf_op jit(solution)/shard_map/ppermute | solution.py:44
  53.9 20.6 %collective-permute-start.3 = (bf16[768,512]{1,0:T(8,128)(2,1)S(1)}, bf16[768,512]{1,0:T(8,128)(2,1)}, u32[]{:S(2)}, u32[]{:S(2)}) collective-permute-start(bf16[768,512]{1,0:T(8,128)(2,1)S(1)} %bitcast.50), channel_id=1, source_target_pairs={{0,1},{1,0},{2,3},{3,2},{4,5},{5,4},{6,7},{7,6},{8,9},{9,8},{10,11... | collective-permute-start | bytes 2359304 | tf_op jit(solution)/shard_map/ppermute | solution.py:48
  53.9 21.1 %collective-permute-start.4 = (bf16[768,512]{1,0:T(8,128)(2,1)S(1)}, bf16[768,512]{1,0:T(8,128)(2,1)}, u32[]{:S(2)}, u32[]{:S(2)}) collective-permute-start(bf16[768,512]{1,0:T(8,128)(2,1)S(1)} %collective-permute-done.refs_2_), channel_id=1, source_target_pairs={{0,1},{1,0},{2,3},{3,2},{4,5},{5,4},{6,7},{7,6},{8,9},{9,8},{10,11... | collective-permute-start | bytes 2359304 | tf_op jit(solution)/shard_map/ppermute | solution.py:48
  67.4 29.0 %copy-start.2 = (bf16[32,24,512]{2,1,0:T(8,128)(2,1)}, bf16[32,24,512]{2,1,0:T(8,128)(2,1)S(1)}, u32[]{:S(2)}) copy-start(bf16[32,24,512]{2,1,0:T(8,128)(2,1)S(1)} %all-to-all-done.1) | copy-start | bytes 2359300
  71.2 16.4 %collective-permute-start.2 = (bf16[768,512]{1,0:T(8,128)(2,1)S(1)}, bf16[768,512]{1,0:T(8,128)(2,1)S(1)}, u32[]{:S(2)}, u32[]{:S(2)}) collective-permute-start(bf16[768,512]{1,0:T(8,128)(2,1)S(1)} %bitcast.41), channel_id=1, source_target_pairs={{0,2},{1,7},{2,4},{3,1},{4,6},{5,3},{6,0},{7,5},{8,10},{9,15},{10,... | collective-permute-start | bytes 2359304 | tf_op jit(solution)/shard_map/ppermute | solution.py:44
  71.2 16.4 %collective-permute-start.11 = (bf16[768,512]{1,0:T(8,128)(2,1)S(1)}, bf16[768,512]{1,0:T(8,128)(2,1)S(1)}, u32[]{:S(2)}, u32[]{:S(2)}) collective-permute-start(bf16[768,512]{1,0:T(8,128)(2,1)S(1)} %bitcast.42), channel_id=1, source_target_pairs={{0,6},{1,3},{2,0},{3,5},{4,2},{5,7},{6,4},{7,1},{8,14},{9,11},{10,... | collective-permute-start | bytes 2359304 | tf_op jit(solution)/shard_map/ppermute | solution.py:44
  74.5 13.7 %collective-permute-start.6 = (bf16[768,512]{1,0:T(8,128)(2,1)}, bf16[768,512]{1,0:T(8,128)(2,1)S(1)}, u32[]{:S(2)}, u32[]{:S(2)}) collective-permute-start(bf16[768,512]{1,0:T(8,128)(2,1)} %collective-permute-done.5.refs_4_), channel_id=1, source_target_pairs={{0,1},{1,0},{2,3},{3,2},{4,5},{5,4},{6,7},{7,6},{8,9},{9,8},{10,11... | collective-permute-start | bytes 2359304 | tf_op jit(solution)/shard_map/ppermute | solution.py:48
  74.5 13.7 %collective-permute-start.7 = (bf16[768,512]{1,0:T(8,128)(2,1)}, bf16[768,512]{1,0:T(8,128)(2,1)S(1)}, u32[]{:S(2)}, u32[]{:S(2)}) collective-permute-start(bf16[768,512]{1,0:T(8,128)(2,1)} %collective-permute-done.1.refs_6_), channel_id=1, source_target_pairs={{0,1},{1,0},{2,3},{3,2},{4,5},{5,4},{6,7},{7,6},{8,9},{9,8},{10,11... | collective-permute-start | bytes 2359304 | tf_op jit(solution)/shard_map/ppermute | solution.py:48
  75.0 21.9 %collective-permute-start.9 = (bf16[768,512]{1,0:T(8,128)(2,1)S(1)}, bf16[768,512]{1,0:T(8,128)(2,1)S(1)}, u32[]{:S(2)}, u32[]{:S(2)}) collective-permute-start(bf16[768,512]{1,0:T(8,128)(2,1)S(1)} %bitcast.43), channel_id=1, source_target_pairs={{0,1},{1,0},{2,3},{3,2},{4,5},{5,4},{6,7},{7,6},{8,9},{9,8},{10,11... | collective-permute-start | bytes 2359304 | tf_op jit(solution)/shard_map/ppermute | solution.py:48
  87.7 9.3 %collective-permute-start.10 = (bf16[768,512]{1,0:T(8,128)(2,1)S(1)}, bf16[768,512]{1,0:T(8,128)(2,1)S(1)}, u32[]{:S(2)}, u32[]{:S(2)}) collective-permute-start(bf16[768,512]{1,0:T(8,128)(2,1)S(1)} %collective-permute-done.2.refs_2_), channel_id=1, source_target_pairs={{0,1},{1,0},{2,3},{3,2},{4,5},{5,4},{6,7},{7,6},{8,9},{9,8},{10,11... | collective-permute-start | bytes 2359304 | tf_op jit(solution)/shard_map/ppermute | solution.py:48
  87.7 9.3 %collective-permute-start.12 = (bf16[768,512]{1,0:T(8,128)(2,1)S(1)}, bf16[768,512]{1,0:T(8,128)(2,1)S(1)}, u32[]{:S(2)}, u32[]{:S(2)}) collective-permute-start(bf16[768,512]{1,0:T(8,128)(2,1)S(1)} %collective-permute-done.11.refs_4_), channel_id=1, source_target_pairs={{0,1},{1,0},{2,3},{3,2},{4,5},{5,4},{6,7},{7,6},{8,9},{9,8},{10,11... | collective-permute-start | bytes 2359304 | tf_op jit(solution)/shard_map/ppermute | solution.py:48
  96.4 13.3 %collective-permute-start.8 = (bf16[768,512]{1,0:T(8,128)(2,1)S(1)}, bf16[768,512]{1,0:T(8,128)(2,1)S(1)}, u32[]{:S(2)}, u32[]{:S(2)}) collective-permute-start(bf16[768,512]{1,0:T(8,128)(2,1)S(1)} %collective-permute-done.2.refs_2_), channel_id=1, source_target_pairs={{0,2},{1,7},{2,4},{3,1},{4,6},{5,3},{6,0},{7,5},{8,10},{9,15},{10,... | collective-permute-start | bytes 2359304 | tf_op jit(solution)/shard_map/ppermute | solution.py:44
  96.5 18.7 %collective-permute-start.15 = (bf16[4,512,512]{2,1,0:T(8,128)(2,1)S(1)}, bf16[4,512,512]{2,1,0:T(8,128)(2,1)S(1)}, u32[]{:S(2)}, u32[]{:S(2)}) collective-permute-start(bf16[4,512,512]{2,1,0:T(8,128)(2,1)S(1)} %copy-done.13), channel_id=1, source_target_pairs={{0,1},{1,0},{2,3},{3,2},{4,5},{5,4},{6,7},{7,6},{8,9},{9,8},{10,11... | collective-permute-start | bytes 6291464 | tf_op jit(solution)/shard_map/ppermute | solution.py:48
  109.7 2.3 %collective-permute-start.13 = (bf16[768,512]{1,0:T(8,128)(2,1)S(1)}, bf16[768,512]{1,0:T(8,128)(2,1)S(1)}, u32[]{:S(2)}, u32[]{:S(2)}) collective-permute-start(bf16[768,512]{1,0:T(8,128)(2,1)S(1)} %collective-permute-done.8.refs_0_.refs_6_), channel_id=1, source_target_pairs={{0,1},{1,0},{2,3},{3,2},{4,5},{5,4},{6,7},{7,6},{8,9},{9,8},{10,11... | collective-permute-start | bytes 2359304 | tf_op jit(solution)/shard_map/ppermute | solution.py:48
  115.0 2.4 %collective-permute-start.14 = (bf16[768,512]{1,0:T(8,128)(2,1)S(1)}, bf16[768,512]{1,0:T(8,128)(2,1)S(1)}, u32[]{:S(2)}, u32[]{:S(2)}) collective-permute-start(bf16[768,512]{1,0:T(8,128)(2,1)S(1)} %hidden_end.1.refs_0_.refs_8_), channel_id=1, source_target_pairs={{0,1},{1,0},{2,3},{3,2},{4,5},{5,4},{6,7},{7,6},{8,9},{9,8},{10,11... | collective-permute-start | bytes 2359304 | tf_op jit(solution)/shard_map/ppermute | solution.py:48
  120.4 16.3 %collective-permute-start.17 = (bf16[768,512]{1,0:T(8,128)(2,1)}, bf16[768,512]{1,0:T(8,128)(2,1)S(1)}, u32[]{:S(2)}, u32[]{:S(2)}) collective-permute-start(bf16[768,512]{1,0:T(8,128)(2,1)} %partial.5), channel_id=1, source_target_pairs={{0,2},{1,7},{2,4},{3,1},{4,6},{5,3},{6,0},{7,5},{8,10},{9,15},{10,... | collective-permute-start | bytes 2359304 | tf_op jit(solution)/shard_map/ppermute | solution.py:44
  129.3 17.1 %collective-permute-start.16 = (bf16[768,512]{1,0:T(8,128)(2,1)}, bf16[768,512]{1,0:T(8,128)(2,1)S(1)}, u32[]{:S(2)}, u32[]{:S(2)}) collective-permute-start(bf16[768,512]{1,0:T(8,128)(2,1)} %partial.4), channel_id=1, source_target_pairs={{0,6},{1,3},{2,0},{3,5},{4,2},{5,7},{6,4},{7,1},{8,14},{9,11},{10,... | collective-permute-start | bytes 2359304 | tf_op jit(solution)/shard_map/ppermute | solution.py:44
  138.2 13.3 %collective-permute-start.18 = (bf16[768,512]{1,0:T(8,128)(2,1)S(1)}, bf16[768,512]{1,0:T(8,128)(2,1)S(1)}, u32[]{:S(2)}, u32[]{:S(2)}) collective-permute-start(bf16[768,512]{1,0:T(8,128)(2,1)S(1)} %add_convert_fusion.1), channel_id=1, source_target_pairs={{0,2},{1,7},{2,4},{3,1},{4,6},{5,3},{6,0},{7,5},{8,10},{9,15},{10,... | collective-permute-start | bytes 2359304 | tf_op jit(solution)/shard_map/ppermute | solution.py:44
  (14 other events, 81.7 us)

commit v3 on v2

--- a/solution.py
+++ b/solution.py
@@ -9,6 +9,7 @@
 
 F32 = jnp.float32
 BF16 = jnp.bfloat16
+ANY = pl.BlockSpec(memory_space=pl.ANY)
 HBM = pl.BlockSpec(memory_space=pltpu.HBM)
 SMEM = pl.BlockSpec(memory_space=pltpu.SMEM)
 VMEM = pl.BlockSpec(memory_space=pltpu.VMEM)
@@ -56,12 +57,11 @@
     return lax.optimization_barrier((value, *others))[0]
 
 
-def ring_gather(own, beside=()):
+def ring_gather(own, beside=(), between=()):
     back = chip_step(own, 1)
-    on = chip_step(own, -1)
-    sibling = core_swap(own)
-    far = chip_step(after(back, *beside), 1)
-    return (own, sibling, back, core_swap(back), on, core_swap(on)), far
+    on = chip_step(after(own, *beside), -1)
+    far = chip_step(after(back, *between), 1)
+    return back, on, far
 
 
 def ring_order():
@@ -158,7 +158,7 @@
 
 def gate_up_kernel(*refs):
     pieces, weights = refs[:8], refs[8]
-    active, swish, slope, rows_in, w_gu, acc, row_sem, w_sem = refs[9:]
+    active, factors, rows_in, w_gu, acc, row_sem, w_sem = refs[9:]
     hidden = active.shape[1]
     for j in range(8):
         pltpu.make_async_copy(weights.at[j], w_gu.at[j], w_sem.at[j]).start()
@@ -177,9 +177,9 @@
     up_pre = acc[:, hidden:]
     sigmoid_gate = jax.nn.sigmoid(gate_pre)
     swish_gate = gate_pre * sigmoid_gate
-    swish[...] = swish_gate
     active[...] = (swish_gate * up_pre).astype(BF16)
-    slope[...] = up_pre * sigmoid_gate * (1.0 + gate_pre * (1.0 - sigmoid_gate))
+    factors[:, :hidden] = up_pre * sigmoid_gate * (1.0 + gate_pre * (1.0 - sigmoid_gate))
+    factors[:, hidden:] = swish_gate
 
 
 def gate_up_call(pieces, w_gu):
@@ -191,11 +191,10 @@
         gate_up_kernel,
         out_shape=(
             jax.ShapeDtypeStruct((rows, hidden), BF16),
-            jax.ShapeDtypeStruct((rows, hidden), F32),
-            jax.ShapeDtypeStruct((rows, hidden), F32),
+            jax.ShapeDtypeStruct((rows, both), F32),
         ),
         in_specs=[HBM] * 9,
-        out_specs=(VMEM, VMEM, VMEM),
+        out_specs=(VMEM, VMEM),
         scratch_shapes=[
             pltpu.VMEM((8, rows, width), BF16),
             pltpu.VMEM((8, width, both), BF16),
@@ -209,16 +208,19 @@
     )(*pin((*pieces, w_gu)))
 
 
-def hidden_kernel(first, count, *refs):
-    pieces, weights, before = refs[:count], refs[count], refs[count + 1]
-    total, rows_grad, w_dn, row_sem, w_sem = refs[count + 2 :]
+def add_hidden(first, pieces, own_w, other_w, total, rows_grad, w_dn, row_sem, own_sem, other_sem):
+    count = len(pieces)
+    hidden = own_w.shape[2]
     for j in range(count):
-        pltpu.make_async_copy(weights.at[first + j], w_dn.at[j], w_sem.at[j]).start()
+        own = w_dn.at[j, :, pl.ds(0, hidden)]
+        other = w_dn.at[j, :, pl.ds(hidden, hidden)]
+        pltpu.make_async_copy(own_w.at[first + j], own, own_sem.at[j]).start()
+        pltpu.make_async_copy(other_w.at[(first + j) ^ 1], other, other_sem.at[j]).start()
         pltpu.make_async_copy(pieces[j], rows_grad.at[j], row_sem.at[j]).start()
-    total[...] = jnp.zeros_like(total) if before is None else before[...]
 
     def step(j, carry):
-        wait_for(w_dn.at[j], w_sem.at[j])
+        wait_for(own_w.at[0], own_sem.at[j])
+        wait_for(other_w.at[0], other_sem.at[j])
         wait_for(rows_grad.at[j], row_sem.at[j])
         total[...] += jnp.dot(rows_grad[j], w_dn[j], preferred_element_type=F32)
         return carry
@@ -227,101 +229,131 @@
 
 
 def hidden_start_kernel(count, *refs):
-    hidden_kernel(0, count, *refs[: count + 1], None, *refs[count + 1 :])
-
-
-def hidden_end_kernel(first, count, *refs):
-    before, swish, slope, grads, rows_grad, w_dn, acc, row_sem, w_sem = refs[count + 1 :]
-    hidden_kernel(
-        first, count, *refs[: count + 1], before, acc, rows_grad, w_dn, row_sem, w_sem
+    total = refs[count + 2]
+    total[...] = jnp.zeros_like(total)
+    add_hidden(0, refs[:count], *refs[count : count + 3], *refs[count + 3 :])
+
+
+def hidden_start_call(pieces, own_w, other_w):
+    rows, width = pieces[0].shape
+    both, count = 2 * own_w.shape[2], len(pieces)
+    dma = pltpu.SemaphoreType.DMA((count,))
+    return pl.pallas_call(
+        functools.partial(hidden_start_kernel, count),
+        out_shape=jax.ShapeDtypeStruct((rows, both), F32),
+        in_specs=[ANY] * count + [HBM] * 2,
+        out_specs=VMEM,
+        scratch_shapes=[
+            pltpu.VMEM((count, rows, width), BF16),
+            pltpu.VMEM((count, width, both), BF16),
+            dma,
+            dma,
+            dma,
+        ],
+        compiler_params=params(16),
+        cost_estimate=cost(rows, count * width, both, count * width * (rows + both) * 2),
+        name="hidden_start",
+    )(*pieces, *pin((own_w, other_w)))
+
+
+def start_weights(own_w, other_w, block, buffer, own_sem, other_sem):
+    both = own_w.shape[1]
+    pltpu.make_async_copy(own_w.at[block], buffer.at[pl.ds(0, both), :], own_sem).start()
+    pltpu.make_async_copy(other_w.at[block], buffer.at[pl.ds(both, both), :], other_sem).start()
+
+
+def hidden_end_kernel(first, count, block, *refs):
+    pieces = refs[:count]
+    own_dn, other_dn, own_w, other_w, before, own_factors, other_factors = refs[count : count + 7]
+    grads, out = refs[count + 7 : count + 9]
+    total, rows_grad, w_dn, w_gu, result = refs[count + 9 : count + 14]
+    row_sem, own_sem, other_sem, w_sem, out_sem = refs[count + 14 :]
+    start_weights(own_w, other_w, block, w_gu, w_sem.at[0], w_sem.at[1])
+    total[...] = before[...]
+    add_hidden(
+        first, pieces, own_dn, other_dn, total, rows_grad, w_dn, row_sem, own_sem, other_sem
     )
-    hidden = acc.shape[1]
-    hidden_grad = acc[...]
-    grads[:, :hidden] = (hidden_grad * slope[...]).astype(BF16)
-    grads[:, hidden:] = (hidden_grad * swish[...]).astype(BF16)
-
-
-def hidden_scratch(count, rows, width, hidden):
-    dma = pltpu.SemaphoreType.DMA((count,))
-    return [pltpu.VMEM((count, rows, width), BF16), pltpu.VMEM((count, width, hidden), BF16)], [
-        dma,
-        dma,
-    ]
-
-
-def hidden_start_call(pieces, w_dn):
+    hidden = own_dn.shape[2]
+    for core, factors in enumerate((own_factors, other_factors)):
+        hidden_grad = total[:, core * hidden : (core + 1) * hidden]
+        at = 2 * core * hidden
+        grads[:, at : at + hidden] = (hidden_grad * factors[:, :hidden]).astype(BF16)
+        grads[:, at + hidden : at + 2 * hidden] = (hidden_grad * factors[:, hidden:]).astype(BF16)
+    wait_for(own_w.at[0], w_sem.at[0])
+    wait_for(other_w.at[0], w_sem.at[1])
+    result[...] = jnp.dot(grads[...], w_gu[...], preferred_element_type=F32).astype(BF16)
+    copy = pltpu.make_async_copy(result, out, out_sem)
+    copy.start()
+    copy.wait()
+
+
+def hidden_end_call(pieces, own_dn, other_dn, own_w, other_w, before, factors, others, block):
     rows, width = pieces[0].shape
-    hidden, count = w_dn.shape[2], len(pieces)
-    buffers, sems = hidden_scratch(count, rows, width, hidden)
-    return pl.pallas_call(
-        functools.partial(hidden_start_kernel, count),
-        out_shape=jax.ShapeDtypeStruct((rows, hidden), F32),
-        in_specs=[HBM] * (count + 1),
-        out_specs=VMEM,
-        scratch_shapes=buffers + sems,
-        compiler_params=params(15),
-        cost_estimate=cost(rows, count * width, hidden, count * width * (rows + hidden) * 2),
-        name="hidden_start",
-    )(*pin((*pieces, w_dn)))
-
-
-def hidden_end_call(pieces, w_dn, before, swish, slope):
-    rows, width = pieces[0].shape
-    hidden, count = w_dn.shape[2], len(pieces)
-    buffers, sems = hidden_scratch(count, rows, width, hidden)
-    return pl.pallas_call(
-        functools.partial(hidden_end_kernel, w_dn.shape[0] - count, count),
-        out_shape=jax.ShapeDtypeStruct((rows, 2 * hidden), BF16),
-        in_specs=[HBM] * (count + 1) + [VMEM] * 3,
-        out_specs=VMEM,
-        scratch_shapes=buffers + [pltpu.VMEM((rows, hidden), F32)] + sems,
-        compiler_params=params(12),
-        cost_estimate=cost(rows, count * width, hidden, count * width * (rows + hidden) * 2),
+    both, count = 2 * own_dn.shape[2], len(pieces)
+    dma = pltpu.SemaphoreType.DMA
+    return pl.pallas_call(
+        functools.partial(hidden_end_kernel, own_dn.shape[0] - count, count, block),
+        out_shape=(
+            jax.ShapeDtypeStruct((rows, 2 * both), BF16),
+            pltpu.HBM((rows, width), BF16),
+        ),
+        in_specs=[ANY] * count + [HBM] * 4 + [VMEM] * 3,
+        out_specs=(VMEM, HBM),
+        scratch_shapes=[
+            pltpu.VMEM((rows, both), F32),
+            pltpu.VMEM((count, rows, width), BF16),
+            pltpu.VMEM((count, width, both), BF16),
+            pltpu.VMEM((2 * both, width), BF16),
+            pltpu.VMEM((rows, width), BF16),
+            dma((count,)),
+            dma((count,)),
+            dma((count,)),
+            dma((2,)),
+            dma,
+        ],
+        compiler_params=params(20),
+        cost_estimate=cost(rows, (count + 2) * width, both, count * width * (rows + both) * 2),
         name="hidden_end",
-    )(*pin((*pieces, w_dn)), before, swish, slope)
+    )(*pieces, *pin((own_dn, other_dn, own_w, other_w)), before, factors, others)
 
 
 def partial_kernel(blocks, *refs):
     count = len(blocks)
-    grads, other, own_w, other_w = refs[:4]
-    outs = refs[4 : 4 + count]
-    own_buf, other_buf, result, own_sem, other_sem, out_sem = refs[4 + count :]
+    grads, own_w, other_w = refs[:3]
+    outs = refs[3 : 3 + count]
+    w_gu, result, own_sem, other_sem, out_sem = refs[3 + count :]
     for i, j in enumerate(blocks):
-        pltpu.make_async_copy(own_w.at[j], own_buf.at[i], own_sem.at[i]).start()
-        pltpu.make_async_copy(other_w.at[j], other_buf.at[i], other_sem.at[i]).start()
+        start_weights(own_w, other_w, j, w_gu.at[i], own_sem.at[i], other_sem.at[i])
     for i in range(count):
-        wait_for(own_buf.at[i], own_sem.at[i])
-        total = jnp.dot(grads[...], own_buf[i], preferred_element_type=F32)
-        wait_for(other_buf.at[i], other_sem.at[i])
-        total = total + jnp.dot(other[...], other_buf[i], preferred_element_type=F32)
-        result[i] = total.astype(BF16)
+        wait_for(own_w.at[0], own_sem.at[i])
+        wait_for(other_w.at[0], other_sem.at[i])
+        result[i] = jnp.dot(grads[...], w_gu[i], preferred_element_type=F32).astype(BF16)
         pltpu.make_async_copy(result.at[i], outs[i], out_sem.at[i]).start()
     finish(result, out_sem)
 
 
-def partial_call(grads, other, own_w, other_w, blocks):
+def partial_call(grads, own_w, other_w, blocks):
     both, width = own_w.shape[1:]
     rows, count = grads.shape[0], len(blocks)
     dma = pltpu.SemaphoreType.DMA((count,))
     return pl.pallas_call(
         functools.partial(partial_kernel, blocks),
         out_shape=[pltpu.HBM((rows, width), BF16)] * count,
-        in_specs=[VMEM, VMEM, HBM, HBM],
+        in_specs=[VMEM, HBM, HBM],
         out_specs=[HBM] * count,
         scratch_shapes=[
-            pltpu.VMEM((count, both, width), BF16),
-            pltpu.VMEM((count, both, width), BF16),
+            pltpu.VMEM((count, 2 * both, width), BF16),
             pltpu.VMEM((count, rows, width), BF16),
             dma,
             dma,
             dma,
         ],
-        compiler_params=params(12),
+        compiler_params=params(14),
         cost_estimate=cost(
             rows, 2 * both, count * width, count * 2 * width * (rows + 2 * both) * 2
         ),
         name="partial",
-    )(grads, other, *pin((own_w, other_w)))
+    )(grads, *pin((own_w, other_w)))
 
 
 def down_total_kernel(order, *refs):
@@ -373,7 +405,10 @@
     def step(j, carry):
         wait_for(rows_in.at[j], row_sem.at[j])
         both = lax.dot_general(
-            rows_in[j], grads[...], (((0,), (0,)), ((), ())), preferred_element_type=F32
+            rows_in[j],
+            grads[:, : 2 * hidden],
+            (((0,), (0,)), ((), ())),
+            preferred_element_type=F32,
         )
         out_gate[j] = both[:, :hidden].astype(BF16)
         out_up[j] = both[:, hidden:].astype(BF16)
@@ -389,7 +424,7 @@
 
 def gate_up_total_call(order, pieces, grads):
     width = pieces[0].shape[1]
-    rows, both = grads.shape
+    rows, both = grads.shape[0], grads.shape[1] // 2
     hidden = both // 2
     dma = pltpu.SemaphoreType.DMA((8,))
     total = jax.ShapeDtypeStruct((8 * width, hidden), BF16)
@@ -430,31 +465,31 @@
     w_gu, own_w, send_w, w_dn = prepare_call(order, w_gate[0], w_up[0], w_down[0])
     arrived_in = after(exchange(packed(tokens_in)), w_gu)
     arrived_grad = exchange(after(packed_grad, arrived_in))
-    near_in, far_in = ring_gather(arrived_in)
-    pieces_in = (*near_in, far_in, core_swap(far_in))
-    other_w = core_swap(after(send_w, near_in[2]))
-    active, swish, slope = gate_up_call(pieces_in, w_gu)
-    near_grad, far_grad = ring_gather(after(arrived_grad, far_in), (active,))
-    before = hidden_start_call(near_grad, w_dn)
-    far_grad = after(far_grad, before)
-    far_grad = (far_grad, core_swap(far_grad))
-    pieces_grad = (*near_grad, *far_grad)
-    grads = hidden_end_call(far_grad, w_dn, before, swish, slope)
-    other = core_swap(grads)
-
-    def partial_of(*blocks):
-        return partial_call(grads, other, own_w, other_w, blocks)
-
-    far = chip_step(partial_of(3)[0], 1)
-    back = chip_step(partial_of(1)[0], -1)
-    own, on = partial_of(0, 2)
-    down_total = down_total_call(order, pieces_grad, active.T)
-    joined = on.astype(F32) + after(far, down_total).astype(F32)
+    back, on, far = ring_gather(arrived_in)
+    pieces_in = (arrived_in, core_swap(arrived_in), back, core_swap(back), on, core_swap(on))
+    pieces_in = (*pieces_in, far, core_swap(far))
+    other_w = core_swap(after(send_w, back))
+    other_dn = core_swap(after(w_dn, back))
+    active, factors = gate_up_call(pieces_in, w_gu)
+    back, on, far = ring_gather(after(arrived_grad, far))
+    others = core_swap(factors)
+    near = (arrived_grad, core_swap(arrived_grad), back, core_swap(back), on, core_swap(on))
+    before = hidden_start_call(near, w_dn, other_dn)
+    far = after(far, before, active)
+    late = (far, core_swap(far))
+    pieces_grad = (*near, *late)
+    grads, far = hidden_end_call(
+        late, w_dn, other_dn, own_w, other_w, before, factors, others, 3
+    )
+    far = chip_step(far, 1)
+    back, own, on = partial_call(grads, own_w, other_w, (1, 0, 2))
+    back = chip_step(back, -1)
+    joined = on.astype(F32) + far.astype(F32)
     on = chip_step(joined.astype(BF16), 1)
     total = (own.astype(F32) + back.astype(F32) + on.astype(F32)).astype(BF16)
-
+    down_total = down_total_call(order, pieces_grad, active.T)
     gate_total, up_total = gate_up_total_call(order, pieces_in, grads)
-    returned = exchange(after(total, gate_total))
+    returned = exchange(total)
     grad_in = jnp.einsum("st,sd->td", onehot, returned, preferred_element_type=F32)
     return (grad_in.astype(BF16), gate_total[None], up_total[None], down_total[None])
 

time: 184 us -> 171 us (0.929)
  blocking collectives: 30.9 us -> 0 us
  waiting for transfers between devices: 67.8 us -> 80.1 us
  starting transfers between devices: 30 us -> 38.7 us
  local copies, waits for them, and re-layouts: 4.44 us -> 0.61 us
    all_to_all x1 -> x0, blocking collectives: 30.9 us -> none  [exchange(): lax.all_to_all(value, 'node', split_axis=0, concat_axis=0, tiled=True)]
    ppermute x9, waiting for transfers between devices: 36.5 us -> 51.4 us  [chip_step(): return lax.ppermute(value, 'local', pairs)]
    all_to_all x2 -> x3, starting transfers between devices: 16.1 us -> 22.5 us  [exchange(): lax.all_to_all(value, 'node', split_axis=0, concat_axis=0, tiled=True)]
    pallas_call x3 -> x1, Pallas kernels: 10.4 us -> 5.14 us  [partial_call(): pl.pallas_call(functools.partial(partial_kernel, blocks), out_shape=[pltp...]
    unnamed x34 -> x36, local copies, waits for them, and re-layouts: 4.1 us -> 0.25 us
    pallas_call x1, Pallas kernels: 2.11 us -> 5.06 us  [hidden_end_call(): pl.pallas_call(functools.partial(hidden_end_kernel, own_dn.shape[0] - cou...]
    ppermute x10 -> x11, waiting for transfers between devices: 4.44 us -> 2.21 us  [core_swap(): lax.ppermute(value, 'local', [(i, i ^ 1) for i in range(lax.axis_size('lo...]
    ppermute x9, starting transfers between devices: 11.7 us -> 13.8 us  [chip_step(): return lax.ppermute(value, 'local', pairs)]
  transfers between devices with their start and end apart: 21 -> 23, of which waited for: 10 -> 12; matrix products, arithmetic and copies ran while one was open for 2% -> 2% of each run, Pallas kernels for 22% -> 22%
where the time goes in v3:
time: 171 us; the launch traced here: 170 us
  waiting for transfers between devices  80.1 us (47%)
  Pallas kernels  42.5 us (25%)
  starting transfers between devices  38.7 us (23%)
  matrix products  3.58 us (2%)
  other arithmetic  3.48 us (2%)
    ppermute x9, waiting for transfers between devices, chip_step(): return lax.ppermute(value, 'local', pairs)  51.4 us
    all_to_all x3, waiting for transfers between devices, exchange(): lax.all_to_all(value, 'node', split_axis=0, concat_axis=0, tiled=True)  26.4 us
    all_to_all x3, starting transfers between devices, exchange(): lax.all_to_all(value, 'node', split_axis=0, concat_axis=0, tiled=True)  22.5 us
    ppermute x9, starting transfers between devices, chip_step(): return lax.ppermute(value, 'local', pairs)  13.8 us
    pallas_call x1, Pallas kernels, prepare_call(): pl.pallas_call(prepare_kernel, out_shape=(pltpu.HBM((8, width, 2 * hidden...  7.75 us
    pallas_call x1, Pallas kernels, gate_up_total_call(): pl.pallas_call(gate_up_total_kernel, out_shape=(total, total), in_specs=[...  7.66 us
    pallas_call x1, Pallas kernels, gate_up_call(): pl.pallas_call(gate_up_kernel, out_shape=(jax.ShapeDtypeStruct((rows, hid...  6.31 us
    pallas_call x1, Pallas kernels, down_total_call(): pl.pallas_call(down_total_kernel, out_shape=jax.ShapeDtypeStruct((hidden,...  5.49 us
  transfers between devices with their start and end apart: 23, of which 12 were waited for; matrix products, arithmetic and copies ran while one was open for 2% of the time, Pallas kernels for 22%

profile of v3, /device:TPU:32, one launch (start us, length us, event | category | flops | bytes accessed | tf_op | source)
XLA Modules:
  0.0 170.1 jit_solution(16516986427661841211)
XLA Ops:
  3.1 11.2 %all-to-all-start = ((bf16[32,24,512]{2,1,0:T(8,128)(2,1)}), bf16[32,24,512]{2,1,0:T(8,128)(2,1)S(1)}, u32[]{:S(2)}, u32[]{:S(2)}) async-start(bf16[32,24,512]{2,1,0:T(8,128)(2,1)} %bitcast.2), calls=%async_computation | async-start | bytes 1572864 | tf_op jit(solution)/shard_map/all_to_all | solution.py:461
  15.7 7.7 %prepare.1 = (bf16[8,512,512]{2,1,0:T(8,128)(2,1)}, bf16[4,512,512]{2,1,0:T(8,128)(2,1)}, bf16[4,512,512]{2,1,0:T(8,128)(2,1)}, bf16[8,512,256]{2,1,0:T(8,128)(2,1)}) custom-call(s32[8]{0:T(128)S(1)} %stack.35.order, bf16[4096,256]{1,0:T(8,128)(2,1)} %bitcast.40, bf16[4096,256]{1,0:T(8,128)(2,1)} %bitcast.41, bf16[4096,256]{1,0:T(8,128)(2,1)} %bitcast.42, ...), custom_call_target="tpu_custom_call" | custom-call | flops 1610612736 | bytes 16777216 | tf_op jit(solution)/shard_map/prepare/pallas_call | solution.py:134
  23.5 13.9 %all-to-all-done = bf16[32,24,512]{2,1,0:T(8,128)(2,1)S(1)} async-done(((bf16[32,24,512]{2,1,0:T(8,128)(2,1)}), bf16[32,24,512]{2,1,0:T(8,128)(2,1)S(1)}, u32[]{:S(2)}, u32[]{:S(2)}) %all-to-all-start) | async-done | bytes 786464 | tf_op jit(solution)/shard_map/all_to_all | solution.py:461
  39.0 4.9 %all-to-all-start.1 = ((bf16[32,24,512]{2,1,0:T(8,128)(2,1)}), bf16[32,24,512]{2,1,0:T(8,128)(2,1)S(1)}, u32[]{:S(2)}, u32[]{:S(2)}) async-start(bf16[32,24,512]{2,1,0:T(8,128)(2,1)} %bitcast.15), calls=%async_computation.1 | async-start | bytes 1572864 | tf_op jit(solution)/shard_map/all_to_all | solution.py:461
  43.9 1.7 %collective-permute-start.11 = (bf16[768,512]{1,0:T(8,128)(2,1)S(1)}, bf16[768,512]{1,0:T(8,128)(2,1)S(1)}, u32[]{:S(2)}, u32[]{:S(2)}) collective-permute-start(bf16[768,512]{1,0:T(8,128)(2,1)S(1)} %bitcast.49), channel_id=1, source_target_pairs={{0,6},{1,3},{2,0},{3,5},{4,2},{5,7},{6,4},{7,1},{8,14},{9,11},{10,... | collective-permute-start | bytes 2359304 | tf_op jit(solution)/shard_map/ppermute | solution.py:45
  45.7 7.7 %collective-permute-done.refs_2_ = bf16[768,512]{1,0:T(8,128)(2,1)S(1)} collective-permute-done((bf16[768,512]{1,0:T(8,128)(2,1)S(1)}, bf16[768,512]{1,0:T(8,128)(2,1)S(1)}, u32[]{:S(2)}, u32[]{:S(2)}) %collective-permute-start) | collective-permute-done | bytes 786464 | tf_op jit(solution)/shard_map/ppermute | solution.py:45
  53.4 2.0 %collective-permute-start.1 = (bf16[768,512]{1,0:T(8,128)(2,1)S(1)}, bf16[768,512]{1,0:T(8,128)(2,1)}, u32[]{:S(2)}, u32[]{:S(2)}) collective-permute-start(bf16[768,512]{1,0:T(8,128)(2,1)S(1)} %collective-permute-done.refs_2_), channel_id=1, source_target_pairs={{0,2},{1,7},{2,4},{3,1},{4,6},{5,3},{6,0},{7,5},{8,10},{9,15},{10,... | collective-permute-start | bytes 2359304 | tf_op jit(solution)/shard_map/ppermute | solution.py:45
  56.0 6.7 %collective-permute-done.11.refs_4_ = bf16[768,512]{1,0:T(8,128)(2,1)S(1)} collective-permute-done((bf16[768,512]{1,0:T(8,128)(2,1)S(1)}, bf16[768,512]{1,0:T(8,128)(2,1)S(1)}, u32[]{:S(2)}, u32[]{:S(2)}) %collective-permute-start.11) | collective-permute-done | bytes 786464 | tf_op jit(solution)/shard_map/ppermute | solution.py:45
  62.7 4.6 %all-to-all-done.1 = bf16[32,24,512]{2,1,0:T(8,128)(2,1)S(1)} async-done(((bf16[32,24,512]{2,1,0:T(8,128)(2,1)}), bf16[32,24,512]{2,1,0:T(8,128)(2,1)S(1)}, u32[]{:S(2)}, u32[]{:S(2)}) %all-to-all-start.1) | async-done | bytes 786464 | tf_op jit(solution)/shard_map/all_to_all | solution.py:461
  68.5 2.9 %collective-permute-start.6 = (bf16[768,512]{1,0:T(8,128)(2,1)S(1)}, bf16[768,512]{1,0:T(8,128)(2,1)S(1)}, u32[]{:S(2)}, u32[]{:S(2)}) collective-permute-start(bf16[768,512]{1,0:T(8,128)(2,1)S(1)} %bitcast.36), channel_id=1, source_target_pairs={{0,6},{1,3},{2,0},{3,5},{4,2},{5,7},{6,4},{7,1},{8,14},{9,11},{10,... | collective-permute-start | bytes 2359304 | tf_op jit(solution)/shard_map/ppermute | solution.py:45
  71.3 17.9 %collective-permute-done.2.refs_2_ = bf16[768,512]{1,0:T(8,128)(2,1)S(1)} collective-permute-done((bf16[768,512]{1,0:T(8,128)(2,1)S(1)}, bf16[768,512]{1,0:T(8,128)(2,1)S(1)}, u32[]{:S(2)}, u32[]{:S(2)}) %collective-permute-start.2) | collective-permute-done | bytes 786464 | tf_op jit(solution)/shard_map/ppermute | solution.py:45
  90.3 6.3 %gate_up.1 = (bf16[768,256]{1,0:T(8,128)(2,1)S(1)}, f32[768,512]{1,0:T(8,128)S(1)}) custom-call(bf16[768,512]{1,0:T(8,128)(2,1)} %bitcast.51, bf16[768,512]{1,0:T(8,128)(2,1)} %collective-permute-done.9.refs_1_, bf16[768,512]{1,0:T(8,128)(2,1)} %copy-done.15, bf16[768,512]{1,0:T(8,128)(2,1)} %collective-permute-done.10.refs_3_, bf16[768,512]{1,0:T(8,128)(2,1)} %copy-done.16, ...), custom_call_target="tpu_custom_call" | custom-call | flops 3221225472 | bytes 10485760 | tf_op jit(solution)/shard_map/gate_up/pallas_call | solution.py:190
  97.1 5.1 %hidden_start.1.refs_6_ = f32[768,512]{1,0:T(8,128)S(1)} custom-call(bf16[768,512]{1,0:T(8,128)(2,1)S(1)} %bitcast.37, bf16[768,512]{1,0:T(8,128)(2,1)S(1)} %collective-permute-done.4.refs_1_, bf16[768,512]{1,0:T(8,128)(2,1)S(1)} %collective-permute-done.2.refs_2_, bf16[768,512]{1,0:T(8,128)(2,1)S(1)} %collective-permute-done.5.refs_3_, ...), custom_call_target="tpu_custom_call" | custom-call | flops 2415919104 | bytes 7864320 | tf_op jit(solution)/shard_map/hidden_start/pallas_call | solution.py:241
  102.6 2.2 %collective-permute-done.14.refs_1_.refs_7_ = bf16[768,512]{1,0:T(8,128)(2,1)S(1)} collective-permute-done((bf16[768,512]{1,0:T(8,128)(2,1)S(1)}, bf16[768,512]{1,0:T(8,128)(2,1)S(1)}, u32[]{:S(2)}, u32[]{:S(2)}) %collective-permute-start.14) | collective-permute-done | bytes 786464 | tf_op jit(solution)/shard_map/ppermute | solution.py:49
  104.8 5.1 %hidden_end.1 = (bf16[768,1024]{1,0:T(8,128)(2,1)S(1)}, bf16[768,512]{1,0:T(8,128)(2,1)}) custom-call(bf16[768,512]{1,0:T(8,128)(2,1)S(1)} %collective-permute-done.3.refs_0_.refs_6_, bf16[768,512]{1,0:T(8,128)(2,1)S(1)} %collective-permute-done.14.refs_1_.refs_7_, bf16[8,512,256]{2,1,0:T(8,128)(2,1)} %get-tuple-element.30.refs_6_.refs_2_, ...), custom_call_target="tpu_custom_call" | custom-call | flops 1610612736 | bytes 2621440 | tf_op jit(solution)/shard_map/hidden_end/pallas_call | solution.py:294
  111.6 5.1 %partial.1 = (bf16[768,512]{1,0:T(8,128)(2,1)}, bf16[768,512]{1,0:T(8,128)(2,1)}, bf16[768,512]{1,0:T(8,128)(2,1)}) custom-call(bf16[768,1024]{1,0:T(8,128)(2,1)S(1)} %get-tuple-element.37.refs_0_.refs_8_, bf16[4,512,512]{2,1,0:T(8,128)(2,1)} %get-tuple-element.33.refs_4_.refs_1_, bf16[4,512,512]{2,1,0:T(8,128)(2,1)} %copy-done.11), custom_call_target="tpu_custom_call" | custom-call | flops 2415919104 | bytes 11010048 | tf_op jit(solution)/shard_map/partial/pallas_call | solution.py:339
  118.4 6.1 %collective-permute-done.18 = bf16[768,512]{1,0:T(8,128)(2,1)S(1)} collective-permute-done((bf16[768,512]{1,0:T(8,128)(2,1)}, bf16[768,512]{1,0:T(8,128)(2,1)S(1)}, u32[]{:S(2)}, u32[]{:S(2)}) %collective-permute-start.18) | collective-permute-done | bytes 786464 | tf_op jit(solution)/shard_map/ppermute | solution.py:45
  125.9 1.8 %collective-permute-start.19 = (bf16[768,512]{1,0:T(8,128)(2,1)S(1)}, bf16[768,512]{1,0:T(8,128)(2,1)S(1)}, u32[]{:S(2)}, u32[]{:S(2)}) collective-permute-start(bf16[768,512]{1,0:T(8,128)(2,1)S(1)} %add_convert_fusion.1), channel_id=1, source_target_pairs={{0,2},{1,7},{2,4},{3,1},{4,6},{5,3},{6,0},{7,5},{8,10},{9,15},{10,... | collective-permute-start | bytes 2359304 | tf_op jit(solution)/shard_map/ppermute | solution.py:45
  127.7 3.7 %collective-permute-done.17 = bf16[768,512]{1,0:T(8,128)(2,1)S(1)} collective-permute-done((bf16[768,512]{1,0:T(8,128)(2,1)}, bf16[768,512]{1,0:T(8,128)(2,1)S(1)}, u32[]{:S(2)}, u32[]{:S(2)}) %collective-permute-start.17) | collective-permute-done | bytes 786464 | tf_op jit(solution)/shard_map/ppermute | solution.py:45
  131.4 8.9 %collective-permute-done.19 = bf16[768,512]{1,0:T(8,128)(2,1)S(1)} collective-permute-done((bf16[768,512]{1,0:T(8,128)(2,1)S(1)}, bf16[768,512]{1,0:T(8,128)(2,1)S(1)}, u32[]{:S(2)}, u32[]{:S(2)}) %collective-permute-start.19) | collective-permute-done | bytes 786464 | tf_op jit(solution)/shard_map/ppermute | solution.py:45
  141.5 6.4 %all-to-all-start.2 = ((bf16[32,24,512]{2,1,0:T(8,128)(2,1)}), bf16[32,24,512]{2,1,0:T(8,128)(2,1)S(1)}, u32[]{:S(2)}, u32[]{:S(2)}) async-start(bf16[32,24,512]{2,1,0:T(8,128)(2,1)} %bitcast.46), calls=%async_computation.2 | async-start | bytes 1572864 | tf_op jit(solution)/shard_map/all_to_all | solution.py:461
  148.1 5.5 %down_total.1 = bf16[256,4096]{1,0:T(8,128)(2,1)} custom-call(s32[8]{0:T(128)S(1)} %stack.35.order, bf16[768,512]{1,0:T(8,128)(2,1)} %bitcast.38, bf16[768,512]{1,0:T(8,128)(2,1)} %copy-done.5, bf16[768,512]{1,0:T(8,128)(2,1)} %copy-done.4, bf16[768,512]{1,0:T(8,128)(2,1)} %copy-done.7, bf16[768,512]{1,0:T(8,128)(2,1)} %copy-done.6, ...), custom_call_target="tpu_custom_call" | custom-call | flops 1610612736 | bytes 8388608 | tf_op jit(solution)/shard_map/down_total/pallas_call | solution.py:381
  153.6 7.7 %gate_up_total.1 = (bf16[4096,256]{1,0:T(8,128)(2,1)}, bf16[4096,256]{1,0:T(8,128)(2,1)}) custom-call(s32[8]{0:T(128)S(1)} %stack.35.order, bf16[768,512]{1,0:T(8,128)(2,1)} %bitcast.52, bf16[768,512]{1,0:T(8,128)(2,1)} %collective-permute-done.9.refs_1_, bf16[768,512]{1,0:T(8,128)(2,1)} %copy-done.15, bf16[768,512]{1,0:T(8,128)(2,1)} %collective-permute-done.10.refs_3_, ...), custom_call_target="tpu_custom_call" | custom-call | flops 3221225472 | bytes 10485760 | tf_op jit(solution)/shard_map/gate_up_total/pallas_call | solution.py:431
  161.2 7.9 %all-to-all-done.2 = bf16[32,24,512]{2,1,0:T(8,128)(2,1)S(1)} async-done(((bf16[32,24,512]{2,1,0:T(8,128)(2,1)}), bf16[32,24,512]{2,1,0:T(8,128)(2,1)S(1)}, u32[]{:S(2)}, u32[]{:S(2)}) %all-to-all-start.2) | async-done | bytes 786464 | tf_op jit(solution)/shard_map/all_to_all | solution.py:461
  (77 shorter events, 15.9 us)
Async XLA Ops:
  3.1 34.4 %all-to-all-start = ((bf16[32,24,512]{2,1,0:T(8,128)(2,1)}), bf16[32,24,512]{2,1,0:T(8,128)(2,1)S(1)}, u32[]{:S(2)}, u32[]{:S(2)}) async-start(bf16[32,24,512]{2,1,0:T(8,128)(2,1)} %bitcast.2), calls=%async_computation | async-start | bytes 1572864 | tf_op jit(solution)/shard_map/all_to_all | solution.py:461
  37.4 52.7 %copy-start.12 = (bf16[32,24,512]{2,1,0:T(8,128)(2,1)}, bf16[32,24,512]{2,1,0:T(8,128)(2,1)S(1)}, u32[]{:S(2)}) copy-start(bf16[32,24,512]{2,1,0:T(8,128)(2,1)S(1)} %all-to-all-done) | copy-start | bytes 2359300
  37.4 16.0 %collective-permute-start = (bf16[768,512]{1,0:T(8,128)(2,1)S(1)}, bf16[768,512]{1,0:T(8,128)(2,1)S(1)}, u32[]{:S(2)}, u32[]{:S(2)}) collective-permute-start(bf16[768,512]{1,0:T(8,128)(2,1)S(1)} %bitcast.48), channel_id=1, source_target_pairs={{0,2},{1,7},{2,4},{3,1},{4,6},{5,3},{6,0},{7,5},{8,10},{9,15},{10,... | collective-permute-start | bytes 2359304 | tf_op jit(solution)/shard_map/ppermute | solution.py:45
  39.0 28.3 %all-to-all-start.1 = ((bf16[32,24,512]{2,1,0:T(8,128)(2,1)}), bf16[32,24,512]{2,1,0:T(8,128)(2,1)S(1)}, u32[]{:S(2)}, u32[]{:S(2)}) async-start(bf16[32,24,512]{2,1,0:T(8,128)(2,1)} %bitcast.15), calls=%async_computation.1 | async-start | bytes 1572864 | tf_op jit(solution)/shard_map/all_to_all | solution.py:461
  43.9 18.7 %collective-permute-start.11 = (bf16[768,512]{1,0:T(8,128)(2,1)S(1)}, bf16[768,512]{1,0:T(8,128)(2,1)S(1)}, u32[]{:S(2)}, u32[]{:S(2)}) collective-permute-start(bf16[768,512]{1,0:T(8,128)(2,1)S(1)} %bitcast.49), channel_id=1, source_target_pairs={{0,6},{1,3},{2,0},{3,5},{4,2},{5,7},{6,4},{7,1},{8,14},{9,11},{10,... | collective-permute-start | bytes 2359304 | tf_op jit(solution)/shard_map/ppermute | solution.py:45
  53.4 14.2 %collective-permute-start.1 = (bf16[768,512]{1,0:T(8,128)(2,1)S(1)}, bf16[768,512]{1,0:T(8,128)(2,1)}, u32[]{:S(2)}, u32[]{:S(2)}) collective-permute-start(bf16[768,512]{1,0:T(8,128)(2,1)S(1)} %collective-permute-done.refs_2_), channel_id=1, source_target_pairs={{0,2},{1,7},{2,4},{3,1},{4,6},{5,3},{6,0},{7,5},{8,10},{9,15},{10,... | collective-permute-start | bytes 2359304 | tf_op jit(solution)/shard_map/ppermute | solution.py:45
  55.4 41.2 %collective-permute-start.8 = (bf16[8,512,256]{2,1,0:T(8,128)(2,1)}, bf16[8,512,256]{2,1,0:T(8,128)(2,1)}, u32[]{:S(2)}, u32[]{:S(2)}) collective-permute-start(bf16[8,512,256]{2,1,0:T(8,128)(2,1)} %get-tuple-element.30.refs_6_.refs_2_), channel_id=1, source_target_pairs={{0,1},{1,0},{2,3},{3,2},{4,5},{5,4},{6,7},{7,6},{8,9},{9,8},{10,11... | collective-permute-start | bytes 6291464 | tf_op jit(solution)/shard_map/ppermute | solution.py:49
  55.4 12.5 %collective-permute-start.9 = (bf16[768,512]{1,0:T(8,128)(2,1)S(1)}, bf16[768,512]{1,0:T(8,128)(2,1)}, u32[]{:S(2)}, u32[]{:S(2)}) collective-permute-start(bf16[768,512]{1,0:T(8,128)(2,1)S(1)} %bitcast.50), channel_id=1, source_target_pairs={{0,1},{1,0},{2,3},{3,2},{4,5},{5,4},{6,7},{7,6},{8,9},{9,8},{10,11... | collective-permute-start | bytes 2359304 | tf_op jit(solution)/shard_map/ppermute | solution.py:49
  56.0 12.0 %collective-permute-start.10 = (bf16[768,512]{1,0:T(8,128)(2,1)S(1)}, bf16[768,512]{1,0:T(8,128)(2,1)}, u32[]{:S(2)}, u32[]{:S(2)}) collective-permute-start(bf16[768,512]{1,0:T(8,128)(2,1)S(1)} %collective-permute-done.refs_2_), channel_id=1, source_target_pairs={{0,1},{1,0},{2,3},{3,2},{4,5},{5,4},{6,7},{7,6},{8,9},{9,8},{10,11... | collective-permute-start | bytes 2359304 | tf_op jit(solution)/shard_map/ppermute | solution.py:49
  62.7 5.8 %collective-permute-start.12 = (bf16[768,512]{1,0:T(8,128)(2,1)S(1)}, bf16[768,512]{1,0:T(8,128)(2,1)}, u32[]{:S(2)}, u32[]{:S(2)}) collective-permute-start(bf16[768,512]{1,0:T(8,128)(2,1)S(1)} %collective-permute-done.11.refs_4_), channel_id=1, source_target_pairs={{0,1},{1,0},{2,3},{3,2},{4,5},{5,4},{6,7},{7,6},{8,9},{9,8},{10,11... | collective-permute-start | bytes 2359304 | tf_op jit(solution)/shard_map/ppermute | solution.py:49
  67.6 21.6 %collective-permute-start.2 = (bf16[768,512]{1,0:T(8,128)(2,1)S(1)}, bf16[768,512]{1,0:T(8,128)(2,1)S(1)}, u32[]{:S(2)}, u32[]{:S(2)}) collective-permute-start(bf16[768,512]{1,0:T(8,128)(2,1)S(1)} %bitcast.34), channel_id=1, source_target_pairs={{0,2},{1,7},{2,4},{3,1},{4,6},{5,3},{6,0},{7,5},{8,10},{9,15},{10,... | collective-permute-start | bytes 2359304 | tf_op jit(solution)/shard_map/ppermute | solution.py:45
  68.0 21.3 %collective-permute-start.4 = (bf16[768,512]{1,0:T(8,128)(2,1)S(1)}, bf16[768,512]{1,0:T(8,128)(2,1)S(1)}, u32[]{:S(2)}, u32[]{:S(2)}) collective-permute-start(bf16[768,512]{1,0:T(8,128)(2,1)S(1)} %bitcast.35), channel_id=1, source_target_pairs={{0,1},{1,0},{2,3},{3,2},{4,5},{5,4},{6,7},{7,6},{8,9},{9,8},{10,11... | collective-permute-start | bytes 2359304 | tf_op jit(solution)/shard_map/ppermute | solution.py:49
  68.0 21.4 %collective-permute-start.13 = (bf16[768,512]{1,0:T(8,128)(2,1)}, bf16[768,512]{1,0:T(8,128)(2,1)S(1)}, u32[]{:S(2)}, u32[]{:S(2)}) collective-permute-start(bf16[768,512]{1,0:T(8,128)(2,1)} %collective-permute-done.1.refs_6_), channel_id=1, source_target_pairs={{0,1},{1,0},{2,3},{3,2},{4,5},{5,4},{6,7},{7,6},{8,9},{9,8},{10,11... | collective-permute-start | bytes 2359304 | tf_op jit(solution)/shard_map/ppermute | solution.py:49
  68.5 21.4 %collective-permute-start.6 = (bf16[768,512]{1,0:T(8,128)(2,1)S(1)}, bf16[768,512]{1,0:T(8,128)(2,1)S(1)}, u32[]{:S(2)}, u32[]{:S(2)}) collective-permute-start(bf16[768,512]{1,0:T(8,128)(2,1)S(1)} %bitcast.36), channel_id=1, source_target_pairs={{0,6},{1,3},{2,0},{3,5},{4,2},{5,7},{6,4},{7,1},{8,14},{9,11},{10,... | collective-permute-start | bytes 2359304 | tf_op jit(solution)/shard_map/ppermute | solution.py:45
  89.2 13.4 %collective-permute-start.15 = (bf16[4,512,512]{2,1,0:T(8,128)(2,1)}, bf16[4,512,512]{2,1,0:T(8,128)(2,1)S(1)}, u32[]{:S(2)}, u32[]{:S(2)}) collective-permute-start(bf16[4,512,512]{2,1,0:T(8,128)(2,1)} %get-tuple-element.35), channel_id=1, source_target_pairs={{0,1},{1,0},{2,3},{3,2},{4,5},{5,4},{6,7},{7,6},{8,9},{9,8},{10,11... | collective-permute-start | bytes 6291464 | tf_op jit(solution)/shard_map/ppermute | solution.py:49
  89.2 13.3 %collective-permute-start.3 = (bf16[768,512]{1,0:T(8,128)(2,1)S(1)}, bf16[768,512]{1,0:T(8,128)(2,1)S(1)}, u32[]{:S(2)}, u32[]{:S(2)}) collective-permute-start(bf16[768,512]{1,0:T(8,128)(2,1)S(1)} %collective-permute-done.2.refs_2_), channel_id=1, source_target_pairs={{0,2},{1,7},{2,4},{3,1},{4,6},{5,3},{6,0},{7,5},{8,10},{9,15},{10,... | collective-permute-start | bytes 2359304 | tf_op jit(solution)/shard_map/ppermute | solution.py:45
  89.3 7.7 %collective-permute-start.5 = (bf16[768,512]{1,0:T(8,128)(2,1)S(1)}, bf16[768,512]{1,0:T(8,128)(2,1)S(1)}, u32[]{:S(2)}, u32[]{:S(2)}) collective-permute-start(bf16[768,512]{1,0:T(8,128)(2,1)S(1)} %collective-permute-done.2.refs_2_), channel_id=1, source_target_pairs={{0,1},{1,0},{2,3},{3,2},{4,5},{5,4},{6,7},{7,6},{8,9},{9,8},{10,11... | collective-permute-start | bytes 2359304 | tf_op jit(solution)/shard_map/ppermute | solution.py:49
  89.8 7.2 %collective-permute-start.7 = (bf16[768,512]{1,0:T(8,128)(2,1)S(1)}, bf16[768,512]{1,0:T(8,128)(2,1)S(1)}, u32[]{:S(2)}, u32[]{:S(2)}) collective-permute-start(bf16[768,512]{1,0:T(8,128)(2,1)S(1)} %collective-permute-done.6.refs_4_), channel_id=1, source_target_pairs={{0,1},{1,0},{2,3},{3,2},{4,5},{5,4},{6,7},{7,6},{8,9},{9,8},{10,11... | collective-permute-start | bytes 2359304 | tf_op jit(solution)/shard_map/ppermute | solution.py:49
  96.7 8.1 %collective-permute-start.16 = (f32[768,512]{1,0:T(8,128)S(1)}, f32[768,512]{1,0:T(8,128)S(1)}, u32[]{:S(2)}, u32[]{:S(2)}) collective-permute-start(f32[768,512]{1,0:T(8,128)S(1)} %get-tuple-element.36.refs_7_), channel_id=1, source_target_pairs={{0,1},{1,0},{2,3},{3,2},{4,5},{5,4},{6,7},{7,6},{8,9},{9,8},{10,11... | collective-permute-start | bytes 4718600 | tf_op jit(solution)/shard_map/ppermute | solution.py:49
  102.5 2.3 %collective-permute-start.14 = (bf16[768,512]{1,0:T(8,128)(2,1)S(1)}, bf16[768,512]{1,0:T(8,128)(2,1)S(1)}, u32[]{:S(2)}, u32[]{:S(2)}) collective-permute-start(bf16[768,512]{1,0:T(8,128)(2,1)S(1)} %collective-permute-done.3.refs_0_.refs_6_), channel_id=1, source_target_pairs={{0,1},{1,0},{2,3},{3,2},{4,5},{5,4},{6,7},{7,6},{8,9},{9,8},{10,11... | collective-permute-start | bytes 2359304 | tf_op jit(solution)/shard_map/ppermute | solution.py:49
  109.9 14.7 %collective-permute-start.18 = (bf16[768,512]{1,0:T(8,128)(2,1)}, bf16[768,512]{1,0:T(8,128)(2,1)S(1)}, u32[]{:S(2)}, u32[]{:S(2)}) collective-permute-start(bf16[768,512]{1,0:T(8,128)(2,1)} %get-tuple-element.41), channel_id=1, source_target_pairs={{0,2},{1,7},{2,4},{3,1},{4,6},{5,3},{6,0},{7,5},{8,10},{9,15},{10,... | collective-permute-start | bytes 2359304 | tf_op jit(solution)/shard_map/ppermute | solution.py:45
  116.7 14.6 %collective-permute-start.17 = (bf16[768,512]{1,0:T(8,128)(2,1)}, bf16[768,512]{1,0:T(8,128)(2,1)S(1)}, u32[]{:S(2)}, u32[]{:S(2)}) collective-permute-start(bf16[768,512]{1,0:T(8,128)(2,1)} %get-tuple-element.39), channel_id=1, source_target_pairs={{0,6},{1,3},{2,0},{3,5},{4,2},{5,7},{6,4},{7,1},{8,14},{9,11},{10,... | collective-permute-start | bytes 2359304 | tf_op jit(solution)/shard_map/ppermute | solution.py:45
  125.9 14.3 %collective-permute-start.19 = (bf16[768,512]{1,0:T(8,128)(2,1)S(1)}, bf16[768,512]{1,0:T(8,128)(2,1)S(1)}, u32[]{:S(2)}, u32[]{:S(2)}) collective-permute-start(bf16[768,512]{1,0:T(8,128)(2,1)S(1)} %add_convert_fusion.1), channel_id=1, source_target_pairs={{0,2},{1,7},{2,4},{3,1},{4,6},{5,3},{6,0},{7,5},{8,10},{9,15},{10,... | collective-permute-start | bytes 2359304 | tf_op jit(solution)/shard_map/ppermute | solution.py:45
  141.5 27.6 %all-to-all-start.2 = ((bf16[32,24,512]{2,1,0:T(8,128)(2,1)}), bf16[32,24,512]{2,1,0:T(8,128)(2,1)S(1)}, u32[]{:S(2)}, u32[]{:S(2)}) async-start(bf16[32,24,512]{2,1,0:T(8,128)(2,1)} %bitcast.46), calls=%async_computation.2 | async-start | bytes 1572864 | tf_op jit(solution)/shard_map/all_to_all | solution.py:461
  (17 other events, 193.7 us)

commit v4 on v3

--- a/solution.py
+++ b/solution.py
@@ -208,7 +208,7 @@
     )(*pin((*pieces, w_gu)))
 
 
-def add_hidden(first, pieces, own_w, other_w, total, rows_grad, w_dn, row_sem, own_sem, other_sem):
+def add_hidden(first, pieces, own_w, other_w, total, w_dn, own_sem, other_sem):
     count = len(pieces)
     hidden = own_w.shape[2]
     for j in range(count):
@@ -216,11 +216,21 @@
         other = w_dn.at[j, :, pl.ds(hidden, hidden)]
         pltpu.make_async_copy(own_w.at[first + j], own, own_sem.at[j]).start()
         pltpu.make_async_copy(other_w.at[(first + j) ^ 1], other, other_sem.at[j]).start()
-        pltpu.make_async_copy(pieces[j], rows_grad.at[j], row_sem.at[j]).start()
-
-    def step(j, carry):
+    for j in range(count):
         wait_for(own_w.at[0], own_sem.at[j])
         wait_for(other_w.at[0], other_sem.at[j])
+        total[...] += jnp.dot(pieces[j][...], w_dn[j], preferred_element_type=F32)
+
+
+def hidden_start_kernel(count, *refs):
+    pieces, weights, total, rows_grad, w_dn, row_sem, w_sem = refs[:count], *refs[count:]
+    for j in range(count):
+        pltpu.make_async_copy(weights.at[j], w_dn.at[j], w_sem.at[j]).start()
+        pltpu.make_async_copy(pieces[j], rows_grad.at[j], row_sem.at[j]).start()
+    total[...] = jnp.zeros_like(total)
+
+    def step(j, carry):
+        wait_for(w_dn.at[j], w_sem.at[j])
         wait_for(rows_grad.at[j], row_sem.at[j])
         total[...] += jnp.dot(rows_grad[j], w_dn[j], preferred_element_type=F32)
         return carry
@@ -228,32 +238,25 @@
     lax.fori_loop(0, count, step, 0)
 
 
-def hidden_start_kernel(count, *refs):
-    total = refs[count + 2]
-    total[...] = jnp.zeros_like(total)
-    add_hidden(0, refs[:count], *refs[count : count + 3], *refs[count + 3 :])
-
-
-def hidden_start_call(pieces, own_w, other_w):
+def hidden_start_call(pieces, w_dn):
     rows, width = pieces[0].shape
-    both, count = 2 * own_w.shape[2], len(pieces)
+    hidden, count = w_dn.shape[2], len(pieces)
     dma = pltpu.SemaphoreType.DMA((count,))
     return pl.pallas_call(
         functools.partial(hidden_start_kernel, count),
-        out_shape=jax.ShapeDtypeStruct((rows, both), F32),
-        in_specs=[ANY] * count + [HBM] * 2,
+        out_shape=jax.ShapeDtypeStruct((rows, hidden), F32),
+        in_specs=[ANY] * count + [HBM],
         out_specs=VMEM,
         scratch_shapes=[
             pltpu.VMEM((count, rows, width), BF16),
-            pltpu.VMEM((count, width, both), BF16),
-            dma,
+            pltpu.VMEM((count, width, hidden), BF16),
             dma,
             dma,
         ],
-        compiler_params=params(16),
-        cost_estimate=cost(rows, count * width, both, count * width * (rows + both) * 2),
+        compiler_params=params(15),
+        cost_estimate=cost(rows, count * width, hidden, count * width * (rows + hidden) * 2),
         name="hidden_start",
-    )(*pieces, *pin((own_w, other_w)))
+    )(*pieces, *pin((w_dn,)))
 
 
 def start_weights(own_w, other_w, block, buffer, own_sem, other_sem):
@@ -264,15 +267,15 @@
 
 def hidden_end_kernel(first, count, block, *refs):
     pieces = refs[:count]
-    own_dn, other_dn, own_w, other_w, before, own_factors, other_factors = refs[count : count + 7]
-    grads, out = refs[count + 7 : count + 9]
-    total, rows_grad, w_dn, w_gu, result = refs[count + 9 : count + 14]
-    row_sem, own_sem, other_sem, w_sem, out_sem = refs[count + 14 :]
+    own_dn, other_dn, own_w, other_w = refs[count : count + 4]
+    before, other_before, own_factors, other_factors = refs[count + 4 : count + 8]
+    grads, out = refs[count + 8 : count + 10]
+    total, w_dn, w_gu, result, own_sem, other_sem, w_sem, out_sem = refs[count + 10 :]
     start_weights(own_w, other_w, block, w_gu, w_sem.at[0], w_sem.at[1])
-    total[...] = before[...]
-    add_hidden(
-        first, pieces, own_dn, other_dn, total, rows_grad, w_dn, row_sem, own_sem, other_sem
-    )
+    half = before.shape[1]
+    total[:, :half] = before[...]
+    total[:, half:] = other_before[...]
+    add_hidden(first, pieces, own_dn, other_dn, total, w_dn, own_sem, other_sem)
     hidden = own_dn.shape[2]
     for core, factors in enumerate((own_factors, other_factors)):
         hidden_grad = total[:, core * hidden : (core + 1) * hidden]
@@ -287,7 +290,7 @@
     copy.wait()
 
 
-def hidden_end_call(pieces, own_dn, other_dn, own_w, other_w, before, factors, others, block):
+def hidden_end_call(pieces, own_dn, other_dn, own_w, other_w, befores, factors, others, block):
     rows, width = pieces[0].shape
     both, count = 2 * own_dn.shape[2], len(pieces)
     dma = pltpu.SemaphoreType.DMA
@@ -297,24 +300,22 @@
             jax.ShapeDtypeStruct((rows, 2 * both), BF16),
             pltpu.HBM((rows, width), BF16),
         ),
-        in_specs=[ANY] * count + [HBM] * 4 + [VMEM] * 3,
+        in_specs=[VMEM] * count + [HBM] * 4 + [VMEM] * 4,
         out_specs=(VMEM, HBM),
         scratch_shapes=[
             pltpu.VMEM((rows, both), F32),
-            pltpu.VMEM((count, rows, width), BF16),
             pltpu.VMEM((count, width, both), BF16),
             pltpu.VMEM((2 * both, width), BF16),
             pltpu.VMEM((rows, width), BF16),
             dma((count,)),
             dma((count,)),
-            dma((count,)),
             dma((2,)),
             dma,
         ],
         compiler_params=params(20),
         cost_estimate=cost(rows, (count + 2) * width, both, count * width * (rows + both) * 2),
         name="hidden_end",
-    )(*pieces, *pin((own_dn, other_dn, own_w, other_w)), before, factors, others)
+    )(*pieces, *pin((own_dn, other_dn, own_w, other_w)), *befores, factors, others)
 
 
 def partial_kernel(blocks, *refs):
@@ -474,12 +475,13 @@
     back, on, far = ring_gather(after(arrived_grad, far))
     others = core_swap(factors)
     near = (arrived_grad, core_swap(arrived_grad), back, core_swap(back), on, core_swap(on))
-    before = hidden_start_call(near, w_dn, other_dn)
+    before = hidden_start_call(near, w_dn)
+    befores = (before, core_swap(before))
     far = after(far, before, active)
     late = (far, core_swap(far))
     pieces_grad = (*near, *late)
     grads, far = hidden_end_call(
-        late, w_dn, other_dn, own_w, other_w, before, factors, others, 3
+        late, w_dn, other_dn, own_w, other_w, befores, factors, others, 3
     )
     far = chip_step(far, 1)
     back, own, on = partial_call(grads, own_w, other_w, (1, 0, 2))

time: 171 us -> 170 us (level)
  waiting for transfers between devices: 80.1 us -> 84.5 us
  starting transfers between devices: 38.7 us -> 35.9 us
  Pallas kernels: 42.5 us -> 39.9 us
    ppermute x9, waiting for transfers between devices: 51.4 us -> 56.1 us  [chip_step(): return lax.ppermute(value, 'local', pairs)]
    ppermute x9, starting transfers between devices: 13.8 us -> 12.1 us  [chip_step(): return lax.ppermute(value, 'local', pairs)]
  transfers between devices with their start and end apart: 23 -> 24, of which waited for: 12 -> 13; matrix products, arithmetic and copies ran while one was open for 2% -> 2% of each run, Pallas kernels for 22% -> 21%
where the time goes in v4:
time: 170 us; the launch traced here: 169 us
  waiting for transfers between devices  84.5 us (50%)
  Pallas kernels  39.9 us (23%)
  starting transfers between devices  35.9 us (21%)
  matrix products  3.65 us (2%)
  other arithmetic  3.48 us (2%)
    ppermute x9, waiting for transfers between devices, chip_step(): return lax.ppermute(value, 'local', pairs)  56.1 us
    all_to_all x3, waiting for transfers between devices, exchange(): lax.all_to_all(value, 'node', split_axis=0, concat_axis=0, tiled=True)  25.5 us
    all_to_all x3, starting transfers between devices, exchange(): lax.all_to_all(value, 'node', split_axis=0, concat_axis=0, tiled=True)  21.1 us
    ppermute x9, starting transfers between devices, chip_step(): return lax.ppermute(value, 'local', pairs)  12.1 us
    pallas_call x1, Pallas kernels, prepare_call(): pl.pallas_call(prepare_kernel, out_shape=(pltpu.HBM((8, width, 2 * hidden...  7.75 us
    pallas_call x1, Pallas kernels, gate_up_total_call(): pl.pallas_call(gate_up_total_kernel, out_shape=(total, total), in_specs=[...  7.67 us
    pallas_call x1, Pallas kernels, gate_up_call(): pl.pallas_call(gate_up_kernel, out_shape=(jax.ShapeDtypeStruct((rows, hid...  6.32 us
    pallas_call x1, Pallas kernels, down_total_call(): pl.pallas_call(down_total_kernel, out_shape=jax.ShapeDtypeStruct((hidden,...  5.49 us
  transfers between devices with their start and end apart: 24, of which 13 were waited for; matrix products, arithmetic and copies ran while one was open for 2% of the time, Pallas kernels for 21%

profile of v4, /device:TPU:32, one launch (start us, length us, event | category | flops | bytes accessed | tf_op | source)
XLA Modules:
  0.0 169.4 jit_solution(5904837279282195456)
XLA Ops:
  3.1 11.2 %all-to-all-start = ((bf16[32,24,512]{2,1,0:T(8,128)(2,1)}), bf16[32,24,512]{2,1,0:T(8,128)(2,1)S(1)}, u32[]{:S(2)}, u32[]{:S(2)}) async-start(bf16[32,24,512]{2,1,0:T(8,128)(2,1)} %bitcast.2), calls=%async_computation | async-start | bytes 1572864 | tf_op jit(solution)/shard_map/all_to_all | solution.py:462
  15.8 7.7 %prepare.1 = (bf16[8,512,512]{2,1,0:T(8,128)(2,1)}, bf16[4,512,512]{2,1,0:T(8,128)(2,1)}, bf16[4,512,512]{2,1,0:T(8,128)(2,1)}, bf16[8,512,256]{2,1,0:T(8,128)(2,1)}) custom-call(s32[8]{0:T(128)S(1)} %stack.35.order, bf16[4096,256]{1,0:T(8,128)(2,1)} %bitcast.40, bf16[4096,256]{1,0:T(8,128)(2,1)} %bitcast.41, bf16[4096,256]{1,0:T(8,128)(2,1)} %bitcast.42, ...), custom_call_target="tpu_custom_call" | custom-call | flops 1610612736 | bytes 16777216 | tf_op jit(solution)/shard_map/prepare/pallas_call | solution.py:134
  23.6 13.9 %all-to-all-done = bf16[32,24,512]{2,1,0:T(8,128)(2,1)S(1)} async-done(((bf16[32,24,512]{2,1,0:T(8,128)(2,1)}), bf16[32,24,512]{2,1,0:T(8,128)(2,1)S(1)}, u32[]{:S(2)}, u32[]{:S(2)}) %all-to-all-start) | async-done | bytes 786464 | tf_op jit(solution)/shard_map/all_to_all | solution.py:462
  39.0 4.9 %all-to-all-start.1 = ((bf16[32,24,512]{2,1,0:T(8,128)(2,1)}), bf16[32,24,512]{2,1,0:T(8,128)(2,1)S(1)}, u32[]{:S(2)}, u32[]{:S(2)}) async-start(bf16[32,24,512]{2,1,0:T(8,128)(2,1)} %bitcast.15), calls=%async_computation.1 | async-start | bytes 1572864 | tf_op jit(solution)/shard_map/all_to_all | solution.py:462
  45.7 7.7 %collective-permute-done.refs_2_ = bf16[768,512]{1,0:T(8,128)(2,1)S(1)} collective-permute-done((bf16[768,512]{1,0:T(8,128)(2,1)S(1)}, bf16[768,512]{1,0:T(8,128)(2,1)S(1)}, u32[]{:S(2)}, u32[]{:S(2)}) %collective-permute-start) | collective-permute-done | bytes 786464 | tf_op jit(solution)/shard_map/ppermute | solution.py:45
  53.4 2.0 %collective-permute-start.1 = (bf16[768,512]{1,0:T(8,128)(2,1)S(1)}, bf16[768,512]{1,0:T(8,128)(2,1)}, u32[]{:S(2)}, u32[]{:S(2)}) collective-permute-start(bf16[768,512]{1,0:T(8,128)(2,1)S(1)} %collective-permute-done.refs_2_), channel_id=1, source_target_pairs={{0,2},{1,7},{2,4},{3,1},{4,6},{5,3},{6,0},{7,5},{8,10},{9,15},{10,... | collective-permute-start | bytes 2359304 | tf_op jit(solution)/shard_map/ppermute | solution.py:45
  55.5 7.2 %collective-permute-done.10.refs_4_ = bf16[768,512]{1,0:T(8,128)(2,1)S(1)} collective-permute-done((bf16[768,512]{1,0:T(8,128)(2,1)S(1)}, bf16[768,512]{1,0:T(8,128)(2,1)S(1)}, u32[]{:S(2)}, u32[]{:S(2)}) %collective-permute-start.10) | collective-permute-done | bytes 786464 | tf_op jit(solution)/shard_map/ppermute | solution.py:45
  62.7 4.6 %all-to-all-done.1 = bf16[32,24,512]{2,1,0:T(8,128)(2,1)S(1)} async-done(((bf16[32,24,512]{2,1,0:T(8,128)(2,1)}), bf16[32,24,512]{2,1,0:T(8,128)(2,1)S(1)}, u32[]{:S(2)}, u32[]{:S(2)}) %all-to-all-start.1) | async-done | bytes 786464 | tf_op jit(solution)/shard_map/all_to_all | solution.py:462
  68.5 2.9 %collective-permute-start.6 = (bf16[768,512]{1,0:T(8,128)(2,1)S(1)}, bf16[768,512]{1,0:T(8,128)(2,1)S(1)}, u32[]{:S(2)}, u32[]{:S(2)}) collective-permute-start(bf16[768,512]{1,0:T(8,128)(2,1)S(1)} %bitcast.36), channel_id=1, source_target_pairs={{0,6},{1,3},{2,0},{3,5},{4,2},{5,7},{6,4},{7,1},{8,14},{9,11},{10,... | collective-permute-start | bytes 2359304 | tf_op jit(solution)/shard_map/ppermute | solution.py:45
  71.5 17.4 %collective-permute-done.2.refs_2_ = bf16[768,512]{1,0:T(8,128)(2,1)S(1)} collective-permute-done((bf16[768,512]{1,0:T(8,128)(2,1)S(1)}, bf16[768,512]{1,0:T(8,128)(2,1)S(1)}, u32[]{:S(2)}, u32[]{:S(2)}) %collective-permute-start.2) | collective-permute-done | bytes 786464 | tf_op jit(solution)/shard_map/ppermute | solution.py:45
  90.6 6.3 %gate_up.1 = (bf16[768,256]{1,0:T(8,128)(2,1)S(1)}, f32[768,512]{1,0:T(8,128)S(1)}) custom-call(bf16[768,512]{1,0:T(8,128)(2,1)} %bitcast.51, bf16[768,512]{1,0:T(8,128)(2,1)} %collective-permute-done.8.refs_1_, bf16[768,512]{1,0:T(8,128)(2,1)} %copy-done.16, bf16[768,512]{1,0:T(8,128)(2,1)} %copy-done.18, bf16[768,512]{1,0:T(8,128)(2,1)} %copy-done.17, ...), custom_call_target="tpu_custom_call" | custom-call | flops 3221225472 | bytes 10485760 | tf_op jit(solution)/shard_map/gate_up/pallas_call | solution.py:190
  97.3 3.5 %hidden_start.1.refs_6_ = f32[768,256]{1,0:T(8,128)S(1)} custom-call(bf16[768,512]{1,0:T(8,128)(2,1)S(1)} %bitcast.37, bf16[768,512]{1,0:T(8,128)(2,1)S(1)} %collective-permute-done.4.refs_1_, bf16[768,512]{1,0:T(8,128)(2,1)S(1)} %collective-permute-done.2.refs_2_, bf16[768,512]{1,0:T(8,128)(2,1)S(1)} %collective-permute-done.5.refs_3_, ...), custom_call_target="tpu_custom_call" | custom-call | flops 1207959552 | bytes 6291456 | tf_op jit(solution)/shard_map/hidden_start/pallas_call | solution.py:245
  100.8 1.9 %collective-permute-done.3.refs_0_.refs_6_ = bf16[768,512]{1,0:T(8,128)(2,1)S(1)} collective-permute-done((bf16[768,512]{1,0:T(8,128)(2,1)S(1)}, bf16[768,512]{1,0:T(8,128)(2,1)S(1)}, u32[]{:S(2)}, u32[]{:S(2)}) %collective-permute-start.3) | collective-permute-done | bytes 786464 | tf_op jit(solution)/shard_map/ppermute | solution.py:45
  103.3 1.8 %collective-permute-done.13.refs_1_.refs_7_ = bf16[768,512]{1,0:T(8,128)(2,1)S(1)} collective-permute-done((bf16[768,512]{1,0:T(8,128)(2,1)S(1)}, bf16[768,512]{1,0:T(8,128)(2,1)S(1)}, u32[]{:S(2)}, u32[]{:S(2)}) %collective-permute-start.13) | collective-permute-done | bytes 786464 | tf_op jit(solution)/shard_map/ppermute | solution.py:49
  106.2 4.1 %hidden_end.1 = (bf16[768,1024]{1,0:T(8,128)(2,1)S(1)}, bf16[768,512]{1,0:T(8,128)(2,1)}) custom-call(bf16[768,512]{1,0:T(8,128)(2,1)S(1)} %collective-permute-done.3.refs_0_.refs_6_, bf16[768,512]{1,0:T(8,128)(2,1)S(1)} %collective-permute-done.13.refs_1_.refs_7_, bf16[8,512,256]{2,1,0:T(8,128)(2,1)} %get-tuple-element.32.refs_6_.refs_2_, ...), custom_call_target="tpu_custom_call" | custom-call | flops 1610612736 | bytes 2621440 | tf_op jit(solution)/shard_map/hidden_end/pallas_call | solution.py:297
  110.4 5.2 %partial.1 = (bf16[768,512]{1,0:T(8,128)(2,1)}, bf16[768,512]{1,0:T(8,128)(2,1)}, bf16[768,512]{1,0:T(8,128)(2,1)}) custom-call(bf16[768,1024]{1,0:T(8,128)(2,1)S(1)} %get-tuple-element.37.refs_0_.refs_8_, bf16[4,512,512]{2,1,0:T(8,128)(2,1)} %get-tuple-element.33.refs_4_.refs_1_, bf16[4,512,512]{2,1,0:T(8,128)(2,1)} %copy-done.11), custom_call_target="tpu_custom_call" | custom-call | flops 2415919104 | bytes 11010048 | tf_op jit(solution)/shard_map/partial/pallas_call | solution.py:340
  115.5 3.3 %collective-permute-start.18 = (bf16[768,512]{1,0:T(8,128)(2,1)}, bf16[768,512]{1,0:T(8,128)(2,1)S(1)}, u32[]{:S(2)}, u32[]{:S(2)}) collective-permute-start(bf16[768,512]{1,0:T(8,128)(2,1)} %get-tuple-element.39), channel_id=1, source_target_pairs={{0,6},{1,3},{2,0},{3,5},{4,2},{5,7},{6,4},{7,1},{8,14},{9,11},{10,... | collective-permute-start | bytes 2359304 | tf_op jit(solution)/shard_map/ppermute | solution.py:45
  118.8 8.4 %collective-permute-done.19 = bf16[768,512]{1,0:T(8,128)(2,1)S(1)} collective-permute-done((bf16[768,512]{1,0:T(8,128)(2,1)}, bf16[768,512]{1,0:T(8,128)(2,1)S(1)}, u32[]{:S(2)}, u32[]{:S(2)}) %collective-permute-start.19) | collective-permute-done | bytes 786464 | tf_op jit(solution)/shard_map/ppermute | solution.py:45
  128.6 3.5 %collective-permute-done.18 = bf16[768,512]{1,0:T(8,128)(2,1)S(1)} collective-permute-done((bf16[768,512]{1,0:T(8,128)(2,1)}, bf16[768,512]{1,0:T(8,128)(2,1)S(1)}, u32[]{:S(2)}, u32[]{:S(2)}) %collective-permute-start.18) | collective-permute-done | bytes 786464 | tf_op jit(solution)/shard_map/ppermute | solution.py:45
  132.1 9.7 %collective-permute-done.20 = bf16[768,512]{1,0:T(8,128)(2,1)S(1)} collective-permute-done((bf16[768,512]{1,0:T(8,128)(2,1)S(1)}, bf16[768,512]{1,0:T(8,128)(2,1)S(1)}, u32[]{:S(2)}, u32[]{:S(2)}) %collective-permute-start.20) | collective-permute-done | bytes 786464 | tf_op jit(solution)/shard_map/ppermute | solution.py:45
  143.0 5.0 %all-to-all-start.2 = ((bf16[32,24,512]{2,1,0:T(8,128)(2,1)}), bf16[32,24,512]{2,1,0:T(8,128)(2,1)S(1)}, u32[]{:S(2)}, u32[]{:S(2)}) async-start(bf16[32,24,512]{2,1,0:T(8,128)(2,1)} %bitcast.46), calls=%async_computation.2 | async-start | bytes 1572864 | tf_op jit(solution)/shard_map/all_to_all | solution.py:462
  148.3 5.5 %down_total.1 = bf16[256,4096]{1,0:T(8,128)(2,1)} custom-call(s32[8]{0:T(128)S(1)} %stack.35.order, bf16[768,512]{1,0:T(8,128)(2,1)} %bitcast.38, bf16[768,512]{1,0:T(8,128)(2,1)} %copy-done.5, bf16[768,512]{1,0:T(8,128)(2,1)} %copy-done.4, bf16[768,512]{1,0:T(8,128)(2,1)} %copy-done.7, bf16[768,512]{1,0:T(8,128)(2,1)} %copy-done.6, ...), custom_call_target="tpu_custom_call" | custom-call | flops 1610612736 | bytes 8388608 | tf_op jit(solution)/shard_map/down_total/pallas_call | solution.py:382
  153.8 7.7 %gate_up_total.1 = (bf16[4096,256]{1,0:T(8,128)(2,1)}, bf16[4096,256]{1,0:T(8,128)(2,1)}) custom-call(s32[8]{0:T(128)S(1)} %stack.35.order, bf16[768,512]{1,0:T(8,128)(2,1)} %bitcast.52, bf16[768,512]{1,0:T(8,128)(2,1)} %collective-permute-done.8.refs_1_, bf16[768,512]{1,0:T(8,128)(2,1)} %copy-done.16, bf16[768,512]{1,0:T(8,128)(2,1)} %copy-done.18, ...), custom_call_target="tpu_custom_call" | custom-call | flops 3221225472 | bytes 10485760 | tf_op jit(solution)/shard_map/gate_up_total/pallas_call | solution.py:432
  161.4 7.0 %all-to-all-done.2 = bf16[32,24,512]{2,1,0:T(8,128)(2,1)S(1)} async-done(((bf16[32,24,512]{2,1,0:T(8,128)(2,1)}), bf16[32,24,512]{2,1,0:T(8,128)(2,1)S(1)}, u32[]{:S(2)}, u32[]{:S(2)}) %all-to-all-start.2) | async-done | bytes 786464 | tf_op jit(solution)/shard_map/all_to_all | solution.py:462
  (83 shorter events, 15.8 us)
Async XLA Ops:
  3.1 34.4 %all-to-all-start = ((bf16[32,24,512]{2,1,0:T(8,128)(2,1)}), bf16[32,24,512]{2,1,0:T(8,128)(2,1)S(1)}, u32[]{:S(2)}, u32[]{:S(2)}) async-start(bf16[32,24,512]{2,1,0:T(8,128)(2,1)} %bitcast.2), calls=%async_computation | async-start | bytes 1572864 | tf_op jit(solution)/shard_map/all_to_all | solution.py:462
  37.5 16.0 %collective-permute-start = (bf16[768,512]{1,0:T(8,128)(2,1)S(1)}, bf16[768,512]{1,0:T(8,128)(2,1)S(1)}, u32[]{:S(2)}, u32[]{:S(2)}) collective-permute-start(bf16[768,512]{1,0:T(8,128)(2,1)S(1)} %bitcast.48), channel_id=1, source_target_pairs={{0,2},{1,7},{2,4},{3,1},{4,6},{5,3},{6,0},{7,5},{8,10},{9,15},{10,... | collective-permute-start | bytes 2359304 | tf_op jit(solution)/shard_map/ppermute | solution.py:45
  39.0 28.3 %all-to-all-start.1 = ((bf16[32,24,512]{2,1,0:T(8,128)(2,1)}), bf16[32,24,512]{2,1,0:T(8,128)(2,1)S(1)}, u32[]{:S(2)}, u32[]{:S(2)}) async-start(bf16[32,24,512]{2,1,0:T(8,128)(2,1)} %bitcast.15), calls=%async_computation.1 | async-start | bytes 1572864 | tf_op jit(solution)/shard_map/all_to_all | solution.py:462
  44.0 18.7 %collective-permute-start.10 = (bf16[768,512]{1,0:T(8,128)(2,1)S(1)}, bf16[768,512]{1,0:T(8,128)(2,1)S(1)}, u32[]{:S(2)}, u32[]{:S(2)}) collective-permute-start(bf16[768,512]{1,0:T(8,128)(2,1)S(1)} %bitcast.49), channel_id=1, source_target_pairs={{0,6},{1,3},{2,0},{3,5},{4,2},{5,7},{6,4},{7,1},{8,14},{9,11},{10,... | collective-permute-start | bytes 2359304 | tf_op jit(solution)/shard_map/ppermute | solution.py:45
  53.4 14.2 %collective-permute-start.1 = (bf16[768,512]{1,0:T(8,128)(2,1)S(1)}, bf16[768,512]{1,0:T(8,128)(2,1)}, u32[]{:S(2)}, u32[]{:S(2)}) collective-permute-start(bf16[768,512]{1,0:T(8,128)(2,1)S(1)} %collective-permute-done.refs_2_), channel_id=1, source_target_pairs={{0,2},{1,7},{2,4},{3,1},{4,6},{5,3},{6,0},{7,5},{8,10},{9,15},{10,... | collective-permute-start | bytes 2359304 | tf_op jit(solution)/shard_map/ppermute | solution.py:45
  55.5 13.0 %collective-permute-start.8 = (bf16[768,512]{1,0:T(8,128)(2,1)S(1)}, bf16[768,512]{1,0:T(8,128)(2,1)}, u32[]{:S(2)}, u32[]{:S(2)}) collective-permute-start(bf16[768,512]{1,0:T(8,128)(2,1)S(1)} %bitcast.50), channel_id=1, source_target_pairs={{0,1},{1,0},{2,3},{3,2},{4,5},{5,4},{6,7},{7,6},{8,9},{9,8},{10,11... | collective-permute-start | bytes 2359304 | tf_op jit(solution)/shard_map/ppermute | solution.py:49
  62.7 5.8 %collective-permute-start.11 = (bf16[768,512]{1,0:T(8,128)(2,1)S(1)}, bf16[768,512]{1,0:T(8,128)(2,1)}, u32[]{:S(2)}, u32[]{:S(2)}) collective-permute-start(bf16[768,512]{1,0:T(8,128)(2,1)S(1)} %collective-permute-done.10.refs_4_), channel_id=1, source_target_pairs={{0,1},{1,0},{2,3},{3,2},{4,5},{5,4},{6,7},{7,6},{8,9},{9,8},{10,11... | collective-permute-start | bytes 2359304 | tf_op jit(solution)/shard_map/ppermute | solution.py:49
  67.6 21.3 %collective-permute-start.2 = (bf16[768,512]{1,0:T(8,128)(2,1)S(1)}, bf16[768,512]{1,0:T(8,128)(2,1)S(1)}, u32[]{:S(2)}, u32[]{:S(2)}) collective-permute-start(bf16[768,512]{1,0:T(8,128)(2,1)S(1)} %bitcast.34), channel_id=1, source_target_pairs={{0,2},{1,7},{2,4},{3,1},{4,6},{5,3},{6,0},{7,5},{8,10},{9,15},{10,... | collective-permute-start | bytes 2359304 | tf_op jit(solution)/shard_map/ppermute | solution.py:45
  68.0 20.9 %collective-permute-start.9 = (bf16[768,512]{1,0:T(8,128)(2,1)S(1)}, bf16[768,512]{1,0:T(8,128)(2,1)S(1)}, u32[]{:S(2)}, u32[]{:S(2)}) collective-permute-start(bf16[768,512]{1,0:T(8,128)(2,1)S(1)} %collective-permute-done.refs_2_), channel_id=1, source_target_pairs={{0,1},{1,0},{2,3},{3,2},{4,5},{5,4},{6,7},{7,6},{8,9},{9,8},{10,11... | collective-permute-start | bytes 2359304 | tf_op jit(solution)/shard_map/ppermute | solution.py:49
  68.0 21.4 %collective-permute-start.4 = (bf16[768,512]{1,0:T(8,128)(2,1)S(1)}, bf16[768,512]{1,0:T(8,128)(2,1)S(1)}, u32[]{:S(2)}, u32[]{:S(2)}) collective-permute-start(bf16[768,512]{1,0:T(8,128)(2,1)S(1)} %bitcast.35), channel_id=1, source_target_pairs={{0,1},{1,0},{2,3},{3,2},{4,5},{5,4},{6,7},{7,6},{8,9},{9,8},{10,11... | collective-permute-start | bytes 2359304 | tf_op jit(solution)/shard_map/ppermute | solution.py:49
  68.5 21.0 %collective-permute-start.12 = (bf16[768,512]{1,0:T(8,128)(2,1)}, bf16[768,512]{1,0:T(8,128)(2,1)S(1)}, u32[]{:S(2)}, u32[]{:S(2)}) collective-permute-start(bf16[768,512]{1,0:T(8,128)(2,1)} %collective-permute-done.1.refs_6_), channel_id=1, source_target_pairs={{0,1},{1,0},{2,3},{3,2},{4,5},{5,4},{6,7},{7,6},{8,9},{9,8},{10,11... | collective-permute-start | bytes 2359304 | tf_op jit(solution)/shard_map/ppermute | solution.py:49
  68.5 21.0 %collective-permute-start.6 = (bf16[768,512]{1,0:T(8,128)(2,1)S(1)}, bf16[768,512]{1,0:T(8,128)(2,1)S(1)}, u32[]{:S(2)}, u32[]{:S(2)}) collective-permute-start(bf16[768,512]{1,0:T(8,128)(2,1)S(1)} %bitcast.36), channel_id=1, source_target_pairs={{0,6},{1,3},{2,0},{3,5},{4,2},{5,7},{6,4},{7,1},{8,14},{9,11},{10,... | collective-permute-start | bytes 2359304 | tf_op jit(solution)/shard_map/ppermute | solution.py:45
  88.9 8.0 %collective-permute-start.5 = (bf16[768,512]{1,0:T(8,128)(2,1)S(1)}, bf16[768,512]{1,0:T(8,128)(2,1)S(1)}, u32[]{:S(2)}, u32[]{:S(2)}) collective-permute-start(bf16[768,512]{1,0:T(8,128)(2,1)S(1)} %collective-permute-done.2.refs_2_), channel_id=1, source_target_pairs={{0,1},{1,0},{2,3},{3,2},{4,5},{5,4},{6,7},{7,6},{8,9},{9,8},{10,11... | collective-permute-start | bytes 2359304 | tf_op jit(solution)/shard_map/ppermute | solution.py:49
  88.9 14.3 %collective-permute-start.14 = (bf16[8,512,256]{2,1,0:T(8,128)(2,1)}, bf16[8,512,256]{2,1,0:T(8,128)(2,1)S(1)}, u32[]{:S(2)}, u32[]{:S(2)}) collective-permute-start(bf16[8,512,256]{2,1,0:T(8,128)(2,1)} %get-tuple-element.32.refs_6_.refs_2_), channel_id=1, source_target_pairs={{0,1},{1,0},{2,3},{3,2},{4,5},{5,4},{6,7},{7,6},{8,9},{9,8},{10,11... | collective-permute-start | bytes 6291464 | tf_op jit(solution)/shard_map/ppermute | solution.py:49
  89.4 13.8 %collective-permute-start.15 = (bf16[4,512,512]{2,1,0:T(8,128)(2,1)}, bf16[4,512,512]{2,1,0:T(8,128)(2,1)S(1)}, u32[]{:S(2)}, u32[]{:S(2)}) collective-permute-start(bf16[4,512,512]{2,1,0:T(8,128)(2,1)} %get-tuple-element.35), channel_id=1, source_target_pairs={{0,1},{1,0},{2,3},{3,2},{4,5},{5,4},{6,7},{7,6},{8,9},{9,8},{10,11... | collective-permute-start | bytes 6291464 | tf_op jit(solution)/shard_map/ppermute | solution.py:49
  89.5 13.2 %collective-permute-start.3 = (bf16[768,512]{1,0:T(8,128)(2,1)S(1)}, bf16[768,512]{1,0:T(8,128)(2,1)S(1)}, u32[]{:S(2)}, u32[]{:S(2)}) collective-permute-start(bf16[768,512]{1,0:T(8,128)(2,1)S(1)} %collective-permute-done.2.refs_2_), channel_id=1, source_target_pairs={{0,2},{1,7},{2,4},{3,1},{4,6},{5,3},{6,0},{7,5},{8,10},{9,15},{10,... | collective-permute-start | bytes 2359304 | tf_op jit(solution)/shard_map/ppermute | solution.py:45
  89.6 7.7 %collective-permute-start.7 = (bf16[768,512]{1,0:T(8,128)(2,1)S(1)}, bf16[768,512]{1,0:T(8,128)(2,1)S(1)}, u32[]{:S(2)}, u32[]{:S(2)}) collective-permute-start(bf16[768,512]{1,0:T(8,128)(2,1)S(1)} %collective-permute-done.6.refs_4_), channel_id=1, source_target_pairs={{0,1},{1,0},{2,3},{3,2},{4,5},{5,4},{6,7},{7,6},{8,9},{9,8},{10,11... | collective-permute-start | bytes 2359304 | tf_op jit(solution)/shard_map/ppermute | solution.py:49
  96.9 8.1 %collective-permute-start.17 = (f32[768,512]{1,0:T(8,128)S(1)}, f32[768,512]{1,0:T(8,128)S(1)}, u32[]{:S(2)}, u32[]{:S(2)}) collective-permute-start(f32[768,512]{1,0:T(8,128)S(1)} %get-tuple-element.36.refs_8_), channel_id=1, source_target_pairs={{0,1},{1,0},{2,3},{3,2},{4,5},{5,4},{6,7},{7,6},{8,9},{9,8},{10,11... | collective-permute-start | bytes 4718600 | tf_op jit(solution)/shard_map/ppermute | solution.py:49
  102.7 2.3 %collective-permute-start.13 = (bf16[768,512]{1,0:T(8,128)(2,1)S(1)}, bf16[768,512]{1,0:T(8,128)(2,1)S(1)}, u32[]{:S(2)}, u32[]{:S(2)}) collective-permute-start(bf16[768,512]{1,0:T(8,128)(2,1)S(1)} %collective-permute-done.3.refs_0_.refs_6_), channel_id=1, source_target_pairs={{0,1},{1,0},{2,3},{3,2},{4,5},{5,4},{6,7},{7,6},{8,9},{9,8},{10,11... | collective-permute-start | bytes 2359304 | tf_op jit(solution)/shard_map/ppermute | solution.py:49
  102.7 3.4 %collective-permute-start.16 = (f32[768,256]{1,0:T(8,128)S(1)}, f32[768,256]{1,0:T(8,128)S(1)}, u32[]{:S(2)}, u32[]{:S(2)}) collective-permute-start(f32[768,256]{1,0:T(8,128)S(1)} %hidden_start.1.refs_6_), channel_id=1, source_target_pairs={{0,1},{1,0},{2,3},{3,2},{4,5},{5,4},{6,7},{7,6},{8,9},{9,8},{10,11... | collective-permute-start | bytes 2359304 | tf_op jit(solution)/shard_map/ppermute | solution.py:49
  110.3 16.9 %collective-permute-start.19 = (bf16[768,512]{1,0:T(8,128)(2,1)}, bf16[768,512]{1,0:T(8,128)(2,1)S(1)}, u32[]{:S(2)}, u32[]{:S(2)}) collective-permute-start(bf16[768,512]{1,0:T(8,128)(2,1)} %get-tuple-element.41), channel_id=1, source_target_pairs={{0,2},{1,7},{2,4},{3,1},{4,6},{5,3},{6,0},{7,5},{8,10},{9,15},{10,... | collective-permute-start | bytes 2359304 | tf_op jit(solution)/shard_map/ppermute | solution.py:45
  115.5 16.6 %collective-permute-start.18 = (bf16[768,512]{1,0:T(8,128)(2,1)}, bf16[768,512]{1,0:T(8,128)(2,1)S(1)}, u32[]{:S(2)}, u32[]{:S(2)}) collective-permute-start(bf16[768,512]{1,0:T(8,128)(2,1)} %get-tuple-element.39), channel_id=1, source_target_pairs={{0,6},{1,3},{2,0},{3,5},{4,2},{5,7},{6,4},{7,1},{8,14},{9,11},{10,... | collective-permute-start | bytes 2359304 | tf_op jit(solution)/shard_map/ppermute | solution.py:45
  128.5 13.3 %collective-permute-start.20 = (bf16[768,512]{1,0:T(8,128)(2,1)S(1)}, bf16[768,512]{1,0:T(8,128)(2,1)S(1)}, u32[]{:S(2)}, u32[]{:S(2)}) collective-permute-start(bf16[768,512]{1,0:T(8,128)(2,1)S(1)} %add_convert_fusion.1), channel_id=1, source_target_pairs={{0,2},{1,7},{2,4},{3,1},{4,6},{5,3},{6,0},{7,5},{8,10},{9,15},{10,... | collective-permute-start | bytes 2359304 | tf_op jit(solution)/shard_map/ppermute | solution.py:45
  143.0 25.4 %all-to-all-start.2 = ((bf16[32,24,512]{2,1,0:T(8,128)(2,1)}), bf16[32,24,512]{2,1,0:T(8,128)(2,1)S(1)}, u32[]{:S(2)}, u32[]{:S(2)}) async-start(bf16[32,24,512]{2,1,0:T(8,128)(2,1)} %bitcast.46), calls=%async_computation.2 | async-start | bytes 1572864 | tf_op jit(solution)/shard_map/all_to_all | solution.py:462
  (20 other events, 249.8 us)

commit v5 on v3

--- a/solution.py
+++ b/solution.py
@@ -208,7 +208,21 @@
     )(*pin((*pieces, w_gu)))
 
 
-def add_hidden(first, pieces, own_w, other_w, total, rows_grad, w_dn, row_sem, own_sem, other_sem):
+def add_hidden(first, pieces, own_w, other_w, total, w_dn, own_sem, other_sem):
+    count = len(pieces)
+    hidden = own_w.shape[2]
+    for j in range(count):
+        own = w_dn.at[j, :, pl.ds(0, hidden)]
+        other = w_dn.at[j, :, pl.ds(hidden, hidden)]
+        pltpu.make_async_copy(own_w.at[first + j], own, own_sem.at[j]).start()
+        pltpu.make_async_copy(other_w.at[(first + j) ^ 1], other, other_sem.at[j]).start()
+    for j in range(count):
+        wait_for(own_w.at[0], own_sem.at[j])
+        wait_for(other_w.at[0], other_sem.at[j])
+        total[...] += jnp.dot(pieces[j][...], w_dn[j], preferred_element_type=F32)
+
+
+def add_hidden_copied(first, pieces, own_w, other_w, total, rows_grad, w_dn, row_sem, own_sem, other_sem):
     count = len(pieces)
     hidden = own_w.shape[2]
     for j in range(count):
@@ -231,7 +245,7 @@
 def hidden_start_kernel(count, *refs):
     total = refs[count + 2]
     total[...] = jnp.zeros_like(total)
-    add_hidden(0, refs[:count], *refs[count : count + 3], *refs[count + 3 :])
+    add_hidden_copied(0, refs[:count], *refs[count : count + 3], *refs[count + 3 :])
 
 
 def hidden_start_call(pieces, own_w, other_w):
@@ -266,13 +280,10 @@
     pieces = refs[:count]
     own_dn, other_dn, own_w, other_w, before, own_factors, other_factors = refs[count : count + 7]
     grads, out = refs[count + 7 : count + 9]
-    total, rows_grad, w_dn, w_gu, result = refs[count + 9 : count + 14]
-    row_sem, own_sem, other_sem, w_sem, out_sem = refs[count + 14 :]
+    total, w_dn, w_gu, result, own_sem, other_sem, w_sem, out_sem = refs[count + 9 :]
     start_weights(own_w, other_w, block, w_gu, w_sem.at[0], w_sem.at[1])
     total[...] = before[...]
-    add_hidden(
-        first, pieces, own_dn, other_dn, total, rows_grad, w_dn, row_sem, own_sem, other_sem
-    )
+    add_hidden(first, pieces, own_dn, other_dn, total, w_dn, own_sem, other_sem)
     hidden = own_dn.shape[2]
     for core, factors in enumerate((own_factors, other_factors)):
         hidden_grad = total[:, core * hidden : (core + 1) * hidden]
@@ -295,17 +306,15 @@
         functools.partial(hidden_end_kernel, own_dn.shape[0] - count, count, block),
         out_shape=(
             jax.ShapeDtypeStruct((rows, 2 * both), BF16),
-            pltpu.HBM((rows, width), BF16),
+            jax.ShapeDtypeStruct((rows, width), BF16),
         ),
-        in_specs=[ANY] * count + [HBM] * 4 + [VMEM] * 3,
-        out_specs=(VMEM, HBM),
+        in_specs=[VMEM] * count + [HBM] * 4 + [VMEM] * 3,
+        out_specs=(VMEM, ANY),
         scratch_shapes=[
             pltpu.VMEM((rows, both), F32),
-            pltpu.VMEM((count, rows, width), BF16),
             pltpu.VMEM((count, width, both), BF16),
             pltpu.VMEM((2 * both, width), BF16),
             pltpu.VMEM((rows, width), BF16),
-            dma((count,)),
             dma((count,)),
             dma((count,)),
             dma((2,)),
@@ -338,9 +347,9 @@
     dma = pltpu.SemaphoreType.DMA((count,))
     return pl.pallas_call(
         functools.partial(partial_kernel, blocks),
-        out_shape=[pltpu.HBM((rows, width), BF16)] * count,
+        out_shape=[jax.ShapeDtypeStruct((rows, width), BF16)] * count,
         in_specs=[VMEM, HBM, HBM],
-        out_specs=[HBM] * count,
+        out_specs=[ANY] * count,
         scratch_shapes=[
             pltpu.VMEM((count, 2 * both, width), BF16),
             pltpu.VMEM((count, rows, width), BF16),

time: 171 us -> 169 us (0.988)
  Pallas kernels: 42.5 us -> 40.2 us
  waiting for transfers between devices: 80.1 us -> 81.9 us
  transfers between devices with their start and end apart: 23 -> 23, of which waited for: 12 -> 12; matrix products, arithmetic and copies ran while one was open for 2% -> 1% of each run, Pallas kernels for 22% -> 22%
where the time goes in v5:
time: 169 us; the launch traced here: 168 us
  waiting for transfers between devices  81.9 us (48%)
  Pallas kernels  40.2 us (24%)
  starting transfers between devices  38.5 us (23%)
  matrix products  3.59 us (2%)
  other arithmetic  2.33 us (1%)
    ppermute x9, waiting for transfers between devices, chip_step(): return lax.ppermute(value, 'local', pairs)  53.1 us
    all_to_all x3, waiting for transfers between devices, exchange(): lax.all_to_all(value, 'node', split_axis=0, concat_axis=0, tiled=True)  26.6 us
    all_to_all x3, starting transfers between devices, exchange(): lax.all_to_all(value, 'node', split_axis=0, concat_axis=0, tiled=True)  22.3 us
    ppermute x9, starting transfers between devices, chip_step(): return lax.ppermute(value, 'local', pairs)  13.8 us
    pallas_call x1, Pallas kernels, prepare_call(): pl.pallas_call(prepare_kernel, out_shape=(pltpu.HBM((8, width, 2 * hidden...  7.75 us
    pallas_call x1, Pallas kernels, gate_up_total_call(): pl.pallas_call(gate_up_total_kernel, out_shape=(total, total), in_specs=[...  7.66 us
    pallas_call x1, Pallas kernels, gate_up_call(): pl.pallas_call(gate_up_kernel, out_shape=(jax.ShapeDtypeStruct((rows, hid...  6.32 us
    pallas_call x1, Pallas kernels, down_total_call(): pl.pallas_call(down_total_kernel, out_shape=jax.ShapeDtypeStruct((hidden,...  5.49 us
  transfers between devices with their start and end apart: 23, of which 12 were waited for; matrix products, arithmetic and copies ran while one was open for 1% of the time, Pallas kernels for 22%

profile of v5, /device:TPU:32, one launch (start us, length us, event | category | flops | bytes accessed | tf_op | source)
XLA Modules:
  0.0 168.3 jit_solution(1335281736478439327)
XLA Ops:
  3.1 11.2 %all-to-all-start = ((bf16[32,24,512]{2,1,0:T(8,128)(2,1)}), bf16[32,24,512]{2,1,0:T(8,128)(2,1)S(1)}, u32[]{:S(2)}, u32[]{:S(2)}) async-start(bf16[32,24,512]{2,1,0:T(8,128)(2,1)} %bitcast.2), calls=%async_computation | async-start | bytes 1572864 | tf_op jit(solution)/shard_map/all_to_all | solution.py:470
  15.8 7.7 %prepare.1 = (bf16[8,512,512]{2,1,0:T(8,128)(2,1)}, bf16[4,512,512]{2,1,0:T(8,128)(2,1)}, bf16[4,512,512]{2,1,0:T(8,128)(2,1)}, bf16[8,512,256]{2,1,0:T(8,128)(2,1)}) custom-call(s32[8]{0:T(128)S(1)} %stack.35.order, bf16[4096,256]{1,0:T(8,128)(2,1)} %bitcast.40, bf16[4096,256]{1,0:T(8,128)(2,1)} %bitcast.41, bf16[4096,256]{1,0:T(8,128)(2,1)} %bitcast.42, ...), custom_call_target="tpu_custom_call" | custom-call | flops 1610612736 | bytes 16777216 | tf_op jit(solution)/shard_map/prepare/pallas_call | solution.py:134
  23.5 13.9 %all-to-all-done = bf16[32,24,512]{2,1,0:T(8,128)(2,1)S(1)} async-done(((bf16[32,24,512]{2,1,0:T(8,128)(2,1)}), bf16[32,24,512]{2,1,0:T(8,128)(2,1)S(1)}, u32[]{:S(2)}, u32[]{:S(2)}) %all-to-all-start) | async-done | bytes 786464 | tf_op jit(solution)/shard_map/all_to_all | solution.py:470
  39.0 4.9 %all-to-all-start.1 = ((bf16[32,24,512]{2,1,0:T(8,128)(2,1)}), bf16[32,24,512]{2,1,0:T(8,128)(2,1)S(1)}, u32[]{:S(2)}, u32[]{:S(2)}) async-start(bf16[32,24,512]{2,1,0:T(8,128)(2,1)} %bitcast.15), calls=%async_computation.1 | async-start | bytes 1572864 | tf_op jit(solution)/shard_map/all_to_all | solution.py:470
  44.0 1.7 %collective-permute-start.11 = (bf16[768,512]{1,0:T(8,128)(2,1)S(1)}, bf16[768,512]{1,0:T(8,128)(2,1)S(1)}, u32[]{:S(2)}, u32[]{:S(2)}) collective-permute-start(bf16[768,512]{1,0:T(8,128)(2,1)S(1)} %bitcast.49), channel_id=1, source_target_pairs={{0,6},{1,3},{2,0},{3,5},{4,2},{5,7},{6,4},{7,1},{8,14},{9,11},{10,... | collective-permute-start | bytes 2359304 | tf_op jit(solution)/shard_map/ppermute | solution.py:45
  45.7 7.7 %collective-permute-done.refs_2_ = bf16[768,512]{1,0:T(8,128)(2,1)S(1)} collective-permute-done((bf16[768,512]{1,0:T(8,128)(2,1)S(1)}, bf16[768,512]{1,0:T(8,128)(2,1)S(1)}, u32[]{:S(2)}, u32[]{:S(2)}) %collective-permute-start) | collective-permute-done | bytes 786464 | tf_op jit(solution)/shard_map/ppermute | solution.py:45
  53.4 2.0 %collective-permute-start.1 = (bf16[768,512]{1,0:T(8,128)(2,1)S(1)}, bf16[768,512]{1,0:T(8,128)(2,1)}, u32[]{:S(2)}, u32[]{:S(2)}) collective-permute-start(bf16[768,512]{1,0:T(8,128)(2,1)S(1)} %collective-permute-done.refs_2_), channel_id=1, source_target_pairs={{0,2},{1,7},{2,4},{3,1},{4,6},{5,3},{6,0},{7,5},{8,10},{9,15},{10,... | collective-permute-start | bytes 2359304 | tf_op jit(solution)/shard_map/ppermute | solution.py:45
  56.0 6.7 %collective-permute-done.11.refs_4_ = bf16[768,512]{1,0:T(8,128)(2,1)S(1)} collective-permute-done((bf16[768,512]{1,0:T(8,128)(2,1)S(1)}, bf16[768,512]{1,0:T(8,128)(2,1)S(1)}, u32[]{:S(2)}, u32[]{:S(2)}) %collective-permute-start.11) | collective-permute-done | bytes 786464 | tf_op jit(solution)/shard_map/ppermute | solution.py:45
  62.7 4.6 %all-to-all-done.1 = bf16[32,24,512]{2,1,0:T(8,128)(2,1)S(1)} async-done(((bf16[32,24,512]{2,1,0:T(8,128)(2,1)}), bf16[32,24,512]{2,1,0:T(8,128)(2,1)S(1)}, u32[]{:S(2)}, u32[]{:S(2)}) %all-to-all-start.1) | async-done | bytes 786464 | tf_op jit(solution)/shard_map/all_to_all | solution.py:470
  68.5 2.9 %collective-permute-start.6 = (bf16[768,512]{1,0:T(8,128)(2,1)S(1)}, bf16[768,512]{1,0:T(8,128)(2,1)S(1)}, u32[]{:S(2)}, u32[]{:S(2)}) collective-permute-start(bf16[768,512]{1,0:T(8,128)(2,1)S(1)} %bitcast.36), channel_id=1, source_target_pairs={{0,6},{1,3},{2,0},{3,5},{4,2},{5,7},{6,4},{7,1},{8,14},{9,11},{10,... | collective-permute-start | bytes 2359304 | tf_op jit(solution)/shard_map/ppermute | solution.py:45
  71.4 17.9 %collective-permute-done.2.refs_2_ = bf16[768,512]{1,0:T(8,128)(2,1)S(1)} collective-permute-done((bf16[768,512]{1,0:T(8,128)(2,1)S(1)}, bf16[768,512]{1,0:T(8,128)(2,1)S(1)}, u32[]{:S(2)}, u32[]{:S(2)}) %collective-permute-start.2) | collective-permute-done | bytes 786464 | tf_op jit(solution)/shard_map/ppermute | solution.py:45
  90.3 6.3 %gate_up.1 = (bf16[768,256]{1,0:T(8,128)(2,1)S(1)}, f32[768,512]{1,0:T(8,128)S(1)}) custom-call(bf16[768,512]{1,0:T(8,128)(2,1)} %bitcast.51, bf16[768,512]{1,0:T(8,128)(2,1)} %collective-permute-done.9.refs_1_, bf16[768,512]{1,0:T(8,128)(2,1)} %copy-done.14, bf16[768,512]{1,0:T(8,128)(2,1)} %collective-permute-done.10.refs_3_, bf16[768,512]{1,0:T(8,128)(2,1)} %copy-done.15, ...), custom_call_target="tpu_custom_call" | custom-call | flops 3221225472 | bytes 10485760 | tf_op jit(solution)/shard_map/gate_up/pallas_call | solution.py:190
  97.2 5.1 %hidden_start.1.refs_6_ = f32[768,512]{1,0:T(8,128)S(1)} custom-call(bf16[768,512]{1,0:T(8,128)(2,1)S(1)} %bitcast.37, bf16[768,512]{1,0:T(8,128)(2,1)S(1)} %collective-permute-done.4.refs_1_, bf16[768,512]{1,0:T(8,128)(2,1)S(1)} %collective-permute-done.2.refs_2_, bf16[768,512]{1,0:T(8,128)(2,1)S(1)} %collective-permute-done.5.refs_3_, ...), custom_call_target="tpu_custom_call" | custom-call | flops 2415919104 | bytes 7864320 | tf_op jit(solution)/shard_map/hidden_start/pallas_call | solution.py:255
  102.6 2.2 %collective-permute-done.14.refs_1_.refs_7_ = bf16[768,512]{1,0:T(8,128)(2,1)S(1)} collective-permute-done((bf16[768,512]{1,0:T(8,128)(2,1)S(1)}, bf16[768,512]{1,0:T(8,128)(2,1)S(1)}, u32[]{:S(2)}, u32[]{:S(2)}) %collective-permute-start.14) | collective-permute-done | bytes 786464 | tf_op jit(solution)/shard_map/ppermute | solution.py:49
  104.8 3.5 %hidden_end.1 = (bf16[768,1024]{1,0:T(8,128)(2,1)S(1)}, bf16[768,512]{1,0:T(8,128)(2,1)S(1)}) custom-call(bf16[768,512]{1,0:T(8,128)(2,1)S(1)} %collective-permute-done.3.refs_0_.refs_6_, bf16[768,512]{1,0:T(8,128)(2,1)S(1)} %collective-permute-done.14.refs_1_.refs_7_, bf16[8,512,256]{2,1,0:T(8,128)(2,1)} %get-tuple-element.30.refs_6_.refs_2_, ...), custom_call_target="tpu_custom_call" | custom-call | flops 1610612736 | bytes 2621440 | tf_op jit(solution)/shard_map/hidden_end/pallas_call | solution.py:305
  110.0 4.4 %partial.1 = (bf16[768,512]{1,0:T(8,128)(2,1)S(1)}, bf16[768,512]{1,0:T(8,128)(2,1)S(1)}, bf16[768,512]{1,0:T(8,128)(2,1)S(1)}) custom-call(bf16[768,1024]{1,0:T(8,128)(2,1)S(1)} %get-tuple-element.37.refs_0_.refs_8_, bf16[4,512,512]{2,1,0:T(8,128)(2,1)} %get-tuple-element.33.refs_4_.refs_1_, bf16[4,512,512]{2,1,0:T(8,128)(2,1)} %copy-done.11), custom_call_target="tpu_custom_call" | custom-call | flops 2415919104 | bytes 11010048 | tf_op jit(solution)/shard_map/partial/pallas_call | solution.py:348
  116.2 7.4 %collective-permute-done.18 = bf16[768,512]{1,0:T(8,128)(2,1)S(1)} collective-permute-done((bf16[768,512]{1,0:T(8,128)(2,1)S(1)}, bf16[768,512]{1,0:T(8,128)(2,1)S(1)}, u32[]{:S(2)}, u32[]{:S(2)}) %collective-permute-start.18) | collective-permute-done | bytes 786464 | tf_op jit(solution)/shard_map/ppermute | solution.py:45
  123.7 1.8 %collective-permute-start.19 = (bf16[768,512]{1,0:T(8,128)(2,1)S(1)}, bf16[768,512]{1,0:T(8,128)(2,1)S(1)}, u32[]{:S(2)}, u32[]{:S(2)}) collective-permute-start(bf16[768,512]{1,0:T(8,128)(2,1)S(1)} %add_convert_fusion.1), channel_id=1, source_target_pairs={{0,2},{1,7},{2,4},{3,1},{4,6},{5,3},{6,0},{7,5},{8,10},{9,15},{10,... | collective-permute-start | bytes 2359304 | tf_op jit(solution)/shard_map/ppermute | solution.py:45
  125.5 4.4 %collective-permute-done.17 = bf16[768,512]{1,0:T(8,128)(2,1)S(1)} collective-permute-done((bf16[768,512]{1,0:T(8,128)(2,1)S(1)}, bf16[768,512]{1,0:T(8,128)(2,1)S(1)}, u32[]{:S(2)}, u32[]{:S(2)}) %collective-permute-start.17) | collective-permute-done | bytes 786464 | tf_op jit(solution)/shard_map/ppermute | solution.py:45
  129.9 8.6 %collective-permute-done.19 = bf16[768,512]{1,0:T(8,128)(2,1)S(1)} collective-permute-done((bf16[768,512]{1,0:T(8,128)(2,1)S(1)}, bf16[768,512]{1,0:T(8,128)(2,1)S(1)}, u32[]{:S(2)}, u32[]{:S(2)}) %collective-permute-start.19) | collective-permute-done | bytes 786464 | tf_op jit(solution)/shard_map/ppermute | solution.py:45
  139.7 6.2 %all-to-all-start.2 = ((bf16[32,24,512]{2,1,0:T(8,128)(2,1)}), bf16[32,24,512]{2,1,0:T(8,128)(2,1)S(1)}, u32[]{:S(2)}, u32[]{:S(2)}) async-start(bf16[32,24,512]{2,1,0:T(8,128)(2,1)} %bitcast.46), calls=%async_computation.2 | async-start | bytes 1572864 | tf_op jit(solution)/shard_map/all_to_all | solution.py:470
  146.1 5.5 %down_total.1 = bf16[256,4096]{1,0:T(8,128)(2,1)} custom-call(s32[8]{0:T(128)S(1)} %stack.35.order, bf16[768,512]{1,0:T(8,128)(2,1)} %bitcast.38, bf16[768,512]{1,0:T(8,128)(2,1)} %copy-done.5, bf16[768,512]{1,0:T(8,128)(2,1)} %copy-done.4, bf16[768,512]{1,0:T(8,128)(2,1)} %copy-done.7, bf16[768,512]{1,0:T(8,128)(2,1)} %copy-done.6, ...), custom_call_target="tpu_custom_call" | custom-call | flops 1610612736 | bytes 8388608 | tf_op jit(solution)/shard_map/down_total/pallas_call | solution.py:390
  151.6 7.7 %gate_up_total.1 = (bf16[4096,256]{1,0:T(8,128)(2,1)}, bf16[4096,256]{1,0:T(8,128)(2,1)}) custom-call(s32[8]{0:T(128)S(1)} %stack.35.order, bf16[768,512]{1,0:T(8,128)(2,1)} %bitcast.52, bf16[768,512]{1,0:T(8,128)(2,1)} %collective-permute-done.9.refs_1_, bf16[768,512]{1,0:T(8,128)(2,1)} %copy-done.14, bf16[768,512]{1,0:T(8,128)(2,1)} %collective-permute-done.10.refs_3_, ...), custom_call_target="tpu_custom_call" | custom-call | flops 3221225472 | bytes 10485760 | tf_op jit(solution)/shard_map/gate_up_total/pallas_call | solution.py:440
  159.3 8.1 %all-to-all-done.2 = bf16[32,24,512]{2,1,0:T(8,128)(2,1)S(1)} async-done(((bf16[32,24,512]{2,1,0:T(8,128)(2,1)}), bf16[32,24,512]{2,1,0:T(8,128)(2,1)S(1)}, u32[]{:S(2)}, u32[]{:S(2)}) %all-to-all-start.2) | async-done | bytes 786464 | tf_op jit(solution)/shard_map/all_to_all | solution.py:470
  (75 shorter events, 14.8 us)
Async XLA Ops:
  3.1 34.4 %all-to-all-start = ((bf16[32,24,512]{2,1,0:T(8,128)(2,1)}), bf16[32,24,512]{2,1,0:T(8,128)(2,1)S(1)}, u32[]{:S(2)}, u32[]{:S(2)}) async-start(bf16[32,24,512]{2,1,0:T(8,128)(2,1)} %bitcast.2), calls=%async_computation | async-start | bytes 1572864 | tf_op jit(solution)/shard_map/all_to_all | solution.py:470
  37.4 52.7 %copy-start.12 = (bf16[32,24,512]{2,1,0:T(8,128)(2,1)}, bf16[32,24,512]{2,1,0:T(8,128)(2,1)S(1)}, u32[]{:S(2)}) copy-start(bf16[32,24,512]{2,1,0:T(8,128)(2,1)S(1)} %all-to-all-done) | copy-start | bytes 2359300
  37.4 16.0 %collective-permute-start = (bf16[768,512]{1,0:T(8,128)(2,1)S(1)}, bf16[768,512]{1,0:T(8,128)(2,1)S(1)}, u32[]{:S(2)}, u32[]{:S(2)}) collective-permute-start(bf16[768,512]{1,0:T(8,128)(2,1)S(1)} %bitcast.48), channel_id=1, source_target_pairs={{0,2},{1,7},{2,4},{3,1},{4,6},{5,3},{6,0},{7,5},{8,10},{9,15},{10,... | collective-permute-start | bytes 2359304 | tf_op jit(solution)/shard_map/ppermute | solution.py:45
  39.0 28.3 %all-to-all-start.1 = ((bf16[32,24,512]{2,1,0:T(8,128)(2,1)}), bf16[32,24,512]{2,1,0:T(8,128)(2,1)S(1)}, u32[]{:S(2)}, u32[]{:S(2)}) async-start(bf16[32,24,512]{2,1,0:T(8,128)(2,1)} %bitcast.15), calls=%async_computation.1 | async-start | bytes 1572864 | tf_op jit(solution)/shard_map/all_to_all | solution.py:470
  44.0 18.7 %collective-permute-start.11 = (bf16[768,512]{1,0:T(8,128)(2,1)S(1)}, bf16[768,512]{1,0:T(8,128)(2,1)S(1)}, u32[]{:S(2)}, u32[]{:S(2)}) collective-permute-start(bf16[768,512]{1,0:T(8,128)(2,1)S(1)} %bitcast.49), channel_id=1, source_target_pairs={{0,6},{1,3},{2,0},{3,5},{4,2},{5,7},{6,4},{7,1},{8,14},{9,11},{10,... | collective-permute-start | bytes 2359304 | tf_op jit(solution)/shard_map/ppermute | solution.py:45
  53.4 14.2 %collective-permute-start.1 = (bf16[768,512]{1,0:T(8,128)(2,1)S(1)}, bf16[768,512]{1,0:T(8,128)(2,1)}, u32[]{:S(2)}, u32[]{:S(2)}) collective-permute-start(bf16[768,512]{1,0:T(8,128)(2,1)S(1)} %collective-permute-done.refs_2_), channel_id=1, source_target_pairs={{0,2},{1,7},{2,4},{3,1},{4,6},{5,3},{6,0},{7,5},{8,10},{9,15},{10,... | collective-permute-start | bytes 2359304 | tf_op jit(solution)/shard_map/ppermute | solution.py:45
  55.4 41.2 %collective-permute-start.8 = (bf16[8,512,256]{2,1,0:T(8,128)(2,1)}, bf16[8,512,256]{2,1,0:T(8,128)(2,1)}, u32[]{:S(2)}, u32[]{:S(2)}) collective-permute-start(bf16[8,512,256]{2,1,0:T(8,128)(2,1)} %get-tuple-element.30.refs_6_.refs_2_), channel_id=1, source_target_pairs={{0,1},{1,0},{2,3},{3,2},{4,5},{5,4},{6,7},{7,6},{8,9},{9,8},{10,11... | collective-permute-start | bytes 6291464 | tf_op jit(solution)/shard_map/ppermute | solution.py:49
  55.5 12.5 %collective-permute-start.9 = (bf16[768,512]{1,0:T(8,128)(2,1)S(1)}, bf16[768,512]{1,0:T(8,128)(2,1)}, u32[]{:S(2)}, u32[]{:S(2)}) collective-permute-start(bf16[768,512]{1,0:T(8,128)(2,1)S(1)} %bitcast.50), channel_id=1, source_target_pairs={{0,1},{1,0},{2,3},{3,2},{4,5},{5,4},{6,7},{7,6},{8,9},{9,8},{10,11... | collective-permute-start | bytes 2359304 | tf_op jit(solution)/shard_map/ppermute | solution.py:49
  56.0 12.0 %collective-permute-start.10 = (bf16[768,512]{1,0:T(8,128)(2,1)S(1)}, bf16[768,512]{1,0:T(8,128)(2,1)}, u32[]{:S(2)}, u32[]{:S(2)}) collective-permute-start(bf16[768,512]{1,0:T(8,128)(2,1)S(1)} %collective-permute-done.refs_2_), channel_id=1, source_target_pairs={{0,1},{1,0},{2,3},{3,2},{4,5},{5,4},{6,7},{7,6},{8,9},{9,8},{10,11... | collective-permute-start | bytes 2359304 | tf_op jit(solution)/shard_map/ppermute | solution.py:49
  62.7 5.8 %collective-permute-start.12 = (bf16[768,512]{1,0:T(8,128)(2,1)S(1)}, bf16[768,512]{1,0:T(8,128)(2,1)}, u32[]{:S(2)}, u32[]{:S(2)}) collective-permute-start(bf16[768,512]{1,0:T(8,128)(2,1)S(1)} %collective-permute-done.11.refs_4_), channel_id=1, source_target_pairs={{0,1},{1,0},{2,3},{3,2},{4,5},{5,4},{6,7},{7,6},{8,9},{9,8},{10,11... | collective-permute-start | bytes 2359304 | tf_op jit(solution)/shard_map/ppermute | solution.py:49
  67.6 21.6 %collective-permute-start.2 = (bf16[768,512]{1,0:T(8,128)(2,1)S(1)}, bf16[768,512]{1,0:T(8,128)(2,1)S(1)}, u32[]{:S(2)}, u32[]{:S(2)}) collective-permute-start(bf16[768,512]{1,0:T(8,128)(2,1)S(1)} %bitcast.34), channel_id=1, source_target_pairs={{0,2},{1,7},{2,4},{3,1},{4,6},{5,3},{6,0},{7,5},{8,10},{9,15},{10,... | collective-permute-start | bytes 2359304 | tf_op jit(solution)/shard_map/ppermute | solution.py:45
  68.0 21.3 %collective-permute-start.4 = (bf16[768,512]{1,0:T(8,128)(2,1)S(1)}, bf16[768,512]{1,0:T(8,128)(2,1)S(1)}, u32[]{:S(2)}, u32[]{:S(2)}) collective-permute-start(bf16[768,512]{1,0:T(8,128)(2,1)S(1)} %bitcast.35), channel_id=1, source_target_pairs={{0,1},{1,0},{2,3},{3,2},{4,5},{5,4},{6,7},{7,6},{8,9},{9,8},{10,11... | collective-permute-start | bytes 2359304 | tf_op jit(solution)/shard_map/ppermute | solution.py:49
  68.0 21.4 %collective-permute-start.13 = (bf16[768,512]{1,0:T(8,128)(2,1)}, bf16[768,512]{1,0:T(8,128)(2,1)S(1)}, u32[]{:S(2)}, u32[]{:S(2)}) collective-permute-start(bf16[768,512]{1,0:T(8,128)(2,1)} %collective-permute-done.1.refs_6_), channel_id=1, source_target_pairs={{0,1},{1,0},{2,3},{3,2},{4,5},{5,4},{6,7},{7,6},{8,9},{9,8},{10,11... | collective-permute-start | bytes 2359304 | tf_op jit(solution)/shard_map/ppermute | solution.py:49
  68.5 21.4 %collective-permute-start.6 = (bf16[768,512]{1,0:T(8,128)(2,1)S(1)}, bf16[768,512]{1,0:T(8,128)(2,1)S(1)}, u32[]{:S(2)}, u32[]{:S(2)}) collective-permute-start(bf16[768,512]{1,0:T(8,128)(2,1)S(1)} %bitcast.36), channel_id=1, source_target_pairs={{0,6},{1,3},{2,0},{3,5},{4,2},{5,7},{6,4},{7,1},{8,14},{9,11},{10,... | collective-permute-start | bytes 2359304 | tf_op jit(solution)/shard_map/ppermute | solution.py:45
  89.2 13.4 %collective-permute-start.15 = (bf16[4,512,512]{2,1,0:T(8,128)(2,1)}, bf16[4,512,512]{2,1,0:T(8,128)(2,1)S(1)}, u32[]{:S(2)}, u32[]{:S(2)}) collective-permute-start(bf16[4,512,512]{2,1,0:T(8,128)(2,1)} %get-tuple-element.35), channel_id=1, source_target_pairs={{0,1},{1,0},{2,3},{3,2},{4,5},{5,4},{6,7},{7,6},{8,9},{9,8},{10,11... | collective-permute-start | bytes 6291464 | tf_op jit(solution)/shard_map/ppermute | solution.py:49
  89.2 13.3 %collective-permute-start.3 = (bf16[768,512]{1,0:T(8,128)(2,1)S(1)}, bf16[768,512]{1,0:T(8,128)(2,1)S(1)}, u32[]{:S(2)}, u32[]{:S(2)}) collective-permute-start(bf16[768,512]{1,0:T(8,128)(2,1)S(1)} %collective-permute-done.2.refs_2_), channel_id=1, source_target_pairs={{0,2},{1,7},{2,4},{3,1},{4,6},{5,3},{6,0},{7,5},{8,10},{9,15},{10,... | collective-permute-start | bytes 2359304 | tf_op jit(solution)/shard_map/ppermute | solution.py:45
  89.3 7.8 %collective-permute-start.5 = (bf16[768,512]{1,0:T(8,128)(2,1)S(1)}, bf16[768,512]{1,0:T(8,128)(2,1)S(1)}, u32[]{:S(2)}, u32[]{:S(2)}) collective-permute-start(bf16[768,512]{1,0:T(8,128)(2,1)S(1)} %collective-permute-done.2.refs_2_), channel_id=1, source_target_pairs={{0,1},{1,0},{2,3},{3,2},{4,5},{5,4},{6,7},{7,6},{8,9},{9,8},{10,11... | collective-permute-start | bytes 2359304 | tf_op jit(solution)/shard_map/ppermute | solution.py:49
  89.8 7.3 %collective-permute-start.7 = (bf16[768,512]{1,0:T(8,128)(2,1)S(1)}, bf16[768,512]{1,0:T(8,128)(2,1)S(1)}, u32[]{:S(2)}, u32[]{:S(2)}) collective-permute-start(bf16[768,512]{1,0:T(8,128)(2,1)S(1)} %collective-permute-done.6.refs_4_), channel_id=1, source_target_pairs={{0,1},{1,0},{2,3},{3,2},{4,5},{5,4},{6,7},{7,6},{8,9},{9,8},{10,11... | collective-permute-start | bytes 2359304 | tf_op jit(solution)/shard_map/ppermute | solution.py:49
  96.7 8.1 %collective-permute-start.16 = (f32[768,512]{1,0:T(8,128)S(1)}, f32[768,512]{1,0:T(8,128)S(1)}, u32[]{:S(2)}, u32[]{:S(2)}) collective-permute-start(f32[768,512]{1,0:T(8,128)S(1)} %get-tuple-element.36.refs_7_), channel_id=1, source_target_pairs={{0,1},{1,0},{2,3},{3,2},{4,5},{5,4},{6,7},{7,6},{8,9},{9,8},{10,11... | collective-permute-start | bytes 4718600 | tf_op jit(solution)/shard_map/ppermute | solution.py:49
  102.5 2.3 %collective-permute-start.14 = (bf16[768,512]{1,0:T(8,128)(2,1)S(1)}, bf16[768,512]{1,0:T(8,128)(2,1)S(1)}, u32[]{:S(2)}, u32[]{:S(2)}) collective-permute-start(bf16[768,512]{1,0:T(8,128)(2,1)S(1)} %collective-permute-done.3.refs_0_.refs_6_), channel_id=1, source_target_pairs={{0,1},{1,0},{2,3},{3,2},{4,5},{5,4},{6,7},{7,6},{8,9},{9,8},{10,11... | collective-permute-start | bytes 2359304 | tf_op jit(solution)/shard_map/ppermute | solution.py:49
  108.3 15.2 %collective-permute-start.18 = (bf16[768,512]{1,0:T(8,128)(2,1)S(1)}, bf16[768,512]{1,0:T(8,128)(2,1)S(1)}, u32[]{:S(2)}, u32[]{:S(2)}) collective-permute-start(bf16[768,512]{1,0:T(8,128)(2,1)S(1)} %get-tuple-element.41), channel_id=1, source_target_pairs={{0,2},{1,7},{2,4},{3,1},{4,6},{5,3},{6,0},{7,5},{8,10},{9,15},{10,... | collective-permute-start | bytes 2359304 | tf_op jit(solution)/shard_map/ppermute | solution.py:45
  114.4 15.5 %collective-permute-start.17 = (bf16[768,512]{1,0:T(8,128)(2,1)S(1)}, bf16[768,512]{1,0:T(8,128)(2,1)S(1)}, u32[]{:S(2)}, u32[]{:S(2)}) collective-permute-start(bf16[768,512]{1,0:T(8,128)(2,1)S(1)} %get-tuple-element.39), channel_id=1, source_target_pairs={{0,6},{1,3},{2,0},{3,5},{4,2},{5,7},{6,4},{7,1},{8,14},{9,11},{10,... | collective-permute-start | bytes 2359304 | tf_op jit(solution)/shard_map/ppermute | solution.py:45
  123.7 14.7 %collective-permute-start.19 = (bf16[768,512]{1,0:T(8,128)(2,1)S(1)}, bf16[768,512]{1,0:T(8,128)(2,1)S(1)}, u32[]{:S(2)}, u32[]{:S(2)}) collective-permute-start(bf16[768,512]{1,0:T(8,128)(2,1)S(1)} %add_convert_fusion.1), channel_id=1, source_target_pairs={{0,2},{1,7},{2,4},{3,1},{4,6},{5,3},{6,0},{7,5},{8,10},{9,15},{10,... | collective-permute-start | bytes 2359304 | tf_op jit(solution)/shard_map/ppermute | solution.py:45
  139.7 27.6 %all-to-all-start.2 = ((bf16[32,24,512]{2,1,0:T(8,128)(2,1)}), bf16[32,24,512]{2,1,0:T(8,128)(2,1)S(1)}, u32[]{:S(2)}, u32[]{:S(2)}) async-start(bf16[32,24,512]{2,1,0:T(8,128)(2,1)} %bitcast.46), calls=%async_computation.2 | async-start | bytes 1572864 | tf_op jit(solution)/shard_map/all_to_all | solution.py:470
  (16 other events, 167.0 us)

commit v6 on v5

--- a/solution.py
+++ b/solution.py
@@ -280,7 +280,7 @@
     pieces = refs[:count]
     own_dn, other_dn, own_w, other_w, before, own_factors, other_factors = refs[count : count + 7]
     grads, out = refs[count + 7 : count + 9]
-    total, w_dn, w_gu, result, own_sem, other_sem, w_sem, out_sem = refs[count + 9 :]
+    total, w_dn, w_gu, own_sem, other_sem, w_sem = refs[count + 9 :]
     start_weights(own_w, other_w, block, w_gu, w_sem.at[0], w_sem.at[1])
     total[...] = before[...]
     add_hidden(first, pieces, own_dn, other_dn, total, w_dn, own_sem, other_sem)
@@ -292,10 +292,7 @@
         grads[:, at + hidden : at + 2 * hidden] = (hidden_grad * factors[:, hidden:]).astype(BF16)
     wait_for(own_w.at[0], w_sem.at[0])
     wait_for(other_w.at[0], w_sem.at[1])
-    result[...] = jnp.dot(grads[...], w_gu[...], preferred_element_type=F32).astype(BF16)
-    copy = pltpu.make_async_copy(result, out, out_sem)
-    copy.start()
-    copy.wait()
+    out[...] = jnp.dot(grads[...], w_gu[...], preferred_element_type=F32).astype(BF16)
 
 
 def hidden_end_call(pieces, own_dn, other_dn, own_w, other_w, before, factors, others, block):
@@ -309,16 +306,14 @@
             jax.ShapeDtypeStruct((rows, width), BF16),
         ),
         in_specs=[VMEM] * count + [HBM] * 4 + [VMEM] * 3,
-        out_specs=(VMEM, ANY),
+        out_specs=(VMEM, VMEM),
         scratch_shapes=[
             pltpu.VMEM((rows, both), F32),
             pltpu.VMEM((count, width, both), BF16),
             pltpu.VMEM((2 * both, width), BF16),
-            pltpu.VMEM((rows, width), BF16),
             dma((count,)),
             dma((count,)),
             dma((2,)),
-            dma,
         ],
         compiler_params=params(20),
         cost_estimate=cost(rows, (count + 2) * width, both, count * width * (rows + both) * 2),
@@ -330,15 +325,13 @@
     count = len(blocks)
     grads, own_w, other_w = refs[:3]
     outs = refs[3 : 3 + count]
-    w_gu, result, own_sem, other_sem, out_sem = refs[3 + count :]
+    w_gu, own_sem, other_sem = refs[3 + count :]
     for i, j in enumerate(blocks):
         start_weights(own_w, other_w, j, w_gu.at[i], own_sem.at[i], other_sem.at[i])
     for i in range(count):
         wait_for(own_w.at[0], own_sem.at[i])
         wait_for(other_w.at[0], other_sem.at[i])
-        result[i] = jnp.dot(grads[...], w_gu[i], preferred_element_type=F32).astype(BF16)
-        pltpu.make_async_copy(result.at[i], outs[i], out_sem.at[i]).start()
-    finish(result, out_sem)
+        outs[i][...] = jnp.dot(grads[...], w_gu[i], preferred_element_type=F32).astype(BF16)
 
 
 def partial_call(grads, own_w, other_w, blocks):
@@ -349,11 +342,9 @@
         functools.partial(partial_kernel, blocks),
         out_shape=[jax.ShapeDtypeStruct((rows, width), BF16)] * count,
         in_specs=[VMEM, HBM, HBM],
-        out_specs=[ANY] * count,
+        out_specs=[VMEM] * count,
         scratch_shapes=[
             pltpu.VMEM((count, 2 * both, width), BF16),
-            pltpu.VMEM((count, rows, width), BF16),
-            dma,
             dma,
             dma,
         ],

time: 169 us -> 169 us (level)
  no operation moved by 1% of the time
where the time goes in v6:
time: 169 us; the launch traced here: 168 us
  waiting for transfers between devices  82.1 us (49%)
  Pallas kernels  40 us (24%)
  starting transfers between devices  38.5 us (23%)
  matrix products  3.58 us (2%)
  other arithmetic  2.33 us (1%)
    ppermute x9, waiting for transfers between devices, chip_step(): return lax.ppermute(value, 'local', pairs)  53.3 us
    all_to_all x3, waiting for transfers between devices, exchange(): lax.all_to_all(value, 'node', split_axis=0, concat_axis=0, tiled=True)  26.6 us
    all_to_all x3, starting transfers between devices, exchange(): lax.all_to_all(value, 'node', split_axis=0, concat_axis=0, tiled=True)  22.3 us
    ppermute x9, starting transfers between devices, chip_step(): return lax.ppermute(value, 'local', pairs)  13.8 us
    pallas_call x1, Pallas kernels, prepare_call(): pl.pallas_call(prepare_kernel, out_shape=(pltpu.HBM((8, width, 2 * hidden...  7.75 us
    pallas_call x1, Pallas kernels, gate_up_total_call(): pl.pallas_call(gate_up_total_kernel, out_shape=(total, total), in_specs=[...  7.66 us
    pallas_call x1, Pallas kernels, gate_up_call(): pl.pallas_call(gate_up_kernel, out_shape=(jax.ShapeDtypeStruct((rows, hid...  6.32 us
    pallas_call x1, Pallas kernels, down_total_call(): pl.pallas_call(down_total_kernel, out_shape=jax.ShapeDtypeStruct((hidden,...  5.49 us
  transfers between devices with their start and end apart: 23, of which 12 were waited for; matrix products, arithmetic and copies ran while one was open for 1% of the time, Pallas kernels for 22%

profile of v6, /device:TPU:32, one launch (start us, length us, event | category | flops | bytes accessed | tf_op | source)
XLA Modules:
  0.0 168.2 jit_solution(699186847927491511)
XLA Ops:
  3.1 11.2 %all-to-all-start = ((bf16[32,24,512]{2,1,0:T(8,128)(2,1)}), bf16[32,24,512]{2,1,0:T(8,128)(2,1)S(1)}, u32[]{:S(2)}, u32[]{:S(2)}) async-start(bf16[32,24,512]{2,1,0:T(8,128)(2,1)} %bitcast.2), calls=%async_computation | async-start | bytes 1572864 | tf_op jit(solution)/shard_map/all_to_all | solution.py:461
  15.8 7.7 %prepare.1 = (bf16[8,512,512]{2,1,0:T(8,128)(2,1)}, bf16[4,512,512]{2,1,0:T(8,128)(2,1)}, bf16[4,512,512]{2,1,0:T(8,128)(2,1)}, bf16[8,512,256]{2,1,0:T(8,128)(2,1)}) custom-call(s32[8]{0:T(128)S(1)} %stack.35.order, bf16[4096,256]{1,0:T(8,128)(2,1)} %bitcast.40, bf16[4096,256]{1,0:T(8,128)(2,1)} %bitcast.41, bf16[4096,256]{1,0:T(8,128)(2,1)} %bitcast.42, ...), custom_call_target="tpu_custom_call" | custom-call | flops 1610612736 | bytes 16777216 | tf_op jit(solution)/shard_map/prepare/pallas_call | solution.py:134
  23.5 13.9 %all-to-all-done = bf16[32,24,512]{2,1,0:T(8,128)(2,1)S(1)} async-done(((bf16[32,24,512]{2,1,0:T(8,128)(2,1)}), bf16[32,24,512]{2,1,0:T(8,128)(2,1)S(1)}, u32[]{:S(2)}, u32[]{:S(2)}) %all-to-all-start) | async-done | bytes 786464 | tf_op jit(solution)/shard_map/all_to_all | solution.py:461
  39.0 4.9 %all-to-all-start.1 = ((bf16[32,24,512]{2,1,0:T(8,128)(2,1)}), bf16[32,24,512]{2,1,0:T(8,128)(2,1)S(1)}, u32[]{:S(2)}, u32[]{:S(2)}) async-start(bf16[32,24,512]{2,1,0:T(8,128)(2,1)} %bitcast.15), calls=%async_computation.1 | async-start | bytes 1572864 | tf_op jit(solution)/shard_map/all_to_all | solution.py:461
  44.0 1.7 %collective-permute-start.11 = (bf16[768,512]{1,0:T(8,128)(2,1)S(1)}, bf16[768,512]{1,0:T(8,128)(2,1)S(1)}, u32[]{:S(2)}, u32[]{:S(2)}) collective-permute-start(bf16[768,512]{1,0:T(8,128)(2,1)S(1)} %bitcast.49), channel_id=1, source_target_pairs={{0,6},{1,3},{2,0},{3,5},{4,2},{5,7},{6,4},{7,1},{8,14},{9,11},{10,... | collective-permute-start | bytes 2359304 | tf_op jit(solution)/shard_map/ppermute | solution.py:45
  45.7 7.7 %collective-permute-done.refs_2_ = bf16[768,512]{1,0:T(8,128)(2,1)S(1)} collective-permute-done((bf16[768,512]{1,0:T(8,128)(2,1)S(1)}, bf16[768,512]{1,0:T(8,128)(2,1)S(1)}, u32[]{:S(2)}, u32[]{:S(2)}) %collective-permute-start) | collective-permute-done | bytes 786464 | tf_op jit(solution)/shard_map/ppermute | solution.py:45
  53.4 2.0 %collective-permute-start.1 = (bf16[768,512]{1,0:T(8,128)(2,1)S(1)}, bf16[768,512]{1,0:T(8,128)(2,1)}, u32[]{:S(2)}, u32[]{:S(2)}) collective-permute-start(bf16[768,512]{1,0:T(8,128)(2,1)S(1)} %collective-permute-done.refs_2_), channel_id=1, source_target_pairs={{0,2},{1,7},{2,4},{3,1},{4,6},{5,3},{6,0},{7,5},{8,10},{9,15},{10,... | collective-permute-start | bytes 2359304 | tf_op jit(solution)/shard_map/ppermute | solution.py:45
  56.0 6.7 %collective-permute-done.11.refs_4_ = bf16[768,512]{1,0:T(8,128)(2,1)S(1)} collective-permute-done((bf16[768,512]{1,0:T(8,128)(2,1)S(1)}, bf16[768,512]{1,0:T(8,128)(2,1)S(1)}, u32[]{:S(2)}, u32[]{:S(2)}) %collective-permute-start.11) | collective-permute-done | bytes 786464 | tf_op jit(solution)/shard_map/ppermute | solution.py:45
  62.7 4.6 %all-to-all-done.1 = bf16[32,24,512]{2,1,0:T(8,128)(2,1)S(1)} async-done(((bf16[32,24,512]{2,1,0:T(8,128)(2,1)}), bf16[32,24,512]{2,1,0:T(8,128)(2,1)S(1)}, u32[]{:S(2)}, u32[]{:S(2)}) %all-to-all-start.1) | async-done | bytes 786464 | tf_op jit(solution)/shard_map/all_to_all | solution.py:461
  68.5 2.9 %collective-permute-start.6 = (bf16[768,512]{1,0:T(8,128)(2,1)S(1)}, bf16[768,512]{1,0:T(8,128)(2,1)S(1)}, u32[]{:S(2)}, u32[]{:S(2)}) collective-permute-start(bf16[768,512]{1,0:T(8,128)(2,1)S(1)} %bitcast.36), channel_id=1, source_target_pairs={{0,6},{1,3},{2,0},{3,5},{4,2},{5,7},{6,4},{7,1},{8,14},{9,11},{10,... | collective-permute-start | bytes 2359304 | tf_op jit(solution)/shard_map/ppermute | solution.py:45
  71.4 17.9 %collective-permute-done.2.refs_2_ = bf16[768,512]{1,0:T(8,128)(2,1)S(1)} collective-permute-done((bf16[768,512]{1,0:T(8,128)(2,1)S(1)}, bf16[768,512]{1,0:T(8,128)(2,1)S(1)}, u32[]{:S(2)}, u32[]{:S(2)}) %collective-permute-start.2) | collective-permute-done | bytes 786464 | tf_op jit(solution)/shard_map/ppermute | solution.py:45
  90.3 6.3 %gate_up.1 = (bf16[768,256]{1,0:T(8,128)(2,1)S(1)}, f32[768,512]{1,0:T(8,128)S(1)}) custom-call(bf16[768,512]{1,0:T(8,128)(2,1)} %bitcast.51, bf16[768,512]{1,0:T(8,128)(2,1)} %collective-permute-done.9.refs_1_, bf16[768,512]{1,0:T(8,128)(2,1)} %copy-done.14, bf16[768,512]{1,0:T(8,128)(2,1)} %collective-permute-done.10.refs_3_, bf16[768,512]{1,0:T(8,128)(2,1)} %copy-done.15, ...), custom_call_target="tpu_custom_call" | custom-call | flops 3221225472 | bytes 10485760 | tf_op jit(solution)/shard_map/gate_up/pallas_call | solution.py:190
  97.2 5.1 %hidden_start.1.refs_6_ = f32[768,512]{1,0:T(8,128)S(1)} custom-call(bf16[768,512]{1,0:T(8,128)(2,1)S(1)} %bitcast.37, bf16[768,512]{1,0:T(8,128)(2,1)S(1)} %collective-permute-done.4.refs_1_, bf16[768,512]{1,0:T(8,128)(2,1)S(1)} %collective-permute-done.2.refs_2_, bf16[768,512]{1,0:T(8,128)(2,1)S(1)} %collective-permute-done.5.refs_3_, ...), custom_call_target="tpu_custom_call" | custom-call | flops 2415919104 | bytes 7864320 | tf_op jit(solution)/shard_map/hidden_start/pallas_call | solution.py:255
  102.6 2.2 %collective-permute-done.14.refs_1_.refs_7_ = bf16[768,512]{1,0:T(8,128)(2,1)S(1)} collective-permute-done((bf16[768,512]{1,0:T(8,128)(2,1)S(1)}, bf16[768,512]{1,0:T(8,128)(2,1)S(1)}, u32[]{:S(2)}, u32[]{:S(2)}) %collective-permute-start.14) | collective-permute-done | bytes 786464 | tf_op jit(solution)/shard_map/ppermute | solution.py:49
  104.8 3.4 %hidden_end.1 = (bf16[768,1024]{1,0:T(8,128)(2,1)S(1)}, bf16[768,512]{1,0:T(8,128)(2,1)S(1)}) custom-call(bf16[768,512]{1,0:T(8,128)(2,1)S(1)} %collective-permute-done.3.refs_0_.refs_6_, bf16[768,512]{1,0:T(8,128)(2,1)S(1)} %collective-permute-done.14.refs_1_.refs_7_, bf16[8,512,256]{2,1,0:T(8,128)(2,1)} %get-tuple-element.30.refs_6_.refs_2_, ...), custom_call_target="tpu_custom_call" | custom-call | flops 1610612736 | bytes 2621440 | tf_op jit(solution)/shard_map/hidden_end/pallas_call | solution.py:302
  109.9 4.2 %partial.1 = (bf16[768,512]{1,0:T(8,128)(2,1)S(1)}, bf16[768,512]{1,0:T(8,128)(2,1)S(1)}, bf16[768,512]{1,0:T(8,128)(2,1)S(1)}) custom-call(bf16[768,1024]{1,0:T(8,128)(2,1)S(1)} %get-tuple-element.37.refs_0_.refs_8_, bf16[4,512,512]{2,1,0:T(8,128)(2,1)} %get-tuple-element.33.refs_4_.refs_1_, bf16[4,512,512]{2,1,0:T(8,128)(2,1)} %copy-done.11), custom_call_target="tpu_custom_call" | custom-call | flops 2415919104 | bytes 11010048 | tf_op jit(solution)/shard_map/partial/pallas_call | solution.py:341
  115.9 7.8 %collective-permute-done.18 = bf16[768,512]{1,0:T(8,128)(2,1)S(1)} collective-permute-done((bf16[768,512]{1,0:T(8,128)(2,1)S(1)}, bf16[768,512]{1,0:T(8,128)(2,1)S(1)}, u32[]{:S(2)}, u32[]{:S(2)}) %collective-permute-start.18) | collective-permute-done | bytes 786464 | tf_op jit(solution)/shard_map/ppermute | solution.py:45
  123.9 1.8 %collective-permute-start.19 = (bf16[768,512]{1,0:T(8,128)(2,1)S(1)}, bf16[768,512]{1,0:T(8,128)(2,1)S(1)}, u32[]{:S(2)}, u32[]{:S(2)}) collective-permute-start(bf16[768,512]{1,0:T(8,128)(2,1)S(1)} %add_convert_fusion.1), channel_id=1, source_target_pairs={{0,2},{1,7},{2,4},{3,1},{4,6},{5,3},{6,0},{7,5},{8,10},{9,15},{10,... | collective-permute-start | bytes 2359304 | tf_op jit(solution)/shard_map/ppermute | solution.py:45
  125.7 4.0 %collective-permute-done.17 = bf16[768,512]{1,0:T(8,128)(2,1)S(1)} collective-permute-done((bf16[768,512]{1,0:T(8,128)(2,1)S(1)}, bf16[768,512]{1,0:T(8,128)(2,1)S(1)}, u32[]{:S(2)}, u32[]{:S(2)}) %collective-permute-start.17) | collective-permute-done | bytes 786464 | tf_op jit(solution)/shard_map/ppermute | solution.py:45
  129.6 8.8 %collective-permute-done.19 = bf16[768,512]{1,0:T(8,128)(2,1)S(1)} collective-permute-done((bf16[768,512]{1,0:T(8,128)(2,1)S(1)}, bf16[768,512]{1,0:T(8,128)(2,1)S(1)}, u32[]{:S(2)}, u32[]{:S(2)}) %collective-permute-start.19) | collective-permute-done | bytes 786464 | tf_op jit(solution)/shard_map/ppermute | solution.py:45
  139.6 6.2 %all-to-all-start.2 = ((bf16[32,24,512]{2,1,0:T(8,128)(2,1)}), bf16[32,24,512]{2,1,0:T(8,128)(2,1)S(1)}, u32[]{:S(2)}, u32[]{:S(2)}) async-start(bf16[32,24,512]{2,1,0:T(8,128)(2,1)} %bitcast.46), calls=%async_computation.2 | async-start | bytes 1572864 | tf_op jit(solution)/shard_map/all_to_all | solution.py:461
  146.0 5.5 %down_total.1 = bf16[256,4096]{1,0:T(8,128)(2,1)} custom-call(s32[8]{0:T(128)S(1)} %stack.35.order, bf16[768,512]{1,0:T(8,128)(2,1)} %bitcast.38, bf16[768,512]{1,0:T(8,128)(2,1)} %copy-done.5, bf16[768,512]{1,0:T(8,128)(2,1)} %copy-done.4, bf16[768,512]{1,0:T(8,128)(2,1)} %copy-done.7, bf16[768,512]{1,0:T(8,128)(2,1)} %copy-done.6, ...), custom_call_target="tpu_custom_call" | custom-call | flops 1610612736 | bytes 8388608 | tf_op jit(solution)/shard_map/down_total/pallas_call | solution.py:381
  151.5 7.7 %gate_up_total.1 = (bf16[4096,256]{1,0:T(8,128)(2,1)}, bf16[4096,256]{1,0:T(8,128)(2,1)}) custom-call(s32[8]{0:T(128)S(1)} %stack.35.order, bf16[768,512]{1,0:T(8,128)(2,1)} %bitcast.52, bf16[768,512]{1,0:T(8,128)(2,1)} %collective-permute-done.9.refs_1_, bf16[768,512]{1,0:T(8,128)(2,1)} %copy-done.14, bf16[768,512]{1,0:T(8,128)(2,1)} %collective-permute-done.10.refs_3_, ...), custom_call_target="tpu_custom_call" | custom-call | flops 3221225472 | bytes 10485760 | tf_op jit(solution)/shard_map/gate_up_total/pallas_call | solution.py:431
  159.2 8.1 %all-to-all-done.2 = bf16[32,24,512]{2,1,0:T(8,128)(2,1)S(1)} async-done(((bf16[32,24,512]{2,1,0:T(8,128)(2,1)}), bf16[32,24,512]{2,1,0:T(8,128)(2,1)S(1)}, u32[]{:S(2)}, u32[]{:S(2)}) %all-to-all-start.2) | async-done | bytes 786464 | tf_op jit(solution)/shard_map/all_to_all | solution.py:461
  (75 shorter events, 14.8 us)
Async XLA Ops:
  3.1 34.4 %all-to-all-start = ((bf16[32,24,512]{2,1,0:T(8,128)(2,1)}), bf16[32,24,512]{2,1,0:T(8,128)(2,1)S(1)}, u32[]{:S(2)}, u32[]{:S(2)}) async-start(bf16[32,24,512]{2,1,0:T(8,128)(2,1)} %bitcast.2), calls=%async_computation | async-start | bytes 1572864 | tf_op jit(solution)/shard_map/all_to_all | solution.py:461
  37.4 52.7 %copy-start.12 = (bf16[32,24,512]{2,1,0:T(8,128)(2,1)}, bf16[32,24,512]{2,1,0:T(8,128)(2,1)S(1)}, u32[]{:S(2)}) copy-start(bf16[32,24,512]{2,1,0:T(8,128)(2,1)S(1)} %all-to-all-done) | copy-start | bytes 2359300
  37.4 16.0 %collective-permute-start = (bf16[768,512]{1,0:T(8,128)(2,1)S(1)}, bf16[768,512]{1,0:T(8,128)(2,1)S(1)}, u32[]{:S(2)}, u32[]{:S(2)}) collective-permute-start(bf16[768,512]{1,0:T(8,128)(2,1)S(1)} %bitcast.48), channel_id=1, source_target_pairs={{0,2},{1,7},{2,4},{3,1},{4,6},{5,3},{6,0},{7,5},{8,10},{9,15},{10,... | collective-permute-start | bytes 2359304 | tf_op jit(solution)/shard_map/ppermute | solution.py:45
  39.0 28.3 %all-to-all-start.1 = ((bf16[32,24,512]{2,1,0:T(8,128)(2,1)}), bf16[32,24,512]{2,1,0:T(8,128)(2,1)S(1)}, u32[]{:S(2)}, u32[]{:S(2)}) async-start(bf16[32,24,512]{2,1,0:T(8,128)(2,1)} %bitcast.15), calls=%async_computation.1 | async-start | bytes 1572864 | tf_op jit(solution)/shard_map/all_to_all | solution.py:461
  44.0 18.7 %collective-permute-start.11 = (bf16[768,512]{1,0:T(8,128)(2,1)S(1)}, bf16[768,512]{1,0:T(8,128)(2,1)S(1)}, u32[]{:S(2)}, u32[]{:S(2)}) collective-permute-start(bf16[768,512]{1,0:T(8,128)(2,1)S(1)} %bitcast.49), channel_id=1, source_target_pairs={{0,6},{1,3},{2,0},{3,5},{4,2},{5,7},{6,4},{7,1},{8,14},{9,11},{10,... | collective-permute-start | bytes 2359304 | tf_op jit(solution)/shard_map/ppermute | solution.py:45
  53.4 14.2 %collective-permute-start.1 = (bf16[768,512]{1,0:T(8,128)(2,1)S(1)}, bf16[768,512]{1,0:T(8,128)(2,1)}, u32[]{:S(2)}, u32[]{:S(2)}) collective-permute-start(bf16[768,512]{1,0:T(8,128)(2,1)S(1)} %collective-permute-done.refs_2_), channel_id=1, source_target_pairs={{0,2},{1,7},{2,4},{3,1},{4,6},{5,3},{6,0},{7,5},{8,10},{9,15},{10,... | collective-permute-start | bytes 2359304 | tf_op jit(solution)/shard_map/ppermute | solution.py:45
  55.4 41.2 %collective-permute-start.8 = (bf16[8,512,256]{2,1,0:T(8,128)(2,1)}, bf16[8,512,256]{2,1,0:T(8,128)(2,1)}, u32[]{:S(2)}, u32[]{:S(2)}) collective-permute-start(bf16[8,512,256]{2,1,0:T(8,128)(2,1)} %get-tuple-element.30.refs_6_.refs_2_), channel_id=1, source_target_pairs={{0,1},{1,0},{2,3},{3,2},{4,5},{5,4},{6,7},{7,6},{8,9},{9,8},{10,11... | collective-permute-start | bytes 6291464 | tf_op jit(solution)/shard_map/ppermute | solution.py:49
  55.5 12.5 %collective-permute-start.9 = (bf16[768,512]{1,0:T(8,128)(2,1)S(1)}, bf16[768,512]{1,0:T(8,128)(2,1)}, u32[]{:S(2)}, u32[]{:S(2)}) collective-permute-start(bf16[768,512]{1,0:T(8,128)(2,1)S(1)} %bitcast.50), channel_id=1, source_target_pairs={{0,1},{1,0},{2,3},{3,2},{4,5},{5,4},{6,7},{7,6},{8,9},{9,8},{10,11... | collective-permute-start | bytes 2359304 | tf_op jit(solution)/shard_map/ppermute | solution.py:49
  56.0 12.0 %collective-permute-start.10 = (bf16[768,512]{1,0:T(8,128)(2,1)S(1)}, bf16[768,512]{1,0:T(8,128)(2,1)}, u32[]{:S(2)}, u32[]{:S(2)}) collective-permute-start(bf16[768,512]{1,0:T(8,128)(2,1)S(1)} %collective-permute-done.refs_2_), channel_id=1, source_target_pairs={{0,1},{1,0},{2,3},{3,2},{4,5},{5,4},{6,7},{7,6},{8,9},{9,8},{10,11... | collective-permute-start | bytes 2359304 | tf_op jit(solution)/shard_map/ppermute | solution.py:49
  62.7 5.8 %collective-permute-start.12 = (bf16[768,512]{1,0:T(8,128)(2,1)S(1)}, bf16[768,512]{1,0:T(8,128)(2,1)}, u32[]{:S(2)}, u32[]{:S(2)}) collective-permute-start(bf16[768,512]{1,0:T(8,128)(2,1)S(1)} %collective-permute-done.11.refs_4_), channel_id=1, source_target_pairs={{0,1},{1,0},{2,3},{3,2},{4,5},{5,4},{6,7},{7,6},{8,9},{9,8},{10,11... | collective-permute-start | bytes 2359304 | tf_op jit(solution)/shard_map/ppermute | solution.py:49
  67.6 21.6 %collective-permute-start.2 = (bf16[768,512]{1,0:T(8,128)(2,1)S(1)}, bf16[768,512]{1,0:T(8,128)(2,1)S(1)}, u32[]{:S(2)}, u32[]{:S(2)}) collective-permute-start(bf16[768,512]{1,0:T(8,128)(2,1)S(1)} %bitcast.34), channel_id=1, source_target_pairs={{0,2},{1,7},{2,4},{3,1},{4,6},{5,3},{6,0},{7,5},{8,10},{9,15},{10,... | collective-permute-start | bytes 2359304 | tf_op jit(solution)/shard_map/ppermute | solution.py:45
  68.0 21.3 %collective-permute-start.4 = (bf16[768,512]{1,0:T(8,128)(2,1)S(1)}, bf16[768,512]{1,0:T(8,128)(2,1)S(1)}, u32[]{:S(2)}, u32[]{:S(2)}) collective-permute-start(bf16[768,512]{1,0:T(8,128)(2,1)S(1)} %bitcast.35), channel_id=1, source_target_pairs={{0,1},{1,0},{2,3},{3,2},{4,5},{5,4},{6,7},{7,6},{8,9},{9,8},{10,11... | collective-permute-start | bytes 2359304 | tf_op jit(solution)/shard_map/ppermute | solution.py:49
  68.0 21.4 %collective-permute-start.13 = (bf16[768,512]{1,0:T(8,128)(2,1)}, bf16[768,512]{1,0:T(8,128)(2,1)S(1)}, u32[]{:S(2)}, u32[]{:S(2)}) collective-permute-start(bf16[768,512]{1,0:T(8,128)(2,1)} %collective-permute-done.1.refs_6_), channel_id=1, source_target_pairs={{0,1},{1,0},{2,3},{3,2},{4,5},{5,4},{6,7},{7,6},{8,9},{9,8},{10,11... | collective-permute-start | bytes 2359304 | tf_op jit(solution)/shard_map/ppermute | solution.py:49
  68.5 21.4 %collective-permute-start.6 = (bf16[768,512]{1,0:T(8,128)(2,1)S(1)}, bf16[768,512]{1,0:T(8,128)(2,1)S(1)}, u32[]{:S(2)}, u32[]{:S(2)}) collective-permute-start(bf16[768,512]{1,0:T(8,128)(2,1)S(1)} %bitcast.36), channel_id=1, source_target_pairs={{0,6},{1,3},{2,0},{3,5},{4,2},{5,7},{6,4},{7,1},{8,14},{9,11},{10,... | collective-permute-start | bytes 2359304 | tf_op jit(solution)/shard_map/ppermute | solution.py:45
  89.2 13.4 %collective-permute-start.15 = (bf16[4,512,512]{2,1,0:T(8,128)(2,1)}, bf16[4,512,512]{2,1,0:T(8,128)(2,1)S(1)}, u32[]{:S(2)}, u32[]{:S(2)}) collective-permute-start(bf16[4,512,512]{2,1,0:T(8,128)(2,1)} %get-tuple-element.35), channel_id=1, source_target_pairs={{0,1},{1,0},{2,3},{3,2},{4,5},{5,4},{6,7},{7,6},{8,9},{9,8},{10,11... | collective-permute-start | bytes 6291464 | tf_op jit(solution)/shard_map/ppermute | solution.py:49
  89.2 13.3 %collective-permute-start.3 = (bf16[768,512]{1,0:T(8,128)(2,1)S(1)}, bf16[768,512]{1,0:T(8,128)(2,1)S(1)}, u32[]{:S(2)}, u32[]{:S(2)}) collective-permute-start(bf16[768,512]{1,0:T(8,128)(2,1)S(1)} %collective-permute-done.2.refs_2_), channel_id=1, source_target_pairs={{0,2},{1,7},{2,4},{3,1},{4,6},{5,3},{6,0},{7,5},{8,10},{9,15},{10,... | collective-permute-start | bytes 2359304 | tf_op jit(solution)/shard_map/ppermute | solution.py:45
  89.3 7.8 %collective-permute-start.5 = (bf16[768,512]{1,0:T(8,128)(2,1)S(1)}, bf16[768,512]{1,0:T(8,128)(2,1)S(1)}, u32[]{:S(2)}, u32[]{:S(2)}) collective-permute-start(bf16[768,512]{1,0:T(8,128)(2,1)S(1)} %collective-permute-done.2.refs_2_), channel_id=1, source_target_pairs={{0,1},{1,0},{2,3},{3,2},{4,5},{5,4},{6,7},{7,6},{8,9},{9,8},{10,11... | collective-permute-start | bytes 2359304 | tf_op jit(solution)/shard_map/ppermute | solution.py:49
  89.8 7.3 %collective-permute-start.7 = (bf16[768,512]{1,0:T(8,128)(2,1)S(1)}, bf16[768,512]{1,0:T(8,128)(2,1)S(1)}, u32[]{:S(2)}, u32[]{:S(2)}) collective-permute-start(bf16[768,512]{1,0:T(8,128)(2,1)S(1)} %collective-permute-done.6.refs_4_), channel_id=1, source_target_pairs={{0,1},{1,0},{2,3},{3,2},{4,5},{5,4},{6,7},{7,6},{8,9},{9,8},{10,11... | collective-permute-start | bytes 2359304 | tf_op jit(solution)/shard_map/ppermute | solution.py:49
  96.7 8.1 %collective-permute-start.16 = (f32[768,512]{1,0:T(8,128)S(1)}, f32[768,512]{1,0:T(8,128)S(1)}, u32[]{:S(2)}, u32[]{:S(2)}) collective-permute-start(f32[768,512]{1,0:T(8,128)S(1)} %get-tuple-element.36.refs_7_), channel_id=1, source_target_pairs={{0,1},{1,0},{2,3},{3,2},{4,5},{5,4},{6,7},{7,6},{8,9},{9,8},{10,11... | collective-permute-start | bytes 4718600 | tf_op jit(solution)/shard_map/ppermute | solution.py:49
  102.5 2.3 %collective-permute-start.14 = (bf16[768,512]{1,0:T(8,128)(2,1)S(1)}, bf16[768,512]{1,0:T(8,128)(2,1)S(1)}, u32[]{:S(2)}, u32[]{:S(2)}) collective-permute-start(bf16[768,512]{1,0:T(8,128)(2,1)S(1)} %collective-permute-done.3.refs_0_.refs_6_), channel_id=1, source_target_pairs={{0,1},{1,0},{2,3},{3,2},{4,5},{5,4},{6,7},{7,6},{8,9},{9,8},{10,11... | collective-permute-start | bytes 2359304 | tf_op jit(solution)/shard_map/ppermute | solution.py:49
  108.3 15.4 %collective-permute-start.18 = (bf16[768,512]{1,0:T(8,128)(2,1)S(1)}, bf16[768,512]{1,0:T(8,128)(2,1)S(1)}, u32[]{:S(2)}, u32[]{:S(2)}) collective-permute-start(bf16[768,512]{1,0:T(8,128)(2,1)S(1)} %get-tuple-element.41), channel_id=1, source_target_pairs={{0,2},{1,7},{2,4},{3,1},{4,6},{5,3},{6,0},{7,5},{8,10},{9,15},{10,... | collective-permute-start | bytes 2359304 | tf_op jit(solution)/shard_map/ppermute | solution.py:45
  114.2 15.5 %collective-permute-start.17 = (bf16[768,512]{1,0:T(8,128)(2,1)S(1)}, bf16[768,512]{1,0:T(8,128)(2,1)S(1)}, u32[]{:S(2)}, u32[]{:S(2)}) collective-permute-start(bf16[768,512]{1,0:T(8,128)(2,1)S(1)} %get-tuple-element.39), channel_id=1, source_target_pairs={{0,6},{1,3},{2,0},{3,5},{4,2},{5,7},{6,4},{7,1},{8,14},{9,11},{10,... | collective-permute-start | bytes 2359304 | tf_op jit(solution)/shard_map/ppermute | solution.py:45
  123.9 14.5 %collective-permute-start.19 = (bf16[768,512]{1,0:T(8,128)(2,1)S(1)}, bf16[768,512]{1,0:T(8,128)(2,1)S(1)}, u32[]{:S(2)}, u32[]{:S(2)}) collective-permute-start(bf16[768,512]{1,0:T(8,128)(2,1)S(1)} %add_convert_fusion.1), channel_id=1, source_target_pairs={{0,2},{1,7},{2,4},{3,1},{4,6},{5,3},{6,0},{7,5},{8,10},{9,15},{10,... | collective-permute-start | bytes 2359304 | tf_op jit(solution)/shard_map/ppermute | solution.py:45
  139.6 27.6 %all-to-all-start.2 = ((bf16[32,24,512]{2,1,0:T(8,128)(2,1)}), bf16[32,24,512]{2,1,0:T(8,128)(2,1)S(1)}, u32[]{:S(2)}, u32[]{:S(2)}) async-start(bf16[32,24,512]{2,1,0:T(8,128)(2,1)} %bitcast.46), calls=%async_computation.2 | async-start | bytes 1572864 | tf_op jit(solution)/shard_map/all_to_all | solution.py:461
  (16 other events, 166.9 us)
